TPU v7x, 32 devices: a whole 2x2x4 slice. The times are simulated.
32 devices in a mesh: seq: 4 (over y, core), shard: 8 (over z, x).
Axes of the slice: x: 2, y: 2, z: 4, core: 2. Of those that a mesh axis runs over, the one named last changes fastest.
Arguments:
- inputs: bfloat16 [8, 512, 2048], P('shard', 'seq'), may hold values from -6 to 6
- out_grad: bfloat16 [8, 512, 2048], P('shard', 'seq'), may hold values from -6 to 6
- segments: int32 [8, 512], P('shard', 'seq'), may hold values from 0 to 3, never falling along the last dimension, each value on 1 to 256 neighbouring positions
- w_in: float32 [2048, 24576], P(('seq', 'shard'))
- w_down: float32 [8192, 2048], P(('seq', 'shard'))
- conv_taps: float32 [2048, 3], P(('seq', 'shard'))
- norm_gains: float32 [2048, 2], P(('seq', 'shard'))
- m_in: float32 [2048, 24576], P(('seq', 'shard'))
- m_down: float32 [8192, 2048], P(('seq', 'shard'))
- m_taps: float32 [2048, 3], P(('seq', 'shard'))
- m_gains: float32 [2048, 2], P(('seq', 'shard'))
- v_in: float32 [2048, 24576], P(('seq', 'shard')), may hold values from 4.096 to 40.96
- v_down: float32 [8192, 2048], P(('seq', 'shard')), may hold values from 4.096 to 40.96
- v_taps: float32 [2048, 3], P(('seq', 'shard')), may hold values from 4.096 to 40.96
- v_gains: float32 [2048, 2], P(('seq', 'shard')), may hold values from 4.096 to 40.96
Outputs:
- block_out: bfloat16 [8, 512, 2048], P('shard', 'seq')
- input_grad: float32 [8, 512, 2048], P('shard', 'seq')
- grad_in: float32 [2048, 24576], P(('seq', 'shard'))
- grad_down: float32 [8192, 2048], P(('seq', 'shard'))
- grad_taps: float32 [2048, 3], P(('seq', 'shard'))
- grad_gains: float32 [2048, 2], P(('seq', 'shard'))
- new_m_in: float32 [2048, 24576], P(('seq', 'shard'))
- new_m_down: float32 [8192, 2048], P(('seq', 'shard'))
- new_m_taps: float32 [2048, 3], P(('seq', 'shard'))
- new_m_gains: float32 [2048, 2], P(('seq', 'shard'))
- new_v_in: float32 [2048, 24576], P(('seq', 'shard'))
- new_v_down: float32 [8192, 2048], P(('seq', 'shard'))
- new_v_taps: float32 [2048, 3], P(('seq', 'shard'))
- new_v_gains: float32 [2048, 2], P(('seq', 'shard'))
- new_w_in: float32 [2048, 24576], P(('seq', 'shard'))
- new_w_down: float32 [8192, 2048], P(('seq', 'shard'))
- new_w_taps: float32 [2048, 3], P(('seq', 'shard'))
- new_w_gains: float32 [2048, 2], P(('seq', 'shard'))
- lamb_norms: float32 [2, 8], replicated
Inputs may be any that keep to these rules, and one draw needn't show every extreme that they name: `segments`: segment numbers never fall along a sequence; each of the 4 numbers holds 1 to 256 tokens of every sequence.
All inputs are finite; a program needn't handle non-finite values.
Results may differ from a plain program's by a relative error of at most 0.012.
The roundings to bfloat16 on the way count: a program that leaves them out, or rounds other values in their place, can miss the bound.
Values may be sent and summed in bfloat16 or wider, within the bound.
No kernel may reach another device: no remote copies, remote signals or barrier semaphores. Data moves between devices by JAX's collectives and lax.ppermute only.
A program may use at most 384 MiB of HBM per device.

v0:
```python
import jax
import jax.numpy as jnp
from jax import lax
from jax.sharding import PartitionSpec as P

D = 2048
FF = 8192
TAPS = 3
STEP = 4


EPS_NORM = 1e-05
BETA_ONE = 0.9
BETA_TWO = 0.999
EPS_ADAM = 1e-08
DECAY = 0.01
RATE = 0.3


def shifted(value, axis, steps):
    count = lax.axis_size(axis)
    leading, last = (max(0, -steps), min(count, count - steps))
    return lax.ppermute(value, axis, [(source, source + steps) for source in range(leading, last)])


def norm_forward(values, gain):
    scale = lax.rsqrt(jnp.mean(values * values, axis=-1, keepdims=True) + EPS_NORM)
    return (values * scale * gain, scale)


def norm_backward(values, scale, gain, grad):
    along = grad * gain
    inner = jnp.mean(along * values, axis=-1, keepdims=True)
    d_values = scale * along - scale * scale * scale * values * inner
    d_gain = jnp.sum(grad * values * scale, axis=0)
    return (d_values, d_gain)


def times_wide(left, right):
    return lax.dot_general(
        left, right, (((1,), (1,)), ((), ())), preferred_element_type=jnp.float32
    )


def over_tokens(left, right):
    return lax.dot_general(
        left, right, (((0,), (0,)), ((), ())), preferred_element_type=jnp.float32
    )


def piece_squares(a_in, a_down, a_taps, a_gains):
    parts = [
        a_in[:, : 3 * D],
        a_in[:, 3 * D : 4 * D],
        a_in[:, 4 * D : 4 * D + FF],
        a_in[:, 4 * D + FF :],
        a_down,
        a_taps,
        a_gains[:, 0],
        a_gains[:, 1],
    ]
    return jnp.stack([jnp.sum(p * p) for p in parts])


def adam_direction(weight, grad, first, second):
    new_first = BETA_ONE * first + (1.0 - BETA_ONE) * grad
    new_second = BETA_TWO * second + (1.0 - BETA_TWO) * grad * grad
    first_hat = new_first / (1.0 - BETA_ONE**STEP)
    second_hat = new_second / (1.0 - BETA_TWO**STEP)
    direction = first_hat / (jnp.sqrt(second_hat) + EPS_ADAM) + DECAY * weight
    return (new_first, new_second, direction)


def local(
    inputs,
    out_grad,
    segments,
    w_in,
    w_down,
    conv_taps,
    norm_gains,
    m_in,
    m_down,
    m_taps,
    m_gains,
    v_in,
    v_down,
    v_taps,
    v_gains,
):
    count = inputs.shape[1]
    width = inputs.shape[2]
    full_in, full_down, full_taps, full_gains = (
        lax.all_gather(w_in.astype(jnp.bfloat16), ("seq", "shard"), axis=0, tiled=True),
        lax.all_gather(w_down.astype(jnp.bfloat16), ("seq", "shard"), axis=0, tiled=True),
        lax.all_gather(conv_taps.astype(jnp.bfloat16), ("seq", "shard"), axis=0, tiled=True),
        lax.all_gather(norm_gains.astype(jnp.bfloat16), ("seq", "shard"), axis=0, tiled=True),
    )
    taps = full_taps.astype(jnp.float32)
    gains = full_gains.astype(jnp.float32)
    gain_one = gains[:, 0]
    gain_two = gains[:, 1]
    seq_ids = segments.reshape(count).astype(jnp.float32)
    values = inputs.reshape(count, width).astype(jnp.float32)
    norm_one, scale_one = norm_forward(values, gain_one)
    h_one = norm_one.astype(jnp.bfloat16)
    bcx = jnp.dot(h_one, full_in[:, : 3 * D], preferred_element_type=jnp.float32)
    b_part = bcx[:, :D]
    c_part = bcx[:, D : 2 * D]
    x_part = bcx[:, 2 * D : 3 * D]
    mixed_in = b_part * x_part
    prev_rows, prev_ids = shifted((mixed_in[-2:], seq_ids[-2:]), "seq", 1)
    extended = jnp.concatenate([prev_rows, mixed_in], 0)
    ext_ids = jnp.concatenate([prev_ids, seq_ids], 0)
    keeps = []
    conv = jnp.zeros((count, width), jnp.float32)
    for lag in range(TAPS):
        keep = (ext_ids[2 - lag : 2 - lag + count] == seq_ids).astype(jnp.float32)[:, None]
        keeps.append(keep)
        conv = conv + taps[:, lag] * extended[2 - lag : 2 - lag + count] * keep
    y_mix = (c_part * conv).astype(jnp.bfloat16)
    middle = values + jnp.dot(y_mix, full_in[:, 3 * D : 4 * D], preferred_element_type=jnp.float32)
    norm_two, scale_two = norm_forward(middle, gain_two)
    h_two = norm_two.astype(jnp.bfloat16)
    gate_up = jnp.dot(h_two, full_in[:, 4 * D :], preferred_element_type=jnp.float32)
    gate = gate_up[:, :FF]
    up_part = gate_up[:, FF:]
    sig = jax.nn.sigmoid(gate)
    activated = gate * sig
    hidden = (activated * up_part).astype(jnp.bfloat16)
    result = middle + jnp.dot(hidden, full_down, preferred_element_type=jnp.float32)
    block_out = result.astype(jnp.bfloat16).reshape(inputs.shape)
    grad_top = out_grad.reshape(count, width).astype(jnp.float32)
    d_ffn = grad_top.astype(jnp.bfloat16)
    d_hidden = times_wide(d_ffn, full_down)
    d_gate = d_hidden * up_part * sig * (1.0 + gate * (1.0 - sig))
    d_up = d_hidden * activated
    d_gate_up = jnp.concatenate([d_gate, d_up], 1).astype(jnp.bfloat16)
    d_h_two = times_wide(d_gate_up, full_in[:, 4 * D :])
    d_middle, d_gain_two = norm_backward(middle, scale_two, gain_two, d_h_two)
    d_middle = d_middle + grad_top
    d_branch = d_middle.astype(jnp.bfloat16)
    d_mix = times_wide(d_branch, full_in[:, 3 * D : 4 * D])
    d_c = d_mix * conv
    d_conv = d_mix * c_part
    d_extended = jnp.zeros((count + 2, width), jnp.float32)
    tap_grads = []
    for lag in range(TAPS):
        counted = d_conv * keeps[lag]
        tap_grads.append(jnp.sum(counted * extended[2 - lag : 2 - lag + count], axis=0))
        d_extended = d_extended + jnp.pad(taps[:, lag] * counted, ((2 - lag, lag), (0, 0)))
    back_state = shifted(d_extended[:2], "seq", -1)
    d_mixed_in = d_extended[2:] + jnp.pad(back_state, ((count - 2, 0), (0, 0)))
    d_bcx = jnp.concatenate([d_mixed_in * x_part, d_c, d_mixed_in * b_part], 1).astype(jnp.bfloat16)
    d_h_one = times_wide(d_bcx, full_in[:, : 3 * D])
    d_values, d_gain_one = norm_backward(values, scale_one, gain_one, d_h_one)
    input_grad = (d_values + d_middle).reshape(inputs.shape)
    small_terms = jnp.concatenate(
        [jnp.stack(tap_grads, 1), jnp.stack([d_gain_one, d_gain_two], 1)], 1
    )
    n_seq = lax.axis_size("seq")
    n_shard = lax.axis_size("shard")
    left_cols = (
        lax.all_to_all(h_one, "seq", split_axis=1, concat_axis=0, tiled=True),
        lax.all_to_all(y_mix, "seq", split_axis=1, concat_axis=0, tiled=True),
        lax.all_to_all(h_two, "seq", split_axis=1, concat_axis=0, tiled=True),
        lax.all_to_all(hidden, "seq", split_axis=1, concat_axis=0, tiled=True),
    )
    left_all = (
        lax.all_gather(left_cols[0], "shard", axis=0, tiled=True),
        lax.all_gather(left_cols[1], "shard", axis=0, tiled=True),
        lax.all_gather(left_cols[2], "shard", axis=0, tiled=True),
        lax.all_gather(left_cols[3], "shard", axis=0, tiled=True),
    )

    def regroup(gathered):
        cols = gathered.shape[1]
        return jnp.swapaxes(gathered.reshape(n_shard, n_seq, count, cols), 0, 1).reshape(-1, cols)

    left_ordered = [regroup(item) for item in left_all]
    right_cols = (
        lax.all_to_all(d_bcx, "shard", split_axis=1, concat_axis=0, tiled=True),
        lax.all_to_all(d_branch, "shard", split_axis=1, concat_axis=0, tiled=True),
        lax.all_to_all(d_gate_up, "shard", split_axis=1, concat_axis=0, tiled=True),
        lax.all_to_all(d_ffn, "shard", split_axis=1, concat_axis=0, tiled=True),
    )
    right_all = (
        lax.all_gather(right_cols[0], "seq", axis=0, tiled=True),
        lax.all_gather(right_cols[1], "seq", axis=0, tiled=True),
        lax.all_gather(right_cols[2], "seq", axis=0, tiled=True),
        lax.all_gather(right_cols[3], "seq", axis=0, tiled=True),
    )
    blocks = (
        over_tokens(left_ordered[0], right_all[0]),
        over_tokens(left_ordered[1], right_all[1]),
        over_tokens(left_ordered[2], right_all[2]),
        over_tokens(left_ordered[3], right_all[3]),
    )
    owned = (
        lax.all_to_all(blocks[0], "shard", split_axis=0, concat_axis=1, tiled=True),
        lax.all_to_all(blocks[1], "shard", split_axis=0, concat_axis=1, tiled=True),
        lax.all_to_all(blocks[2], "shard", split_axis=0, concat_axis=1, tiled=True),
        lax.all_to_all(blocks[3], "shard", split_axis=0, concat_axis=1, tiled=True),
    )
    grad_in = jnp.concatenate([owned[0], owned[1], owned[2]], 1)
    grad_down = owned[3]
    small_sums = lax.psum_scatter(small_terms, ("seq", "shard"), scatter_dimension=0, tiled=True)
    grad_taps = small_sums[:, :TAPS]
    grad_gains = small_sums[:, TAPS:]
    new_m_in, new_v_in, dir_in = adam_direction(w_in, grad_in, m_in, v_in)
    new_m_down, new_v_down, dir_down = adam_direction(w_down, grad_down, m_down, v_down)
    new_m_taps, new_v_taps, dir_taps = adam_direction(conv_taps, grad_taps, m_taps, v_taps)
    new_m_gains, new_v_gains, dir_gains = adam_direction(norm_gains, grad_gains, m_gains, v_gains)
    dir_local = piece_squares(dir_in, dir_down, dir_taps, dir_gains)
    weight_sums, dir_sums = lax.psum(
        (piece_squares(w_in, w_down, conv_taps, norm_gains), dir_local), ("seq", "shard")
    )
    weight_norm = jnp.sqrt(weight_sums)
    dir_norm = jnp.sqrt(dir_sums)
    ratio = -RATE * weight_norm / (dir_norm + 1e-06)
    ratio_cols = jnp.concatenate(
        [
            jnp.full((3 * D,), ratio[0]),
            jnp.full((D,), ratio[1]),
            jnp.full((FF,), ratio[2]),
            jnp.full((FF,), ratio[3]),
        ]
    )
    new_w_in = w_in + dir_in * ratio_cols[None, :]
    new_w_down = w_down + dir_down * ratio[4]
    new_w_taps = conv_taps + dir_taps * ratio[5]
    new_w_gains = norm_gains + dir_gains * jnp.stack([ratio[6], ratio[7]])[None, :]
    lamb_norms = jnp.stack([weight_norm, dir_norm])
    return (
        block_out,
        input_grad,
        grad_in,
        grad_down,
        grad_taps,
        grad_gains,
        new_m_in,
        new_m_down,
        new_m_taps,
        new_m_gains,
        new_v_in,
        new_v_down,
        new_v_taps,
        new_v_gains,
        new_w_in,
        new_w_down,
        new_w_taps,
        new_w_gains,
        lamb_norms,
    )


def solution(mesh):
    placed = (
        P("shard", "seq", None),
        P("shard", "seq", None),
        P("shard", "seq"),
        P(("seq", "shard"), None),
        P(("seq", "shard"), None),
        P(("seq", "shard"), None),
        P(("seq", "shard"), None),
        P(("seq", "shard"), None),
        P(("seq", "shard"), None),
        P(("seq", "shard"), None),
        P(("seq", "shard"), None),
        P(("seq", "shard"), None),
        P(("seq", "shard"), None),
        P(("seq", "shard"), None),
        P(("seq", "shard"), None),
    )
    return jax.shard_map(
        local,
        mesh=mesh,
        in_specs=placed,
        out_specs=(
            P("shard", "seq", None),
            P("shard", "seq", None),
            P(("seq", "shard"), None),
            P(("seq", "shard"), None),
            P(("seq", "shard"), None),
            P(("seq", "shard"), None),
            P(("seq", "shard"), None),
            P(("seq", "shard"), None),
            P(("seq", "shard"), None),
            P(("seq", "shard"), None),
            P(("seq", "shard"), None),
            P(("seq", "shard"), None),
            P(("seq", "shard"), None),
            P(("seq", "shard"), None),
            P(("seq", "shard"), None),
            P(("seq", "shard"), None),
            P(("seq", "shard"), None),
            P(("seq", "shard"), None),
            P(),
        ),
        check_vma=False,
    )
```

profile of v0, /device:TPU:0, one launch (start us, length us, event | category | flops | bytes accessed | tf_op | source)
XLA Modules:
  0.0 1863.4 jit_solution(1724954138588167762)
XLA Ops:
  7.2 4.9 convert_element_type.100
  16.8 69.3 %all-gather = bf16[32,64,2]{1,2,0:T(2,128)(2,1)S(1)} all-gather(bf16[1,64,2]{1,2,0:T(2,128)(2,1)S(1)} %convert_bitcast_fusion.1), channel_id=1, replica_groups=mesh['seq'=4,'shard'=8] {'seq','shard'}, dimensions={0}, use_global_device_ids=true | all-gather | bytes 8448 | tf_op jit(solution)/shard_map/all_gather | solution.py:97
  93.6 64.7 %all-gather.1 = bf16[32,64,3]{1,2,0:T(4,128)(2,1)S(1)} all-gather(bf16[1,64,3]{1,2,0:T(4,128)(2,1)S(1)} %get-tuple-element.147), channel_id=1, replica_groups=mesh['seq'=4,'shard'=8] {'seq','shard'}, dimensions={0}, use_global_device_ids=true | all-gather | bytes 12672 | tf_op jit(solution)/shard_map/all_gather | solution.py:96
  159.3 373.4 %all-gather.13.cloned.1.call-done = bf16[2048,24576]{1,0:T(8,128)(2,1)} async-done(((bf16[64,24576]{1,0:T(8,128)(2,1)}), bf16[2048,24576]{1,0:T(8,128)(2,1)}) %all-gather.13.cloned.1.call-update) | async-done | bytes 100663312 | tf_op jit(solution)/shard_map/all_gather | solution.py:94
  532.7 10.1 fusion.6
  548.6 5.1 all-to-all-start.3
  554.2 4.8 multiply_reduce_fusion.10
  559.3 27.2 %fusion.2 = f32[128,16384]{1,0:T(8,128)} fusion(bf16[128,2048]{1,0:T(8,128)(2,1)S(1)} %multiply_convert_fusion.3, bf16[2048,24576]{1,0:T(8,128)(2,1)} %all-gather.13.cloned.1.call-done), kind=kOutput, calls=%fused_computation.2 | convolution fusion | flops 8589934592 | bytes 76021760 | tf_op jit(solution)/shard_map/dot_general | solution.py:125
  587.4 142.0 %all-gather.15.cloned.1.call-done = bf16[8192,2048]{1,0:T(8,128)(2,1)} async-done(((bf16[256,2048]{1,0:T(8,128)(2,1)}), bf16[8192,2048]{1,0:T(8,128)(2,1)}) %all-gather.15.cloned.1.call-update) | async-done | bytes 33554448 | tf_op jit(solution)/shard_map/all_gather | solution.py:95
  729.3 19.9 %multiply_convert_fusion.1 = (bf16[128,8192]{1,0:T(8,128)(2,1)}, bf16[128,8192]{1,0:T(8,128)(2,1)}, bf16[128,8192]{1,0:T(8,128)(2,1)S(1)}) fusion(f32[128,16384]{1,0:T(8,128)} %fusion.2, bf16[8192,2048]{1,0:T(8,128)(2,1)} %all-gather.15.cloned.1.call-done, bf16[1,128,2048]{2,1,0:T(8,128)(2,1)} %param.16), kind=kOutput, calls=%fused_computation.26 | convolution fusion | flops 4310695936 | bytes 48758784 | tf_op jit(solution)/shard_map/dot_general | solution.py:40
  749.2 30.1 %multiply_reduce_fusion.5 = (f32[2048]{0:T(1024)S(1)}, f32[128]{0:T(128)S(1)}, f32[128,2048]{1,0:T(8,128)}) fusion(f32[128,2048]{1,0:T(8,128)S(1)} %get-tuple-element.167, f32[128]{0:T(128)S(1)} %get-tuple-element.162, f32[2048]{0:T(1024)S(1)} %bitcast.248, bf16[2048,24576]{1,0:T(8,128)(2,1)} %all-gather.13.cloned.1.call-done, ...), kind=kOutput, calls=%fused_computation.83 | convolution fusion | flops 8599894016 | bytes 73417728 | tf_op jit(solution)/shard_map/dot_general | solution.py:40
  783.7 4.5 all-to-all-start.4
  788.4 8.2 multiply_reduce_fusion.6
  801.6 12.9 all-to-all-done.4
  816.1 56.7 %all_to_all.207 = bf16[128,8,768]{2,0,1:T(8,128)(2,1)} all-to-all(bf16[128,8,768]{2,0,1:T(8,128)(2,1)S(1)} %bitcast.224), channel_id=1, replica_groups=mesh['seq'=4,'shard'=8] {'shard'}, dimensions={1} | all-to-all | bytes 3145728 | tf_op jit(solution)/shard_map/all_to_all | solution.py:182
  873.1 29.0 %all_to_all.208 = bf16[128,4,2048]{2,0,1:T(8,128)(2,1)} all-to-all(bf16[128,4,2048]{2,0,1:T(8,128)(2,1)S(1)} %bitcast.222), channel_id=1, replica_groups=mesh['seq'=4,'shard'=8] {'seq'}, dimensions={1} | all-to-all | bytes 4194304 | tf_op jit(solution)/shard_map/all_to_all | solution.py:167
  903.4 18.2 all_to_all.209
  932.9 6.3 all-to-all-done.6
  939.2 5.5 all-to-all-start.7
  945.5 148.9 %all-to-all-done.7 = bf16[128,8,2048]{2,0,1:T(8,128)(2,1)} async-done(((bf16[128,8,2048]{2,0,1:T(8,128)(2,1)}), bf16[128,8,2048]{2,0,1:T(8,128)(2,1)}, u32[]{:S(2)}, u32[]{:S(2)}) %all-to-all-start.7) | async-done | bytes 4194336 | tf_op jit(solution)/shard_map/all_to_all | solution.py:184
  1094.5 4.7 copy.124
  1099.1 6.3 copy.125
  1105.5 4.9 copy.129
  1110.4 6.5 copy.130
  1116.9 4.9 fusion.31
  1126.0 8.6 fusion.15
  1134.6 18.7 %all-to-all-done.5 = f32[8,64,256]{2,1,0:T(8,128)} async-done(((f32[8,64,256]{2,1,0:T(8,128)}), f32[8,64,256]{2,1,0:T(8,128)}, u32[]{:S(2)}, u32[]{:S(2)}) %all-to-all-start.5) | async-done | bytes 524320 | tf_op jit(solution)/shard_map/all_to_all | solution.py:201
  1153.3 4.5 all-to-all-start.2
  1157.9 135.0 %all-gather.29.cloned.1.call-done = bf16[4096,2048]{1,0:T(8,128)(2,1)} async-done(((bf16[512,2048]{1,0:T(8,128)(2,1)}), bf16[4096,2048]{1,0:T(8,128)(2,1)}) %all-gather.29.cloned.1.call-update) | async-done | bytes 16777232 | tf_op jit(solution)/shard_map/all_gather | solution.py:173
  1292.9 14.3 copy.140
  1307.2 20.9 %copy.141 = bf16[2048,4096]{1,0:T(8,128)(2,1)} copy(bf16[2048,4096]{0,1:T(8,128)(2,1)} %bitcast.212) | data formatting | bytes 33554432 | tf_op jit(solution)/shard_map/dot_general | solution.py:46
  1328.1 12.4 fusion.29
  1352.4 74.7 %all-gather.25.cloned.1.call-done = bf16[4096,512]{1,0:T(8,128)(2,1)} async-done(((bf16[512,512]{1,0:T(8,128)(2,1)}), bf16[4096,512]{1,0:T(8,128)(2,1)}) %all-gather.25.cloned.1.call-update) | async-done | bytes 4194320 | tf_op jit(solution)/shard_map/all_gather | solution.py:172
  1427.1 4.6 copy.134
  1431.8 6.7 copy.135
  1438.4 93.3 %all-gather.27.cloned.1.call-done = bf16[4096,2048]{1,0:T(8,128)(2,1)} async-done(((bf16[1024,2048]{1,0:T(8,128)(2,1)}), bf16[4096,2048]{1,0:T(8,128)(2,1)}) %all-gather.27.cloned.1.call-update) | async-done | bytes 16777232 | tf_op jit(solution)/shard_map/all_gather | solution.py:190
  1531.8 14.9 fusion.8
  1546.7 5.6 all-to-all-start.8
  1562.1 5.3 stack.94
  1567.3 13.8 fusion.25
  1581.2 13.9 fusion.44
  1598.1 150.9 %reduce-scatter.4.cloned.1.call-done = f32[64,5]{1,0:T(8,128)} async-done(((f32[2048,5]{1,0:T(8,128)}), f32[64,5]{1,0:T(8,128)}) %reduce-scatter.4.cloned.1.call-update) | async-done | bytes 1296
  1759.8 7.7 multiply_reduce_fusion
  1777.5 11.4 multiply_add_fusion.1
  1792.5 5.2 stack.103
  1799.5 36.9 %all-reduce.4 = (f32[8]{0:T(128)S(1)}, f32[8]{0:T(128)S(1)}) all-reduce(f32[8]{0:T(128)S(1)} %stack.103, f32[8]{0:T(128)S(1)} %stack.94), channel_id=1, replica_groups=mesh['seq'=4,'shard'=8] {'seq','shard'}, use_global_device_ids=true, to_apply=%region_27.28 | all-reduce | flops 16 | bytes 128 | tf_op jit(solution)/shard_map/psum | solution.py:215
  1837.8 4.6 multiply_add_fusion.3
  1846.8 8.0 multiply_add_fusion
  (195 shorter events, 107.5 us)
Async XLA Ops:
  7.2 5.0 copy-start.6
  7.2 525.5 %all-gather.13.cloned.1.call-start = ((), (), s32[]{:S(2)}) async-start(), calls=%async_computation.13 | async-start | bytes 103809024 | tf_op jit(solution)/shard_map/all_gather | solution.py:94
  12.1 4.6 copy-start.21
  12.1 74.1 %copy-start.7 = (bf16[1,128,2048]{2,1,0:T(8,128)(2,1)S(1)}, bf16[1,128,2048]{2,1,0:T(8,128)(2,1)}, u32[]{:S(2)}) copy-start(bf16[1,128,2048]{2,1,0:T(8,128)(2,1)} %param.15) | copy-start | bytes 1572868
  12.2 80.8 %copy-start.19 = (f32[64,3]{0,1:T(4,128)S(1)}, f32[64,3]{0,1:T(4,128)}, u32[]{:S(2)}) copy-start(f32[64,3]{0,1:T(4,128)} %param.20) | copy-start | bytes 2308
  12.2 717.1 %all-gather.15.cloned.1.call-start = ((), (), s32[]{:S(2)}) async-start(), calls=%async_computation.14 | async-start | bytes 34603008 | tf_op jit(solution)/shard_map/all_gather | solution.py:95
  14.4 144.0 %collective-permute-start.1 = (f32[2]{0:T(128)S(1)}, f32[2]{0:T(128)S(1)}, u32[]{:S(2)}, u32[]{:S(2)}) collective-permute-start(f32[2]{0:T(128)S(1)} %slice_bitcast_fusion), channel_id=1, source_target_pairs={{0,8},{8,16},{16,24},{1,9},{9,17},{17,25},{2,10},{10,18},{18,26},{... | collective-permute-start | bytes 32 | tf_op jit(solution)/shard_map/ppermute | solution.py:23
  86.2 456.7 %copy-start.17 = (f32[2048,1]{0,1:T(1,128)}, f32[2048,1]{0,1:T(1,128)S(1)}, u32[]{:S(2)}) copy-start(f32[2048,1]{0,1:T(1,128)S(1)} %get-tuple-element.145) | copy-start | bytes 24580
  87.8 455.1 %copy-start.25 = (f32[128]{0:T(128)}, f32[128]{0:T(128)S(1)}, u32[]{:S(2)}) copy-start(f32[128]{0:T(128)S(1)} %get-tuple-element.160) | copy-start | bytes 1540
  88.9 69.6 %all-to-all-start = ((bf16[128,4,512]{2,0,1:T(8,128)(2,1)}), bf16[128,4,512]{2,0,1:T(8,128)(2,1)S(1)}, u32[]{:S(2)}, u32[]{:S(2)}) async-start(bf16[128,4,512]{2,0,1:T(8,128)(2,1)} %fusion.46), calls=%async_computation | async-start | bytes 1048576 | tf_op jit(solution)/shard_map/all_to_all | solution.py:164
  93.0 1001.5 %all-gather.17.cloned.1.call-start = ((), (), s32[]{:S(2)}) async-start(), calls=%async_computation.15 | async-start | bytes 4718592 | tf_op jit(solution)/shard_map/all_gather | solution.py:170
  542.9 11.4 copy-start.8
  543.0 4.7 copy-start.10
  543.1 3.1 collective-permute-start
  548.6 37.9 %all-to-all-start.3 = ((bf16[128,4,512]{2,0,1:T(8,128)(2,1)}), bf16[128,4,512]{2,0,1:T(8,128)(2,1)S(1)}, u32[]{:S(2)}, u32[]{:S(2)}) async-start(bf16[128,4,512]{2,0,1:T(8,128)(2,1)} %bitcast.208), calls=%async_computation.3 | async-start | bytes 1048576 | tf_op jit(solution)/shard_map/all_to_all | solution.py:165
  553.7 551.8 %all-gather.21.cloned.1.call-start = ((), (), s32[]{:S(2)}) async-start(), calls=%async_computation.17 | async-start | bytes 4718592 | tf_op jit(solution)/shard_map/all_gather | solution.py:171
  559.3 27.3 %copy-start.16 = (bf16[128,2048]{1,0:T(8,128)(2,1)}, bf16[128,2048]{1,0:T(8,128)(2,1)S(1)}, u32[]{:S(2)}) copy-start(bf16[128,2048]{1,0:T(8,128)(2,1)S(1)} %multiply_convert_fusion.3) | copy-start | bytes 1572868
  783.7 30.8 %all-to-all-start.4 = ((bf16[128,8,256]{2,0,1:T(8,128)(2,1)}), bf16[128,8,256]{2,0,1:T(8,128)(2,1)}, u32[]{:S(2)}, u32[]{:S(2)}) async-start(bf16[128,8,256]{2,0,1:T(8,128)(2,1)} %bitcast.239), calls=%async_computation.4 | async-start | bytes 1048576 | tf_op jit(solution)/shard_map/all_to_all | solution.py:183
  788.2 328.7 %all-gather.23.cloned.1.call-start = ((), (), s32[]{:S(2)}) async-start(), calls=%async_computation.18 | async-start | bytes 2621440 | tf_op jit(solution)/shard_map/all_gather | solution.py:189
  797.0 3.3 collective-permute-start.2
  814.5 311.5 %all-gather.19.cloned.1.call-start = ((), (), s32[]{:S(2)}) async-start(), calls=%async_computation.16 | async-start | bytes 7864320 | tf_op jit(solution)/shard_map/all_gather | solution.py:188
  872.9 420.0 %all-gather.29.cloned.1.call-start = ((), (), s32[]{:S(2)}) async-start(), calls=%async_computation.21 | async-start | bytes 18874368 | tf_op jit(solution)/shard_map/all_gather | solution.py:173
  902.1 426.0 %all-gather.31.cloned.1.call-start = ((), (), s32[]{:S(2)}) async-start(), calls=%async_computation.22 | async-start | bytes 2621440 | tf_op jit(solution)/shard_map/all_gather | solution.py:191
  923.5 15.7 all-to-all-start.6
  939.2 155.2 %all-to-all-start.7 = ((bf16[128,8,2048]{2,0,1:T(8,128)(2,1)}), bf16[128,8,2048]{2,0,1:T(8,128)(2,1)}, u32[]{:S(2)}, u32[]{:S(2)}) async-start(bf16[128,8,2048]{2,0,1:T(8,128)(2,1)} %pad_maximum_fusion), calls=%async_computation.7 | async-start | bytes 8388608 | tf_op jit(solution)/shard_map/all_to_all | solution.py:184
  944.7 482.4 %all-gather.25.cloned.1.call-start = ((), (), s32[]{:S(2)}) async-start(), calls=%async_computation.19 | async-start | bytes 4718592 | tf_op jit(solution)/shard_map/all_gather | solution.py:172
  945.4 586.3 %all-gather.27.cloned.1.call-start = ((), (), s32[]{:S(2)}) async-start(), calls=%async_computation.20 | async-start | bytes 20971520 | tf_op jit(solution)/shard_map/all_gather | solution.py:190
  1121.8 31.5 %all-to-all-start.5 = ((f32[8,64,256]{2,1,0:T(8,128)}), f32[8,64,256]{2,1,0:T(8,128)}, u32[]{:S(2)}, u32[]{:S(2)}) async-start(f32[8,64,256]{2,1,0:T(8,128)} %fusion.31), calls=%async_computation.5 | async-start | bytes 1048576 | tf_op jit(solution)/shard_map/all_to_all | solution.py:201
  1153.3 187.1 %all-to-all-start.2 = ((f32[8,64,768]{2,1,0:T(8,128)}), f32[8,64,768]{2,1,0:T(8,128)}, u32[]{:S(2)}, u32[]{:S(2)}) async-start(f32[8,64,768]{2,1,0:T(8,128)} %fusion.15), calls=%async_computation.2 | async-start | bytes 3145728 | tf_op jit(solution)/shard_map/all_to_all | solution.py:200
  1340.5 206.2 %all-to-all-start.11 = ((f32[8,256,256]{2,1,0:T(8,128)}), f32[8,256,256]{2,1,0:T(8,128)}, u32[]{:S(2)}, u32[]{:S(2)}) async-start(f32[8,256,256]{2,1,0:T(8,128)} %fusion.29), calls=%async_computation.11 | async-start | bytes 4194304 | tf_op jit(solution)/shard_map/all_to_all | solution.py:203
  1546.7 6.1 copy-start.22
  1546.7 225.7 %all-to-all-start.8 = ((f32[8,64,2048]{2,1,0:T(8,128)}), f32[8,64,2048]{2,1,0:T(8,128)}, u32[]{:S(2)}, u32[]{:S(2)}) async-start(f32[8,64,2048]{2,1,0:T(8,128)} %fusion.8), calls=%async_computation.8 | async-start | bytes 8388608 | tf_op jit(solution)/shard_map/all_to_all | solution.py:202
  1552.3 196.6 %reduce-scatter.4.cloned.1.call-start = ((), (), s32[]{:S(2)}) async-start(), calls=%async_computation.23 | async-start | bytes 1081344
  1567.3 13.8 copy-start.18
  1567.3 13.8 copy-start.26
  1581.1 15.5 copy-start.9
  1581.1 15.5 copy-start.11
  1581.2 15.5 copy-start.31
  1595.1 155.6 %copy-start.29 = (f32[64,2]{0,1:T(2,128)S(1)}, f32[64,2]{0,1:T(2,128)}, u32[]{:S(2)}) copy-start(f32[64,2]{0,1:T(2,128)} %param.29) | copy-start | bytes 1540
  1595.1 155.6 %copy-start.30 = (f32[64,2]{0,1:T(2,128)S(1)}, f32[64,2]{0,1:T(2,128)}, u32[]{:S(2)}) copy-start(f32[64,2]{0,1:T(2,128)} %param.25) | copy-start | bytes 1540
  1595.1 156.8 %copy-start.20 = (f32[64,3]{0,1:T(4,128)S(1)}, f32[64,3]{0,1:T(4,128)}, u32[]{:S(2)}) copy-start(f32[64,3]{0,1:T(4,128)} %param.20) | copy-start | bytes 2308
  1595.1 156.8 %copy-start.27 = (f32[64,3]{0,1:T(4,128)S(1)}, f32[64,3]{0,1:T(4,128)}, u32[]{:S(2)}) copy-start(f32[64,3]{0,1:T(4,128)} %param.28) | copy-start | bytes 2308
  1595.1 156.8 %copy-start.28 = (f32[64,3]{0,1:T(4,128)S(1)}, f32[64,3]{0,1:T(4,128)}, u32[]{:S(2)}) copy-start(f32[64,3]{0,1:T(4,128)} %param.24) | copy-start | bytes 2308
  1749.8 8.0 copy-start.24
  1750.7 7.2 copy-start.23
  1759.8 7.8 copy-start.1
  1772.4 4.9 slice-start
  1788.9 8.8 copy-start.2
  (10 other events, 21.5 us)
Sparse Core Ops, SparseCore 0:
  12.3 520.4 all-gather.12
  536.3 192.9 all-gather.14
  732.0 82.8 all-gather.16
  816.9 93.9 all-gather.20
  912.3 25.2 all-gather.22
  939.0 48.8 all-gather.18
  990.1 302.7 all-gather.28
  1294.4 21.6 all-gather.30
  1318.2 108.8 all-gather.24
  1428.5 103.2 all-gather.26
  1596.7 152.1 reduce-scatter.3
where the time goes:
time: 1870 us; the launch traced here: 1860 us
  waiting for transfers between devices  1160 us (62%)
  blocking collectives  275 us (15%)
  matrix products  169 us (9%)
  local copies, waits for them, and re-layouts  127 us (7%)
  other arithmetic  69.9 us (4%)
  starting transfers between devices  49.7 us (3%)
    all_gather x1, waiting for transfers between devices, local(): lax.all_gather(w_in.astype(jnp.bfloat16), ('seq', 'shard'), axis=0, tiled...  373 us
    unnamed x12, waiting for transfers between devices  152 us
    all_to_all x1, waiting for transfers between devices, local(): lax.all_to_all(d_gate_up, 'shard', split_axis=1, concat_axis=0, tiled=True)  149 us
    all_gather x1, waiting for transfers between devices, local(): lax.all_gather(w_down.astype(jnp.bfloat16), ('seq', 'shard'), axis=0, til...  142 us
    all_gather x1, waiting for transfers between devices, local(): lax.all_gather(left_cols[3], 'shard', axis=0, tiled=True)  135 us
    all_gather x1, waiting for transfers between devices, local(): lax.all_gather(right_cols[2], 'seq', axis=0, tiled=True)  93.3 us
    all_gather x1, waiting for transfers between devices, local(): lax.all_gather(left_cols[2], 'shard', axis=0, tiled=True)  74.7 us
    dot_general x4, matrix products, times_wide(): lax.dot_general(left, right, (((1,), (1,)), ((), ())), preferred_element_...  72.1 us
  transfers between devices with their start and end apart: 23, of which 12 were waited for; matrix products, arithmetic and copies ran while one was open for 17% of the time, Pallas kernels for 0%

commit v1 on v0

v1 whole, which is shorter than its diff:
```python
import jax
import jax.numpy as jnp
from jax import lax
from jax.sharding import Mesh
from jax.sharding import PartitionSpec as P

D = 2048
FF = 8192
TAPS = 3
STEP = 4


EPS_NORM = 1e-05
BETA_ONE = 0.9
BETA_TWO = 0.999
EPS_ADAM = 1e-08
DECAY = 0.01
RATE = 0.3

AXES = ("y", "c", "zh", "zl", "x")
GROUP = ("c", "zl", "x")
TOKENS = ("zl", "x", "c")
LOW = jnp.bfloat16
WIDE = jnp.float32


def turned(value, axis, steps):
    n = lax.axis_size(axis)
    return lax.ppermute(value, axis, [(i, (i + steps) % n) for i in range(n)])


def moved(value, axis, steps):
    n = lax.axis_size(axis)
    return lax.ppermute(
        value, axis, [(i, i + steps) for i in range(max(0, -steps), min(n, n - steps))]
    )


def after(value, *others):
    return lax.optimization_barrier((value,) + others)[0]


def picked(value, index, dim):
    return lax.dynamic_index_in_dim(value, index, dim, keepdims=False)


def to_all(value):
    n = lax.axis_size(AXES)
    return lax.all_to_all(
        jnp.broadcast_to(value[None], (n,) + value.shape), AXES, 0, 0, tiled=True
    )


def reduced(value, axis, dim):
    n = lax.axis_size(axis)
    me = lax.axis_index(axis)
    own = picked(value, me, dim)
    for k in range(1, n):
        own = own + turned(
            picked(value, (me + k) % n, dim).astype(LOW), axis, k
        ).astype(WIDE)
    return own


def gather_tokens(value):
    return lax.all_gather(value, TOKENS, axis=0, tiled=True)


def scatter_tokens(partial):
    zl, x, c = (lax.axis_size(a) for a in TOKENS)
    blocks = partial.reshape(zl, x, c, -1, partial.shape[-1])
    own = reduced(blocks, "c", 2)
    half = own.shape[2] // 2
    first = reduced(reduced(own[:, :, :half], "zl", 0), "x", 0)
    second = reduced(reduced(own[:, :, half:], "x", 1), "zl", 0)
    return jnp.concatenate([first, second], 0)


def gather_rows(value):
    ny, nzh = lax.axis_size("y"), lax.axis_size("zh")
    yi, zi = lax.axis_index("y"), lax.axis_index("zh")
    out = jnp.zeros((ny, nzh) + value.shape, value.dtype)
    far = [(0, value)] + [(k, turned(value, "zh", k)) for k in range(1, nzh)]
    tail = (0,) * value.ndim
    for k, piece in far:
        for j in range(ny):
            got = turned(piece, "y", j) if j else piece
            place = ((yi - j) % ny, (zi - k) % nzh) + tail
            out = lax.dynamic_update_slice(out, got[None, None], place)
    return out, far[-1][1]


def scatter_rows(partial):
    ny, nzh = lax.axis_size("y"), lax.axis_size("zh")
    blocks = partial.reshape(ny, nzh, -1, partial.shape[-1])
    return reduced(reduced(blocks, "y", 0), "zh", 0)


def in_group(value):
    return lax.all_to_all(value, GROUP, 0, 0, tiled=True)


def norm_forward(values, gain):
    scale = lax.rsqrt(jnp.mean(values * values, axis=-1, keepdims=True) + EPS_NORM)
    return (values * scale * gain, scale)


def norm_backward(values, scale, gain, grad):
    along = grad * gain
    inner = jnp.mean(along * values, axis=-1, keepdims=True)
    d_values = scale * along - scale * scale * scale * values * inner
    d_gain = jnp.sum(grad * values * scale, axis=0)
    return (d_values, d_gain)


def times(left, right):
    return jnp.dot(left, right, preferred_element_type=WIDE)


def times_wide(left, right):
    return lax.dot_general(
        left, right, (((1,), (1,)), ((), ())), preferred_element_type=WIDE
    )


def over_tokens(left, right):
    return lax.dot_general(
        left, right, (((0,), (0,)), ((), ())), preferred_element_type=WIDE
    )


def piece_squares(a_in, a_down, a_taps, a_gains):
    parts = [
        a_in[:, : 3 * D],
        a_in[:, 3 * D : 4 * D],
        a_in[:, 4 * D : 4 * D + FF],
        a_in[:, 4 * D + FF :],
        a_down,
        a_taps,
        a_gains[:, 0],
        a_gains[:, 1],
    ]
    return jnp.stack([jnp.sum(p * p) for p in parts])


def adam_direction(weight, grad, first, second):
    new_first = BETA_ONE * first + (1.0 - BETA_ONE) * grad
    new_second = BETA_TWO * second + (1.0 - BETA_TWO) * grad * grad
    first_hat = new_first / (1.0 - BETA_ONE**STEP)
    second_hat = new_second / (1.0 - BETA_TWO**STEP)
    direction = first_hat / (jnp.sqrt(second_hat) + EPS_ADAM) + DECAY * weight
    return (new_first, new_second, direction)


def local(
    inputs,
    out_grad,
    segments,
    w_in,
    w_down,
    conv_taps,
    norm_gains,
    m_in,
    m_down,
    m_taps,
    m_gains,
    v_in,
    v_down,
    v_taps,
    v_gains,
):
    ny, nc, nzh, nzl, nx = (lax.axis_size(a) for a in AXES)
    yi, ci, zhi, zli, xi = (lax.axis_index(a) for a in AXES)
    members = nc * nzl * nx
    copies = ny * nzh
    own = inputs.shape[0] * inputs.shape[1]
    rows = w_in.shape[0]
    wide_rows = w_down.shape[0]
    channels = copies * rows
    hidden_own = copies * wide_rows
    seqs = nzl * nx
    span = nc * own

    def spread(a):
        lead = a.shape[0]
        return a.reshape(lead, ny, nc, nzh, -1).swapaxes(2, 3).reshape(lead, D)

    def unspread(a):
        lead = a.shape[0]
        return a.reshape(lead, ny, nzh, nc, -1).swapaxes(2, 3).reshape(lead, D)

    note = jnp.concatenate(
        [norm_gains.reshape(-1), conv_taps.reshape(-1), segments.reshape(-1).astype(WIDE)]
    )
    notes = to_all(note).reshape(ny, nc, nzh, nzl, nx, -1)
    gains = notes[..., : 2 * rows].reshape(D, 2).astype(LOW).astype(WIDE)
    gain_one = gains[:, 0]
    gain_two = gains[:, 1]
    of_group = picked(picked(picked(notes, xi, 4), zli, 3), ci, 1)
    taps = of_group[..., 2 * rows : 5 * rows].reshape(channels, TAPS).astype(LOW).astype(WIDE)
    ids_all = picked(notes[..., 5 * rows :], zhi, 2)
    ids = picked(ids_all, yi, 0).transpose(1, 2, 0, 3).reshape(seqs, span)
    prev_ids = picked(ids_all, jnp.maximum(yi - 1, 0), 0)[nc - 1, :, :, own - 2 :].reshape(seqs, 2)

    low_in = w_in.astype(LOW)
    low_down = w_down.astype(LOW)

    def by_member(part, kinds, width):
        split = part.reshape(rows, kinds, ny, nc, nzh, nzl, nx, width)
        return split.transpose(3, 5, 6, 0, 1, 2, 4, 7).reshape(members, rows, -1)

    def from_member(got, kinds, width):
        split = got.reshape(nc, nzl, nx, rows, kinds, ny, nzh, width)
        return split.transpose(3, 4, 5, 0, 6, 1, 2, 7).reshape(rows, -1)

    cols_p = in_group(by_member(low_in[:, : 3 * D], 3, rows))
    cols_gate = in_group(by_member(low_in[:, 4 * D : 4 * D + FF], 1, wide_rows))
    cols_up = in_group(by_member(low_in[:, 4 * D + FF :], 1, wide_rows))
    full_p, last = gather_rows(cols_p)
    full_p = full_p.reshape(D, 3 * channels)
    full_o, last = gather_rows(after(low_in[:, 3 * D : 4 * D], last))
    full_o = full_o.reshape(channels, D)
    full_gate, last = gather_rows(after(cols_gate, last))
    full_gate = full_gate.reshape(D, hidden_own)
    full_up, last = gather_rows(after(cols_up, last))
    full_up = full_up.reshape(D, hidden_own)
    full_down, last = gather_rows(after(low_down, last))
    full_down = full_down.reshape(hidden_own, D)

    values = inputs.reshape(own, D).astype(WIDE)
    norm_one, scale_one = norm_forward(values, gain_one)
    h_one = gather_tokens(spread(norm_one.astype(LOW)))
    grad_low = out_grad.reshape(own, D)
    grad_top = grad_low.astype(WIDE)
    d_ffn = gather_tokens(after(grad_low, h_one))
    bcx = times(h_one, full_p).reshape(seqs, span, 3, channels)
    b_part = bcx[:, :, 0]
    c_part = bcx[:, :, 1]
    x_part = bcx[:, :, 2]
    mixed_in = b_part * x_part
    prev_rows = moved(mixed_in[:, -2:], "y", 1)
    extended = jnp.concatenate([prev_rows, mixed_in], 1)
    ext_ids = jnp.concatenate([prev_ids, ids], 1)
    keeps = []
    conv = jnp.zeros((seqs, span, channels), WIDE)
    for lag in range(TAPS):
        keep = (ext_ids[:, 2 - lag : 2 - lag + span] == ids).astype(WIDE)[:, :, None]
        keeps.append(keep)
        conv = conv + taps[:, lag] * extended[:, 2 - lag : 2 - lag + span] * keep
    y_mix = (c_part * conv).astype(LOW).reshape(seqs * span, channels)
    middle = values + scatter_tokens(times(y_mix, full_o))

    norm_two, scale_two = norm_forward(middle, gain_two)
    h_two = gather_tokens(spread(norm_two.astype(LOW)))
    gate = times(h_two, full_gate)
    up_part = times(h_two, full_up)
    sig = jax.nn.sigmoid(gate)
    activated = gate * sig
    hidden = (activated * up_part).astype(LOW)
    d_hidden = times_wide(d_ffn, full_down)
    d_gate = (d_hidden * up_part * sig * (1.0 + gate * (1.0 - sig))).astype(LOW)
    d_up = (d_hidden * activated).astype(LOW)
    d_h_two = unspread(scatter_tokens(times_wide(d_gate, full_gate) + times_wide(d_up, full_up)))
    d_middle, d_gain_two = norm_backward(middle, scale_two, gain_two, d_h_two)
    d_middle = d_middle + grad_top

    d_branch = gather_tokens(d_middle.astype(LOW))
    d_mix = times_wide(d_branch, full_o).reshape(seqs, span, channels)
    d_c = d_mix * conv
    d_conv = d_mix * c_part
    d_extended = jnp.zeros((seqs, span + 2, channels), WIDE)
    tap_grads = []
    for lag in range(TAPS):
        counted = d_conv * keeps[lag]
        tap_grads.append(jnp.sum(counted * extended[:, 2 - lag : 2 - lag + span], axis=(0, 1)))
        d_extended = d_extended + jnp.pad(taps[:, lag] * counted, ((0, 0), (2 - lag, lag), (0, 0)))
    back_state = moved(d_extended[:, :2], "y", -1)
    d_mixed_in = d_extended[:, 2:] + jnp.pad(back_state, ((0, 0), (span - 2, 0), (0, 0)))
    d_bcx = jnp.stack([d_mixed_in * x_part, d_c, d_mixed_in * b_part], 2)
    d_bcx = d_bcx.astype(LOW).reshape(seqs * span, 3 * channels)
    d_h_one = unspread(scatter_tokens(times_wide(d_bcx, full_p)))
    d_values, d_gain_one = norm_backward(values, scale_one, gain_one, d_h_one)
    input_grad = (d_values + d_middle).reshape(inputs.shape)
    result = middle + scatter_tokens(times(hidden, full_down))
    block_out = result.astype(LOW).reshape(inputs.shape)

    def owned(partial, kinds, width):
        mine = scatter_rows(partial).astype(LOW)
        return from_member(in_group(mine.reshape(members, rows, -1)), kinds, width)

    grad_down = scatter_rows(over_tokens(hidden, d_ffn))
    grad_gate = owned(over_tokens(h_two, d_gate), 1, wide_rows)
    grad_up = owned(over_tokens(h_two, d_up), 1, wide_rows)
    grad_o = scatter_rows(over_tokens(y_mix, d_branch))
    grad_p = owned(over_tokens(h_one, d_bcx), 3, rows)
    grad_in = jnp.concatenate(
        [grad_p.astype(WIDE), grad_o, grad_gate.astype(WIDE), grad_up.astype(WIDE)], 1
    )
    gain_terms = jnp.stack([d_gain_one, d_gain_two], 1).reshape(-1, rows, 2)
    grad_gains = jnp.sum(lax.all_to_all(gain_terms, AXES, 0, 0, tiled=True), axis=0)
    tap_terms = jnp.stack(tap_grads, 1).reshape(copies, rows, TAPS)
    grad_taps = jnp.sum(lax.all_to_all(tap_terms, ("y", "zh"), 0, 0, tiled=True), axis=0)

    new_m_in, new_v_in, dir_in = adam_direction(w_in, grad_in, m_in, v_in)
    new_m_down, new_v_down, dir_down = adam_direction(w_down, grad_down, m_down, v_down)
    new_m_taps, new_v_taps, dir_taps = adam_direction(conv_taps, grad_taps, m_taps, v_taps)
    new_m_gains, new_v_gains, dir_gains = adam_direction(norm_gains, grad_gains, m_gains, v_gains)
    squares = jnp.stack(
        [
            piece_squares(w_in, w_down, conv_taps, norm_gains),
            piece_squares(dir_in, dir_down, dir_taps, dir_gains),
        ]
    )
    lamb_norms = jnp.sqrt(jnp.sum(to_all(squares), axis=0))
    ratio = -RATE * lamb_norms[0] / (lamb_norms[1] + 1e-06)
    ratio_cols = jnp.concatenate(
        [
            jnp.full((3 * D,), ratio[0]),
            jnp.full((D,), ratio[1]),
            jnp.full((FF,), ratio[2]),
            jnp.full((FF,), ratio[3]),
        ]
    )
    new_w_in = w_in + dir_in * ratio_cols[None, :]
    new_w_down = w_down + dir_down * ratio[4]
    new_w_taps = conv_taps + dir_taps * ratio[5]
    new_w_gains = norm_gains + dir_gains * jnp.stack([ratio[6], ratio[7]])[None, :]
    return (
        block_out,
        input_grad,
        grad_in,
        grad_down,
        grad_taps,
        grad_gains,
        new_m_in,
        new_m_down,
        new_m_taps,
        new_m_gains,
        new_v_in,
        new_v_down,
        new_v_taps,
        new_v_gains,
        new_w_in,
        new_w_down,
        new_w_taps,
        new_w_gains,
        lamb_norms,
    )


def solution(mesh):
    seq, shard = mesh.shape["seq"], mesh.shape["shard"]
    grid = Mesh(mesh.devices.reshape(seq // 2, 2, 2, 2, shard // 4), AXES)
    tokens = P(("zh", "zl", "x"), ("y", "c"), None)
    weights = P(AXES, None)
    return jax.shard_map(
        local,
        mesh=grid,
        in_specs=(tokens, tokens, P(("zh", "zl", "x"), ("y", "c"))) + (weights,) * 12,
        out_specs=(tokens, tokens) + (weights,) * 16 + (P(),),
        check_vma=False,
    )
```

time: 1870 us -> 1030 us (0.55)
  waiting for transfers between devices: 1160 us -> 446 us
  blocking collectives: 275 us -> 0 us
  local copies, waits for them, and re-layouts: 127 us -> 231 us
  matrix products: 169 us -> 90.5 us
  other arithmetic: 69.9 us -> 128 us
  starting transfers between devices: 49.7 us -> 99 us
    all_gather x10 -> x4, waiting for transfers between devices: 818 us -> 0.03 us  [gather_tokens(): return lax.all_gather(value, TOKENS, axis=0, tiled=True)]
    ppermute x3 -> x47, waiting for transfers between devices: 1.3 us -> 387 us  [the longest x45 386 us: turned(): return lax.ppermute(value, axis, [(i, (i + steps) % n) for i in range(n)])]
    unnamed x12 -> x4, waiting for transfers between devices: 152 us -> 0.07 us
    all_gather x2 -> x0, blocking collectives: 134 us -> none  [the longest x1 69.3 us: local(): lax.all_gather(norm_gains.astype(jnp.bfloat16), ('seq', 'shard'), axis=0,...]
    all_to_all x9 -> x10, waiting for transfers between devices: 187 us -> 58.9 us  [the longest x6 48.2 us: in_group(): return lax.all_to_all(value, GROUP, 0, 0, tiled=True)]
    all_to_all x3 -> x0, blocking collectives: 104 us -> none  [the longest x1 56.7 us: local(): lax.all_to_all(d_bcx, 'shard', split_axis=1, concat_axis=0, tiled=True)]
    convert_element_type x4 -> x46, local copies, waits for them, and re-layouts: 1.12 us -> 84.4 us  [the longest x30 27.1 us: reduced(): picked(value, (me + k) % n, dim).astype(LOW)]
    ppermute x3 -> x47, starting transfers between devices: 6.19 us -> 55.7 us  [the longest x45 51.1 us: turned(): return lax.ppermute(value, axis, [(i, (i + steps) % n) for i in range(n)])]
  transfers between devices with their start and end apart: 23 -> 61, of which waited for: 12 -> 30; matrix products, arithmetic and copies ran while one was open for 17% -> 31% of each run, Pallas kernels for 0% -> 0%
where the time goes in v1:
time: 1030 us; the launch traced here: 1010 us
  waiting for transfers between devices  446 us (43%)
  local copies, waits for them, and re-layouts  231 us (22%)
  other arithmetic  128 us (12%)
  starting transfers between devices  99 us (10%)
  matrix products  90.5 us (9%)
  between operations  16 us (2%)
    ppermute x45, waiting for transfers between devices, turned(): return lax.ppermute(value, axis, [(i, (i + steps) % n) for i in range(n)])  386 us
    ppermute x45, starting transfers between devices, turned(): return lax.ppermute(value, axis, [(i, (i + steps) % n) for i in range(n)])  51.1 us
    all_to_all x6, waiting for transfers between devices, in_group(): return lax.all_to_all(value, GROUP, 0, 0, tiled=True)  48.2 us
    dot_general x5, matrix products, times_wide(): lax.dot_general(left, right, (((1,), (1,)), ((), ())), preferred_element_...  36.2 us
    add x24, other arithmetic, reduced(): own + turned(picked(value, (me + k) % n, dim).astype(LOW), axis, k).astyp...  32.8 us
    dot_general x5, matrix products, times(): return jnp.dot(left, right, preferred_element_type=WIDE)  31.3 us
    convert_element_type x30, local copies, waits for them, and re-layouts, reduced(): picked(value, (me + k) % n, dim).astype(LOW)  27.1 us
    unnamed x201, local copies, waits for them, and re-layouts  26.8 us
  transfers between devices with their start and end apart: 61, of which 30 were waited for; matrix products, arithmetic and copies ran while one was open for 31% of the time, Pallas kernels for 0%

profile of v1, /device:TPU:0, one launch (start us, length us, event | category | flops | bytes accessed | tf_op | source)
XLA Modules:
  0.0 1010.8 jit_solution(2187873159287997716)
XLA Ops:
  10.4 7.3 all-to-all-start
  50.6 14.3 %all-to-all-done.1 = bf16[8,64,768]{2,1,0:T(8,128)(2,1)S(1)} async-done(((bf16[8,64,768]{2,1,0:T(8,128)(2,1)}), bf16[8,64,768]{2,1,0:T(8,128)(2,1)S(1)}, u32[]{:S(2)}, u32[]{:S(2)}) %all-to-all-start.1) | async-done | bytes 786464 | tf_op jit(solution)/shard_map/all_to_all | solution.py:100
  72.2 29.7 %collective-permute-done.1 = bf16[8,64,768]{2,1,0:T(8,128)(2,1)} collective-permute-done((bf16[8,64,768]{2,1,0:T(8,128)(2,1)S(1)}, bf16[8,64,768]{2,1,0:T(8,128)(2,1)}, u32[]{:S(2)}, u32[]{:S(2)}) %collective-permute-start.1) | collective-permute-done | bytes 786464 | tf_op jit(solution)/shard_map/ppermute | solution.py:29
  107.2 8.3 collective-permute-done.5
  117.0 10.9 %collective-permute-done.2 = bf16[8,64,768]{2,1,0:T(8,128)(2,1)S(1)} collective-permute-done((bf16[8,64,768]{2,1,0:T(8,128)(2,1)}, bf16[8,64,768]{2,1,0:T(8,128)(2,1)S(1)}, u32[]{:S(2)}, u32[]{:S(2)}) %collective-permute-start.2) | collective-permute-done | bytes 786464 | tf_op jit(solution)/shard_map/ppermute | solution.py:29
  128.9 4.6 copy.220
  133.5 6.2 fusion.74
  180.2 10.5 %collective-permute-done.8 = bf16[2,64,2048]{2,1,0:T(8,128)(2,1)} collective-permute-done((bf16[2,64,2048]{2,1,0:T(8,128)(2,1)}, bf16[2,64,2048]{2,1,0:T(8,128)(2,1)}, u32[]{:S(2)}, u32[]{:S(2)}) %collective-permute-start.8) | collective-permute-done | bytes 524320 | tf_op jit(solution)/shard_map/ppermute | solution.py:29
  192.3 14.3 %collective-permute-done.10 = bf16[2,64,2048]{2,1,0:T(8,128)(2,1)S(1)} collective-permute-done((bf16[2,64,2048]{2,1,0:T(8,128)(2,1)S(1)}, bf16[2,64,2048]{2,1,0:T(8,128)(2,1)S(1)}, u32[]{:S(2)}, u32[]{:S(2)}) %collective-permute-start.10) | collective-permute-done | bytes 524320 | tf_op jit(solution)/shard_map/ppermute | solution.py:29
  206.9 5.0 collective-permute-done.9
  246.1 34.0 %all-to-all-done.3 = bf16[8,64,1024]{2,1,0:T(8,128)(2,1)} async-done(((bf16[8,64,1024]{2,1,0:T(8,128)(2,1)}), bf16[8,64,1024]{2,1,0:T(8,128)(2,1)}, u32[]{:S(2)}, u32[]{:S(2)}) %all-to-all-start.3) | async-done | bytes 1048608 | tf_op jit(solution)/shard_map/all_to_all | solution.py:100
  280.1 4.5 collective-permute-start.15
  291.2 39.8 %collective-permute-done.16 = bf16[8,64,1024]{2,1,0:T(8,128)(2,1)S(1)} collective-permute-done((bf16[8,64,1024]{2,1,0:T(8,128)(2,1)}, bf16[8,64,1024]{2,1,0:T(8,128)(2,1)S(1)}, u32[]{:S(2)}, u32[]{:S(2)}) %collective-permute-start.16) | collective-permute-done | bytes 1048608 | tf_op jit(solution)/shard_map/ppermute | solution.py:29
  337.3 41.4 %collective-permute-done.19 = bf16[256,2048]{1,0:T(8,128)(2,1)S(1)} collective-permute-done((bf16[256,2048]{1,0:T(8,128)(2,1)S(1)}, bf16[256,2048]{1,0:T(8,128)(2,1)S(1)}, u32[]{:S(2)}, u32[]{:S(2)}) %collective-permute-start.19) | collective-permute-done | bytes 1048608 | tf_op jit(solution)/shard_map/ppermute | solution.py:29
  382.5 21.3 %collective-permute-done.20 = bf16[256,2048]{1,0:T(8,128)(2,1)S(1)} collective-permute-done((bf16[256,2048]{1,0:T(8,128)(2,1)S(1)}, bf16[256,2048]{1,0:T(8,128)(2,1)S(1)}, u32[]{:S(2)}, u32[]{:S(2)}) %collective-permute-start.20) | collective-permute-done | bytes 1048608 | tf_op jit(solution)/shard_map/ppermute | solution.py:29
  404.8 6.6 copy.243
  413.4 10.0 fusion.78
  423.5 7.7 fusion.76
  431.2 9.3 multiply_convert_fusion.1
  440.6 6.8 fusion.79
  447.4 8.0 convolution_add_fusion
  457.6 4.7 fusion.84
  468.2 4.6 fusion.82
  476.9 6.7 fusion.77
  486.7 6.6 fusion.83
  519.9 5.1 collective-permute-done.29
  535.8 4.5 collective-permute-done.30
  572.3 31.7 %collective-permute-done.43 = bf16[2,512,1024]{2,1,0:T(8,128)(2,1)S(1)} collective-permute-done((bf16[2,512,1024]{2,1,0:T(8,128)(2,1)S(1)}, bf16[2,512,1024]{2,1,0:T(8,128)(2,1)S(1)}, u32[]{:S(2)}, u32[]{:S(2)}) %collective-permute-start.43) | collective-permute-done | bytes 2097184 | tf_op jit(solution)/shard_map/ppermute | solution.py:29
  606.7 40.6 %collective-permute-done.42 = bf16[512,1024]{1,0:T(8,128)(2,1)S(1)} collective-permute-done((bf16[512,1024]{1,0:T(8,128)(2,1)S(1)}, bf16[512,1024]{1,0:T(8,128)(2,1)S(1)}, u32[]{:S(2)}, u32[]{:S(2)}) %collective-permute-start.42) | collective-permute-done | bytes 1048608 | tf_op jit(solution)/shard_map/ppermute | solution.py:29
  660.9 18.1 %collective-permute-done.24 = bf16[2,64,2048]{2,1,0:T(8,128)(2,1)S(1)} collective-permute-done((bf16[2,64,2048]{2,1,0:T(8,128)(2,1)S(1)}, bf16[2,64,2048]{2,1,0:T(8,128)(2,1)S(1)}, u32[]{:S(2)}, u32[]{:S(2)}) %collective-permute-start.24) | collective-permute-done | bytes 524320 | tf_op jit(solution)/shard_map/ppermute | solution.py:29
  680.1 23.7 %collective-permute-done.44 = bf16[512,1024]{1,0:T(8,128)(2,1)S(1)} collective-permute-done((bf16[512,1024]{1,0:T(8,128)(2,1)S(1)}, bf16[512,1024]{1,0:T(8,128)(2,1)S(1)}, u32[]{:S(2)}, u32[]{:S(2)}) %collective-permute-start.44) | collective-permute-done | bytes 1048608 | tf_op jit(solution)/shard_map/ppermute | solution.py:29
  717.3 12.4 %collective-permute-done.25 = bf16[64,2048]{1,0:T(8,128)(2,1)} collective-permute-done((bf16[64,2048]{1,0:T(8,128)(2,1)}, bf16[64,2048]{1,0:T(8,128)(2,1)}, u32[]{:S(2)}, u32[]{:S(2)}) %collective-permute-start.25) | collective-permute-done | bytes 262176 | tf_op jit(solution)/shard_map/ppermute | solution.py:29
  731.7 6.9 multiply_reduce_fusion.1
  742.7 4.5 copy.248
  755.2 4.5 copy.249
  764.3 5.5 multiply_reduce_fusion.8
  782.5 5.3 reshape.582
  787.8 5.9 fusion.80
  812.5 5.9 fusion.81
  826.8 27.3 %collective-permute-done.37 = bf16[2,512,768]{2,1,0:T(8,128)(2,1)S(1)} collective-permute-done((bf16[2,512,768]{2,1,0:T(8,128)(2,1)S(1)}, bf16[2,512,768]{2,1,0:T(8,128)(2,1)S(1)}, u32[]{:S(2)}, u32[]{:S(2)}) %collective-permute-start.37) | collective-permute-done | bytes 1572896 | tf_op jit(solution)/shard_map/ppermute | solution.py:29
  859.6 11.7 %collective-permute-done.35 = bf16[2,64,2048]{2,1,0:T(8,128)(2,1)S(1)} collective-permute-done((bf16[2,64,2048]{2,1,0:T(8,128)(2,1)S(1)}, bf16[2,64,2048]{2,1,0:T(8,128)(2,1)S(1)}, u32[]{:S(2)}, u32[]{:S(2)}) %collective-permute-start.35) | collective-permute-done | bytes 524320 | tf_op jit(solution)/shard_map/ppermute | solution.py:29
  874.2 18.6 %collective-permute-done.36 = bf16[64,2048]{1,0:T(8,128)(2,1)S(1)} collective-permute-done((bf16[64,2048]{1,0:T(8,128)(2,1)S(1)}, bf16[64,2048]{1,0:T(8,128)(2,1)S(1)}, u32[]{:S(2)}, u32[]{:S(2)}) %collective-permute-start.36) | collective-permute-done | bytes 262176 | tf_op jit(solution)/shard_map/ppermute | solution.py:29
  916.1 5.0 stack.124
  933.9 6.0 copy.287
  939.9 5.2 reshape.568
  945.1 18.2 %multiply_add_fusion.1 = (f32[64,24576]{1,0:T(8,128)}, f32[64,24576]{1,0:T(8,128)}, f32[64,24576]{1,0:T(8,128)}, f32[64,24576]{1,0:T(8,128)}) fusion(f32[64,24576]{1,0:T(8,128)} %param.18, f32[64,24576]{1,0:T(8,128)} %param.26, f32[64,24576]{1,0:T(8,128)} %param.22, f32[64,8192]{1,0:T(8,128)} %reshape.570, f32[64,8192]{1,0:T(8,128)} %reshape.569, ...), kind=kLoop, calls=%fused_computation.4 | loop fusion | flops 25165824 | bytes 50331648 | tf_op jit(solution)/shard_map/add | solution.py:151
  971.1 5.2 stack.134
  991.6 8.2 multiply_add_fusion
  (524 shorter events, 391.5 us)
Async XLA Ops:
  17.7 115.8 %all-gather.5.cloned.1.call-start = ((), (), s32[]{:S(2)}) async-start(), calls=%async_computation.10 | async-start | bytes 4718592 | tf_op jit(solution)/shard_map/all_gather | solution.py:66
  45.4 19.4 %all-to-all-start.1 = ((bf16[8,64,768]{2,1,0:T(8,128)(2,1)}), bf16[8,64,768]{2,1,0:T(8,128)(2,1)S(1)}, u32[]{:S(2)}, u32[]{:S(2)}) async-start(bf16[8,64,768]{2,1,0:T(8,128)(2,1)} %reshape.538), calls=%async_computation.1 | async-start | bytes 1572864 | tf_op jit(solution)/shard_map/all_to_all | solution.py:100
  49.0 364.5 %all-gather.9.cloned.1.call-start = ((), (), s32[]{:S(2)}) async-start(), calls=%async_computation.12 | async-start | bytes 4718592 | tf_op jit(solution)/shard_map/all_gather | solution.py:66
  64.8 37.1 %collective-permute-start.1 = (bf16[8,64,768]{2,1,0:T(8,128)(2,1)S(1)}, bf16[8,64,768]{2,1,0:T(8,128)(2,1)}, u32[]{:S(2)}, u32[]{:S(2)}) collective-permute-start(bf16[8,64,768]{2,1,0:T(8,128)(2,1)S(1)} %all-to-all-done.1), channel_id=1, source_target_pairs={{0,4},{4,0},{1,5},{5,1},{2,6},{6,2},{3,7},{7,3},{8,12},{12,8},{9,1... | collective-permute-start | bytes 2359304 | tf_op jit(solution)/shard_map/ppermute | solution.py:29
  67.2 36.7 %collective-permute-start = (bf16[8,64,768]{2,1,0:T(8,128)(2,1)S(1)}, bf16[8,64,768]{2,1,0:T(8,128)(2,1)S(1)}, u32[]{:S(2)}, u32[]{:S(2)}) collective-permute-start(bf16[8,64,768]{2,1,0:T(8,128)(2,1)S(1)} %all-to-all-done.1), channel_id=1, source_target_pairs={{0,16},{16,0},{1,17},{17,1},{2,18},{18,2},{3,19},{19,3},{4,20},{20... | collective-permute-start | bytes 2359304 | tf_op jit(solution)/shard_map/ppermute | solution.py:29
  103.4 24.5 %collective-permute-start.2 = (bf16[8,64,768]{2,1,0:T(8,128)(2,1)}, bf16[8,64,768]{2,1,0:T(8,128)(2,1)S(1)}, u32[]{:S(2)}, u32[]{:S(2)}) collective-permute-start(bf16[8,64,768]{2,1,0:T(8,128)(2,1)} %collective-permute-done.1), channel_id=1, source_target_pairs={{0,16},{16,0},{1,17},{17,1},{2,18},{18,2},{3,19},{19,3},{4,20},{20... | collective-permute-start | bytes 2359304 | tf_op jit(solution)/shard_map/ppermute | solution.py:29
  115.5 27.9 %collective-permute-start.6 = (bf16[64,2048]{1,0:T(8,128)(2,1)S(1)}, bf16[64,2048]{1,0:T(8,128)(2,1)S(1)}, u32[]{:S(2)}, u32[]{:S(2)}) collective-permute-start(bf16[64,2048]{1,0:T(8,128)(2,1)S(1)} %collective-permute-done.5), channel_id=1, source_target_pairs={{0,16},{16,0},{1,17},{17,1},{2,18},{18,2},{3,19},{19,3},{4,20},{20... | collective-permute-start | bytes 786440 | tf_op jit(solution)/shard_map/ppermute | solution.py:29
  163.1 27.6 %collective-permute-start.8 = (bf16[2,64,2048]{2,1,0:T(8,128)(2,1)}, bf16[2,64,2048]{2,1,0:T(8,128)(2,1)}, u32[]{:S(2)}, u32[]{:S(2)}) collective-permute-start(bf16[2,64,2048]{2,1,0:T(8,128)(2,1)} %fusion.28), channel_id=1, source_target_pairs={{0,2},{2,0},{1,3},{3,1},{4,6},{6,4},{5,7},{7,5},{8,10},{10,8},{9,1... | collective-permute-start | bytes 1572872 | tf_op jit(solution)/shard_map/ppermute | solution.py:29
  170.7 58.8 %all-to-all-start.2 = ((bf16[8,64,1024]{2,1,0:T(8,128)(2,1)}), bf16[8,64,1024]{2,1,0:T(8,128)(2,1)}, u32[]{:S(2)}, u32[]{:S(2)}) async-start(bf16[8,64,1024]{2,1,0:T(8,128)(2,1)} %reshape.544), calls=%async_computation.2 | async-start | bytes 2097152 | tf_op jit(solution)/shard_map/all_to_all | solution.py:100
  175.0 248.5 %all-gather.7.cloned.1.call-start = ((), (), s32[]{:S(2)}) async-start(), calls=%async_computation.11 | async-start | bytes 4718592 | tf_op jit(solution)/shard_map/all_gather | solution.py:66
  178.2 28.4 %collective-permute-start.10 = (bf16[2,64,2048]{2,1,0:T(8,128)(2,1)S(1)}, bf16[2,64,2048]{2,1,0:T(8,128)(2,1)S(1)}, u32[]{:S(2)}, u32[]{:S(2)}) collective-permute-start(bf16[2,64,2048]{2,1,0:T(8,128)(2,1)S(1)} %fusion.29), channel_id=1, source_target_pairs={{0,1},{1,0},{2,3},{3,2},{4,5},{5,4},{6,7},{7,6},{8,9},{9,8},{10,11... | collective-permute-start | bytes 1572872 | tf_op jit(solution)/shard_map/ppermute | solution.py:29
  192.3 19.7 %collective-permute-start.9 = (bf16[64,2048]{1,0:T(8,128)(2,1)S(1)}, bf16[64,2048]{1,0:T(8,128)(2,1)S(1)}, u32[]{:S(2)}, u32[]{:S(2)}) collective-permute-start(bf16[64,2048]{1,0:T(8,128)(2,1)S(1)} %fusion.46), channel_id=1, source_target_pairs={{0,1},{1,0},{2,3},{3,2},{4,5},{5,4},{6,7},{7,6},{8,9},{9,8},{10,11... | collective-permute-start | bytes 786440 | tf_op jit(solution)/shard_map/ppermute | solution.py:29
  229.5 50.6 %all-to-all-start.3 = ((bf16[8,64,1024]{2,1,0:T(8,128)(2,1)}), bf16[8,64,1024]{2,1,0:T(8,128)(2,1)}, u32[]{:S(2)}, u32[]{:S(2)}) async-start(bf16[8,64,1024]{2,1,0:T(8,128)(2,1)} %reshape.547), calls=%async_computation.3 | async-start | bytes 2097152 | tf_op jit(solution)/shard_map/all_to_all | solution.py:100
  233.9 530.3 %all-gather.11.cloned.1.call-start = ((), (), s32[]{:S(2)}) async-start(), calls=%async_computation.13 | async-start | bytes 4718592 | tf_op jit(solution)/shard_map/all_gather | solution.py:66
  233.9 46.1 %collective-permute-start.13 = (bf16[8,64,1024]{2,1,0:T(8,128)(2,1)}, bf16[8,64,1024]{2,1,0:T(8,128)(2,1)}, u32[]{:S(2)}, u32[]{:S(2)}) collective-permute-start(bf16[8,64,1024]{2,1,0:T(8,128)(2,1)} %all-to-all-done.2), channel_id=1, source_target_pairs={{0,4},{4,0},{1,5},{5,1},{2,6},{6,2},{3,7},{7,3},{8,12},{12,8},{9,1... | collective-permute-start | bytes 3145736 | tf_op jit(solution)/shard_map/ppermute | solution.py:29
  238.6 49.9 %collective-permute-start.12 = (bf16[8,64,1024]{2,1,0:T(8,128)(2,1)}, bf16[8,64,1024]{2,1,0:T(8,128)(2,1)}, u32[]{:S(2)}, u32[]{:S(2)}) collective-permute-start(bf16[8,64,1024]{2,1,0:T(8,128)(2,1)} %all-to-all-done.2), channel_id=1, source_target_pairs={{0,16},{16,0},{1,17},{17,1},{2,18},{18,2},{3,19},{19,3},{4,20},{20... | collective-permute-start | bytes 3145736 | tf_op jit(solution)/shard_map/ppermute | solution.py:29
  280.1 53.0 %collective-permute-start.15 = (bf16[8,64,1024]{2,1,0:T(8,128)(2,1)}, bf16[8,64,1024]{2,1,0:T(8,128)(2,1)S(1)}, u32[]{:S(2)}, u32[]{:S(2)}) collective-permute-start(bf16[8,64,1024]{2,1,0:T(8,128)(2,1)} %all-to-all-done.3), channel_id=1, source_target_pairs={{0,16},{16,0},{1,17},{17,1},{2,18},{18,2},{3,19},{19,3},{4,20},{20... | collective-permute-start | bytes 3145736 | tf_op jit(solution)/shard_map/ppermute | solution.py:29
  284.5 46.4 %collective-permute-start.16 = (bf16[8,64,1024]{2,1,0:T(8,128)(2,1)}, bf16[8,64,1024]{2,1,0:T(8,128)(2,1)S(1)}, u32[]{:S(2)}, u32[]{:S(2)}) collective-permute-start(bf16[8,64,1024]{2,1,0:T(8,128)(2,1)} %all-to-all-done.3), channel_id=1, source_target_pairs={{0,4},{4,0},{1,5},{5,1},{2,6},{6,2},{3,7},{7,3},{8,12},{12,8},{9,1... | collective-permute-start | bytes 3145736 | tf_op jit(solution)/shard_map/ppermute | solution.py:29
  286.4 46.8 %collective-permute-start.14 = (bf16[8,64,1024]{2,1,0:T(8,128)(2,1)}, bf16[8,64,1024]{2,1,0:T(8,128)(2,1)S(1)}, u32[]{:S(2)}, u32[]{:S(2)}) collective-permute-start(bf16[8,64,1024]{2,1,0:T(8,128)(2,1)} %collective-permute-done.13), channel_id=1, source_target_pairs={{0,16},{16,0},{1,17},{17,1},{2,18},{18,2},{3,19},{19,3},{4,20},{20... | collective-permute-start | bytes 3145736 | tf_op jit(solution)/shard_map/ppermute | solution.py:29
  331.0 48.9 %collective-permute-start.18 = (bf16[256,2048]{1,0:T(8,128)(2,1)S(1)}, bf16[256,2048]{1,0:T(8,128)(2,1)S(1)}, u32[]{:S(2)}, u32[]{:S(2)}) collective-permute-start(bf16[256,2048]{1,0:T(8,128)(2,1)S(1)} %copy-done.39), channel_id=1, source_target_pairs={{0,16},{16,0},{1,17},{17,1},{2,18},{18,2},{3,19},{19,3},{4,20},{20... | collective-permute-start | bytes 3145736 | tf_op jit(solution)/shard_map/ppermute | solution.py:29
  332.0 46.7 %collective-permute-start.19 = (bf16[256,2048]{1,0:T(8,128)(2,1)S(1)}, bf16[256,2048]{1,0:T(8,128)(2,1)S(1)}, u32[]{:S(2)}, u32[]{:S(2)}) collective-permute-start(bf16[256,2048]{1,0:T(8,128)(2,1)S(1)} %copy-done.39), channel_id=1, source_target_pairs={{0,4},{4,0},{1,5},{5,1},{2,6},{6,2},{3,7},{7,3},{8,12},{12,8},{9,1... | collective-permute-start | bytes 3145736 | tf_op jit(solution)/shard_map/ppermute | solution.py:29
  332.0 47.8 %collective-permute-start.17 = (bf16[8,64,1024]{2,1,0:T(8,128)(2,1)S(1)}, bf16[8,64,1024]{2,1,0:T(8,128)(2,1)S(1)}, u32[]{:S(2)}, u32[]{:S(2)}) collective-permute-start(bf16[8,64,1024]{2,1,0:T(8,128)(2,1)S(1)} %collective-permute-done.16), channel_id=1, source_target_pairs={{0,16},{16,0},{1,17},{17,1},{2,18},{18,2},{3,19},{19,3},{4,20},{20... | collective-permute-start | bytes 3145736 | tf_op jit(solution)/shard_map/ppermute | solution.py:29
  378.7 25.1 %collective-permute-start.20 = (bf16[256,2048]{1,0:T(8,128)(2,1)S(1)}, bf16[256,2048]{1,0:T(8,128)(2,1)S(1)}, u32[]{:S(2)}, u32[]{:S(2)}) collective-permute-start(bf16[256,2048]{1,0:T(8,128)(2,1)S(1)} %collective-permute-done.19), channel_id=1, source_target_pairs={{0,16},{16,0},{1,17},{17,1},{2,18},{18,2},{3,19},{19,3},{4,20},{20... | collective-permute-start | bytes 3145736 | tf_op jit(solution)/shard_map/ppermute | solution.py:29
  455.7 37.6 %collective-permute-start.26 = (bf16[2,2,128,2048]{3,2,1,0:T(8,128)(2,1)S(1)}, bf16[2,2,128,2048]{3,2,1,0:T(8,128)(2,1)S(1)}, u32[]{:S(2)}, u32[]{:S(2)}) collective-permute-start(bf16[2,2,128,2048]{3,2,1,0:T(8,128)(2,1)S(1)} %fusion.11), channel_id=1, source_target_pairs={{0,8},{8,0},{1,9},{9,1},{2,10},{10,2},{3,11},{11,3},{4,12},{12,4},... | collective-permute-start | bytes 6291464 | tf_op jit(solution)/shard_map/ppermute | solution.py:29
  467.2 86.2 %collective-permute-start.45 = (bf16[2,256,2048]{2,1,0:T(8,128)(2,1)}, bf16[2,256,2048]{2,1,0:T(8,128)(2,1)}, u32[]{:S(2)}, u32[]{:S(2)}) collective-permute-start(bf16[2,256,2048]{2,1,0:T(8,128)(2,1)} %fusion.9), channel_id=1, source_target_pairs={{0,16},{16,0},{1,17},{17,1},{2,18},{18,2},{3,19},{19,3},{4,20},{20... | collective-permute-start | bytes 6291464 | tf_op jit(solution)/shard_map/ppermute | solution.py:29
  474.7 86.3 %collective-permute-start.41 = (bf16[2,512,1024]{2,1,0:T(8,128)(2,1)}, bf16[2,512,1024]{2,1,0:T(8,128)(2,1)}, u32[]{:S(2)}, u32[]{:S(2)}) collective-permute-start(bf16[2,512,1024]{2,1,0:T(8,128)(2,1)} %fusion.7), channel_id=1, source_target_pairs={{0,16},{16,0},{1,17},{17,1},{2,18},{18,2},{3,19},{19,3},{4,20},{20... | collective-permute-start | bytes 6291464 | tf_op jit(solution)/shard_map/ppermute | solution.py:29
  485.3 80.0 %collective-permute-start.21 = (bf16[2,2,128,2048]{3,2,0,1:T(8,128)(2,1)}, bf16[2,2,128,2048]{3,2,0,1:T(8,128)(2,1)}, u32[]{:S(2)}, u32[]{:S(2)}) collective-permute-start(bf16[2,2,128,2048]{3,2,0,1:T(8,128)(2,1)} %fusion.10), channel_id=1, source_target_pairs={{0,8},{8,0},{1,9},{9,1},{2,10},{10,2},{3,11},{11,3},{4,12},{12,4},... | collective-permute-start | bytes 6291464 | tf_op jit(solution)/shard_map/ppermute | solution.py:29
  508.6 16.5 %collective-permute-start.29 = (bf16[2,64,2048]{2,1,0:T(8,128)(2,1)}, bf16[2,64,2048]{2,1,0:T(8,128)(2,1)}, u32[]{:S(2)}, u32[]{:S(2)}) collective-permute-start(bf16[2,64,2048]{2,1,0:T(8,128)(2,1)} %fusion.34), channel_id=1, source_target_pairs={{0,1},{1,0},{2,3},{3,2},{4,5},{5,4},{6,7},{7,6},{8,9},{9,8},{10,11... | collective-permute-start | bytes 1572872 | tf_op jit(solution)/shard_map/ppermute | solution.py:29
  518.5 16.1 %collective-permute-start.28 = (bf16[64,2048]{0,1:T(8,128)(2,1)}, bf16[64,2048]{0,1:T(8,128)(2,1)}, u32[]{:S(2)}, u32[]{:S(2)}) collective-permute-start(bf16[64,2048]{0,1:T(8,128)(2,1)} %fusion.33), channel_id=1, source_target_pairs={{0,1},{1,0},{2,3},{3,2},{4,5},{5,4},{6,7},{7,6},{8,9},{9,8},{10,11... | collective-permute-start | bytes 786440 | tf_op jit(solution)/shard_map/ppermute | solution.py:29
  552.7 51.3 %collective-permute-start.43 = (bf16[2,512,1024]{2,1,0:T(8,128)(2,1)S(1)}, bf16[2,512,1024]{2,1,0:T(8,128)(2,1)S(1)}, u32[]{:S(2)}, u32[]{:S(2)}) collective-permute-start(bf16[2,512,1024]{2,1,0:T(8,128)(2,1)S(1)} %fusion.8), channel_id=1, source_target_pairs={{0,16},{16,0},{1,17},{17,1},{2,18},{18,2},{3,19},{19,3},{4,20},{20... | collective-permute-start | bytes 6291464 | tf_op jit(solution)/shard_map/ppermute | solution.py:29
  558.5 173.2 %collective-permute-start.46 = (bf16[256,2048]{1,0:T(8,128)(2,1)}, bf16[256,2048]{1,0:T(8,128)(2,1)}, u32[]{:S(2)}, u32[]{:S(2)}) collective-permute-start(bf16[256,2048]{1,0:T(8,128)(2,1)} %fusion.22), channel_id=1, source_target_pairs={{0,4},{4,0},{1,5},{5,1},{2,6},{6,2},{3,7},{7,3},{8,12},{12,8},{9,1... | collective-permute-start | bytes 3145736 | tf_op jit(solution)/shard_map/ppermute | solution.py:29
  563.9 83.5 %collective-permute-start.42 = (bf16[512,1024]{1,0:T(8,128)(2,1)S(1)}, bf16[512,1024]{1,0:T(8,128)(2,1)S(1)}, u32[]{:S(2)}, u32[]{:S(2)}) collective-permute-start(bf16[512,1024]{1,0:T(8,128)(2,1)S(1)} %fusion.20), channel_id=1, source_target_pairs={{0,4},{4,0},{1,5},{5,1},{2,6},{6,2},{3,7},{7,3},{8,12},{12,8},{9,1... | collective-permute-start | bytes 3145736 | tf_op jit(solution)/shard_map/ppermute | solution.py:29
  571.7 86.8 %collective-permute-start.22 = (bf16[2,64,2048]{2,1,0:T(8,128)(2,1)S(1)}, bf16[2,64,2048]{2,1,0:T(8,128)(2,1)S(1)}, u32[]{:S(2)}, u32[]{:S(2)}) collective-permute-start(bf16[2,64,2048]{2,1,0:T(8,128)(2,1)S(1)} %fusion.30), channel_id=1, source_target_pairs={{0,2},{2,0},{1,3},{3,1},{4,6},{6,4},{5,7},{7,5},{8,10},{10,8},{9,1... | collective-permute-start | bytes 1572872 | tf_op jit(solution)/shard_map/ppermute | solution.py:29
  648.7 56.4 %all-to-all-start.5 = ((bf16[8,64,1024]{2,1,0:T(8,128)(2,1)}), bf16[8,64,1024]{2,1,0:T(8,128)(2,1)}, u32[]{:S(2)}, u32[]{:S(2)}) async-start(bf16[8,64,1024]{2,1,0:T(8,128)(2,1)} %bitcast.134), calls=%async_computation.5 | async-start | bytes 2097152 | tf_op jit(solution)/shard_map/all_to_all | solution.py:100
  654.9 48.9 %collective-permute-start.44 = (bf16[512,1024]{1,0:T(8,128)(2,1)S(1)}, bf16[512,1024]{1,0:T(8,128)(2,1)S(1)}, u32[]{:S(2)}, u32[]{:S(2)}) collective-permute-start(bf16[512,1024]{1,0:T(8,128)(2,1)S(1)} %fusion.21), channel_id=1, source_target_pairs={{0,4},{4,0},{1,5},{5,1},{2,6},{6,2},{3,7},{7,3},{8,12},{12,8},{9,1... | collective-permute-start | bytes 3145736 | tf_op jit(solution)/shard_map/ppermute | solution.py:29
  656.4 22.6 %collective-permute-start.24 = (bf16[2,64,2048]{2,1,0:T(8,128)(2,1)S(1)}, bf16[2,64,2048]{2,1,0:T(8,128)(2,1)S(1)}, u32[]{:S(2)}, u32[]{:S(2)}) collective-permute-start(bf16[2,64,2048]{2,1,0:T(8,128)(2,1)S(1)} %fusion.31), channel_id=1, source_target_pairs={{0,1},{1,0},{2,3},{3,2},{4,5},{5,4},{6,7},{7,6},{8,9},{9,8},{10,11... | collective-permute-start | bytes 1572872 | tf_op jit(solution)/shard_map/ppermute | solution.py:29
  660.7 54.6 %collective-permute-start.23 = (bf16[64,2048]{1,0:T(8,128)(2,1)}, bf16[64,2048]{1,0:T(8,128)(2,1)S(1)}, u32[]{:S(2)}, u32[]{:S(2)}) collective-permute-start(bf16[64,2048]{1,0:T(8,128)(2,1)} %fusion.48), channel_id=1, source_target_pairs={{0,1},{1,0},{2,3},{3,2},{4,5},{5,4},{6,7},{7,6},{8,9},{9,8},{10,11... | collective-permute-start | bytes 786440 | tf_op jit(solution)/shard_map/ppermute | solution.py:29
  705.1 46.0 %all-to-all-start.6 = ((bf16[8,64,1024]{2,1,0:T(8,128)(2,1)}), bf16[8,64,1024]{2,1,0:T(8,128)(2,1)}, u32[]{:S(2)}, u32[]{:S(2)}) async-start(bf16[8,64,1024]{2,1,0:T(8,128)(2,1)} %bitcast.420), calls=%async_computation.6 | async-start | bytes 2097152 | tf_op jit(solution)/shard_map/all_to_all | solution.py:100
  711.4 18.3 %collective-permute-start.25 = (bf16[64,2048]{1,0:T(8,128)(2,1)}, bf16[64,2048]{1,0:T(8,128)(2,1)}, u32[]{:S(2)}, u32[]{:S(2)}) collective-permute-start(bf16[64,2048]{1,0:T(8,128)(2,1)} %fusion.49), channel_id=1, source_target_pairs={{0,2},{2,0},{1,3},{3,1},{4,6},{6,4},{5,7},{7,5},{8,10},{10,8},{9,1... | collective-permute-start | bytes 786440 | tf_op jit(solution)/shard_map/ppermute | solution.py:29
  772.8 31.0 %all-to-all-start.7 = ((f32[4,1,192]{2,1,0:T(1,128)}), f32[4,1,192]{2,1,0:T(1,128)S(1)}, u32[]{:S(2)}, u32[]{:S(2)}) async-start(f32[4,1,192]{2,1,0:T(1,128)} %reshape.594), calls=%async_computation.7 | async-start | bytes 8192 | tf_op jit(solution)/shard_map/all_to_all | solution.py:302
  795.4 28.0 %collective-permute-start.32 = (bf16[2,2,128,2048]{3,2,1,0:T(8,128)(2,1)}, bf16[2,2,128,2048]{3,2,1,0:T(8,128)(2,1)}, u32[]{:S(2)}, u32[]{:S(2)}) collective-permute-start(bf16[2,2,128,2048]{3,2,1,0:T(8,128)(2,1)} %fusion.6), channel_id=1, source_target_pairs={{0,8},{8,0},{1,9},{9,1},{2,10},{10,2},{3,11},{11,3},{4,12},{12,4},... | collective-permute-start | bytes 6291464 | tf_op jit(solution)/shard_map/ppermute | solution.py:29
  801.6 17.1 %collective-permute-start.39 = (bf16[2,64,2048]{2,1,0:T(8,128)(2,1)S(1)}, bf16[2,64,2048]{2,1,0:T(8,128)(2,1)S(1)}, u32[]{:S(2)}, u32[]{:S(2)}) collective-permute-start(bf16[2,64,2048]{2,1,0:T(8,128)(2,1)S(1)} %fusion.41), channel_id=1, source_target_pairs={{0,16},{16,0},{1,17},{17,1},{2,18},{18,2},{3,19},{19,3},{4,20},{20... | collective-permute-start | bytes 1572872 | tf_op jit(solution)/shard_map/ppermute | solution.py:29
  818.6 35.4 %collective-permute-start.37 = (bf16[2,512,768]{2,1,0:T(8,128)(2,1)S(1)}, bf16[2,512,768]{2,1,0:T(8,128)(2,1)S(1)}, u32[]{:S(2)}, u32[]{:S(2)}) collective-permute-start(bf16[2,512,768]{2,1,0:T(8,128)(2,1)S(1)} %fusion.16), channel_id=1, source_target_pairs={{0,16},{16,0},{1,17},{17,1},{2,18},{18,2},{3,19},{19,3},{4,20},{20... | collective-permute-start | bytes 4718600 | tf_op jit(solution)/shard_map/ppermute | solution.py:29
  821.0 100.1 %collective-permute-start.40 = (bf16[64,2048]{1,0:T(8,128)(2,1)}, bf16[64,2048]{1,0:T(8,128)(2,1)S(1)}, u32[]{:S(2)}, u32[]{:S(2)}) collective-permute-start(bf16[64,2048]{1,0:T(8,128)(2,1)} %fusion.52), channel_id=1, source_target_pairs={{0,4},{4,0},{1,5},{5,1},{2,6},{6,2},{3,7},{7,3},{8,12},{12,8},{9,1... | collective-permute-start | bytes 786440 | tf_op jit(solution)/shard_map/ppermute | solution.py:29
  826.3 32.5 %collective-permute-start.33 = (bf16[2,64,2048]{2,1,0:T(8,128)(2,1)S(1)}, bf16[2,64,2048]{2,1,0:T(8,128)(2,1)S(1)}, u32[]{:S(2)}, u32[]{:S(2)}) collective-permute-start(bf16[2,64,2048]{2,1,0:T(8,128)(2,1)S(1)} %fusion.39), channel_id=1, source_target_pairs={{0,2},{2,0},{1,3},{3,1},{4,6},{6,4},{5,7},{7,5},{8,10},{10,8},{9,1... | collective-permute-start | bytes 1572872 | tf_op jit(solution)/shard_map/ppermute | solution.py:29
  855.4 48.0 %collective-permute-start.38 = (bf16[512,768]{1,0:T(8,128)(2,1)}, bf16[512,768]{1,0:T(8,128)(2,1)}, u32[]{:S(2)}, u32[]{:S(2)}) collective-permute-start(bf16[512,768]{1,0:T(8,128)(2,1)} %fusion.27), channel_id=1, source_target_pairs={{0,4},{4,0},{1,5},{5,1},{2,6},{6,2},{3,7},{7,3},{8,12},{12,8},{9,1... | collective-permute-start | bytes 2359304 | tf_op jit(solution)/shard_map/ppermute | solution.py:29
  871.5 21.3 %collective-permute-start.36 = (bf16[64,2048]{1,0:T(8,128)(2,1)S(1)}, bf16[64,2048]{1,0:T(8,128)(2,1)S(1)}, u32[]{:S(2)}, u32[]{:S(2)}) collective-permute-start(bf16[64,2048]{1,0:T(8,128)(2,1)S(1)} %fusion.51), channel_id=1, source_target_pairs={{0,2},{2,0},{1,3},{3,1},{4,6},{6,4},{5,7},{7,5},{8,10},{10,8},{9,1... | collective-permute-start | bytes 786440 | tf_op jit(solution)/shard_map/ppermute | solution.py:29
  910.4 19.2 %all-to-all-start.4 = ((bf16[8,64,768]{2,1,0:T(8,128)(2,1)}), bf16[8,64,768]{2,1,0:T(8,128)(2,1)}, u32[]{:S(2)}, u32[]{:S(2)}) async-start(bf16[8,64,768]{2,1,0:T(8,128)(2,1)} %bitcast.435), calls=%async_computation.4 | async-start | bytes 1572864 | tf_op jit(solution)/shard_map/all_to_all | solution.py:100
  (110 other events, 2072.0 us)
Sparse Core Ops, SparseCore 0:
  30.2 30.5 all-gather.4
  152.6 42.6 all-gather.8
  221.3 62.8 all-gather.6
  550.1 55.0 all-gather.10

commit v2 on v1

v2 whole, which is shorter than its diff:
```python
import functools

import jax
import jax.numpy as jnp
import numpy as np
from jax import lax
from jax.experimental import pallas as pl
from jax.experimental.pallas import tpu as pltpu
from jax.sharding import Mesh
from jax.sharding import PartitionSpec as P

D = 2048
FF = 8192
TAPS = 3
STEP = 4


EPS_NORM = 1e-05
BETA_ONE = 0.9
BETA_TWO = 0.999
EPS_ADAM = 1e-08
DECAY = 0.01
RATE = 0.3

AXES = ("y", "c", "h", "l")
FEED = ("h", "c")
FEED_COPIES = ("y", "l")
CONV = ("y", "c", "l")
LINES = ("l", "y")
LOW = jnp.bfloat16
WIDE = jnp.float32
ROOM = 56 * 1024 * 1024
SHORT = pl.CostEstimate(flops=1024, bytes_accessed=1024, transcendentals=0)


def turned(value, axes, steps):
    n = lax.axis_size(axes)
    names = (axes,) if isinstance(axes, str) else axes
    ordered = tuple(a for a in AXES if a in names)
    where = np.arange(n).reshape([lax.axis_size(a) for a in ordered])
    where = where.transpose([ordered.index(a) for a in names]).reshape(-1)
    pairs = [(int(where[i]), int(where[(i + steps) % n])) for i in range(n)]
    return lax.ppermute(value, ordered if len(names) > 1 else axes, pairs)


def tied(*values):
    return lax.optimization_barrier(values)


def picked(value, index, dim):
    return lax.dynamic_index_in_dim(value, index, dim, keepdims=False)


def exchanged(value, axes):
    return lax.all_to_all(value, axes, 0, 0, tiled=True)


def spread_to(value, axes):
    return exchanged(jnp.broadcast_to(value[None], (lax.axis_size(axes),) + value.shape), axes)


def rolled(value, axis, dim, sign):
    n, me = lax.axis_size(axis), lax.axis_index(axis)
    twice = jnp.concatenate([value, value], dim)
    return lax.dynamic_slice_in_dim(twice, (sign * me) % n, n, dim)


def placed(pieces, axis):
    n, me = len(pieces), lax.axis_index(axis)
    out = jnp.zeros((n,) + pieces[0].shape, pieces[0].dtype)
    for k, piece in enumerate(pieces):
        out = lax.dynamic_update_slice(
            out, piece[None], ((me + k) % n,) + (0,) * piece.ndim
        )
    return out


def norm_forward(values, gain):
    scale = lax.rsqrt(jnp.mean(values * values, axis=-1, keepdims=True) + EPS_NORM)
    return (values * scale * gain, scale)


def norm_backward(values, scale, gain, grad):
    along = grad * gain
    inner = jnp.mean(along * values, axis=-1, keepdims=True)
    d_values = scale * along - scale * scale * scale * values * inner
    d_gain = jnp.sum(grad * values * scale, axis=0)
    return (d_values, d_gain)


def times(left, right):
    return jnp.dot(left, right, preferred_element_type=WIDE)


def times_wide(left, right):
    return lax.dot_general(
        left, right, (((1,), (1,)), ((), ())), preferred_element_type=WIDE
    )


def over_tokens(left, right):
    return lax.dot_general(
        left, right, (((0,), (0,)), ((), ())), preferred_element_type=WIDE
    )


def adam_direction(weight, grad, first, second):
    new_first = BETA_ONE * first + (1.0 - BETA_ONE) * grad
    new_second = BETA_TWO * second + (1.0 - BETA_TWO) * grad * grad
    first_hat = new_first / (1.0 - BETA_ONE**STEP)
    second_hat = new_second / (1.0 - BETA_TWO**STEP)
    direction = first_hat / (jnp.sqrt(second_hat) + EPS_ADAM) + DECAY * weight
    return (new_first, new_second, direction)


def feed_kernel(h_ref, e_ref, g_ref, u_ref, d_ref, hid_ref, dg_ref, du_ref):
    step = 256
    for j in range(h_ref.shape[0] // step):
        at = slice(j * step, (j + 1) * step)
        gate = times(h_ref[at, :], g_ref[...])
        up = times(h_ref[at, :], u_ref[...])
        d_hidden = times_wide(e_ref[at, :], d_ref[...])
        sig = jax.nn.sigmoid(gate)
        activated = gate * sig
        hid_ref[at, :] = (activated * up).astype(LOW)
        dg_ref[at, :] = (d_hidden * up * (sig * (1.0 + gate * (1.0 - sig)))).astype(LOW)
        du_ref[at, :] = (d_hidden * activated).astype(LOW)


def feed(h, e, gate, up, down):
    count, features = h.shape[0], down.shape[0]
    tile = 256
    whole = pl.BlockSpec((count, D), lambda i: (0, 0), pipeline_mode=pl.Buffered(1))
    made = pl.BlockSpec((count, tile), lambda i: (0, i))
    return pl.pallas_call(
        feed_kernel,
        grid=(features // tile,),
        in_specs=[
            whole,
            whole,
            pl.BlockSpec((D, tile), lambda i: (0, i)),
            pl.BlockSpec((D, tile), lambda i: (0, i)),
            pl.BlockSpec((tile, D), lambda i: (i, 0)),
        ],
        out_specs=[made] * 3,
        out_shape=[jax.ShapeDtypeStruct((count, features), LOW)] * 3,
        compiler_params=pltpu.CompilerParams(vmem_limit_bytes=ROOM),
        cost_estimate=SHORT,
    )(h, e, gate, up, down)


def back_kernel(pairs, *refs):
    out_ref = refs[-1]
    total = None
    for left, right in zip(refs[:pairs], refs[pairs:-1]):
        part = times_wide(left[...], right[...])
        total = part if total is None else total + part
    out_ref[...] = total.astype(out_ref.dtype)


def back(lefts, right, dtype):
    count, width = lefts[0].shape
    tile = 512
    return pl.pallas_call(
        functools.partial(back_kernel, len(lefts)),
        grid=(D // tile,),
        in_specs=[
            pl.BlockSpec(a.shape, lambda i: (0, 0), pipeline_mode=pl.Buffered(1)) for a in lefts
        ]
        + [pl.BlockSpec((tile, width), lambda i, k=k: (i, k)) for k in range(len(lefts))],
        out_specs=pl.BlockSpec((count, tile), lambda i: (0, i)),
        out_shape=jax.ShapeDtypeStruct((count, D), dtype),
        compiler_params=pltpu.CompilerParams(vmem_limit_bytes=ROOM),
        cost_estimate=SHORT,
    )(*lefts, *[right] * len(lefts))


def both_kernel(count, wide, c_ref, *refs):
    out_ref = refs[-1]
    mine, other, rights = refs[:count], refs[count : 2 * count], refs[2 * count : -1]
    product = times_wide if wide else times

    def write(lefts):
        total = None
        for left, right in zip(lefts, rights):
            part = product(left[...], right[...])
            total = part if total is None else total + part
        out_ref[...] = total.astype(out_ref.dtype).reshape(out_ref.shape)

    @pl.when(pl.program_id(0) == 0)
    def _():
        write(mine)

    @pl.when(pl.program_id(0) == 1)
    def _():
        write(other)


def both_cores(core, mine, other, rights, own, wide):
    count, width = mine[0].shape
    tile = 512
    if wide:
        blocks = [pl.BlockSpec((tile, width), lambda g, i, c: (i, 0)) for _ in rights]
    else:
        blocks = [pl.BlockSpec((width, tile), lambda g, i, c: (0, i)) for _ in rights]
    return pl.pallas_call(
        functools.partial(both_kernel, len(mine), wide),
        grid_spec=pltpu.PrefetchScalarGridSpec(
            num_scalar_prefetch=1,
            grid=(2, D // tile),
            in_specs=[
                pl.BlockSpec(a.shape, lambda g, i, c: (0, 0), pipeline_mode=pl.Buffered(1))
                for a in mine + other
            ]
            + blocks,
            out_specs=pl.BlockSpec(
                (count // own, 1, own, tile), lambda g, i, c: (0, (c[0] + g) % 2, 0, i)
            ),
        ),
        out_shape=jax.ShapeDtypeStruct((count // own, 2, own, D), LOW),
        compiler_params=pltpu.CompilerParams(vmem_limit_bytes=ROOM),
        cost_estimate=SHORT,
    )(core, *mine, *other, *rights)


def weight_kernel(parts, outs, *refs):
    lefts, rights, out_ref = refs[:parts], refs[parts:-1], refs[-1]
    width = out_ref.shape[1] // outs
    for j in range(outs):
        total = None
        for i, left in enumerate(lefts):
            part = over_tokens(left[...], rights[i * outs + j][...])
            total = part if total is None else total + part
        out_ref[:, j * width : (j + 1) * width] = total.astype(out_ref.dtype)


def weight_grads(lefts, rights):
    parts, outs = len(lefts), len(rights[0])
    flat = [r for row in rights for r in row]
    rows, tile = lefts[0].shape[1], 512
    width = sum(r.shape[1] for r in rights[0])
    return pl.pallas_call(
        functools.partial(weight_kernel, parts, outs),
        grid=(rows // tile,),
        in_specs=[pl.BlockSpec((a.shape[0], tile), lambda i: (0, i)) for a in lefts]
        + [pl.BlockSpec(r.shape, lambda i: (0, 0), pipeline_mode=pl.Buffered(1)) for r in flat],
        out_specs=pl.BlockSpec((tile, width), lambda i: (i, 0)),
        out_shape=jax.ShapeDtypeStruct((rows, width), LOW),
        compiler_params=pltpu.CompilerParams(vmem_limit_bytes=ROOM),
        cost_estimate=SHORT,
    )(*lefts, *flat)


def prep_feed_kernel(nc, nh, w_ref, out_ref):
    width = out_ref.shape[2]
    for c in range(nc):
        for h in range(nh):
            at = (c * nh + h) * width
            out_ref[h * nc + c] = w_ref[:, at : at + width].astype(LOW)


def prep_feed(sizes, w, first):
    ny, nc, nh, _ = sizes
    rows, block = w.shape[0], FF // ny
    return pl.pallas_call(
        functools.partial(prep_feed_kernel, nc, nh),
        grid=(ny,),
        in_specs=[pl.BlockSpec((rows, block), lambda i: (0, first // block + i))],
        out_specs=pl.BlockSpec((nh * nc, rows, block // (nh * nc)), lambda i: (0, 0, i)),
        out_shape=jax.ShapeDtypeStruct((nh * nc, rows, FF // (nh * nc)), LOW),
        compiler_params=pltpu.CompilerParams(vmem_limit_bytes=ROOM),
        cost_estimate=SHORT,
    )(w)


def prep_conv_kernel(sizes, w_ref, out_ref):
    ny, nc, nh, nl = sizes
    rows = w_ref.shape[0]
    for yc in range(ny * nc):
        for k in range(nl):
            parts = [
                w_ref[:, ((yc * nh + h) * nl + k) * rows : ((yc * nh + h) * nl + k + 1) * rows]
                for h in range(nh)
            ]
            out_ref[yc * nl + k, 0] = jnp.concatenate(parts, 1).astype(LOW)


def prep_conv(sizes, w):
    ny, nc, nh, nl = sizes
    rows = w.shape[0]
    shape = (ny * nc * nl, 3, rows, nh * rows)
    return pl.pallas_call(
        functools.partial(prep_conv_kernel, sizes),
        grid=(3,),
        in_specs=[pl.BlockSpec((rows, D), lambda i: (0, i))],
        out_specs=pl.BlockSpec((shape[0], 1) + shape[2:], lambda i: (0, i, 0, 0)),
        out_shape=jax.ShapeDtypeStruct(shape, LOW),
        compiler_params=pltpu.CompilerParams(vmem_limit_bytes=ROOM),
        cost_estimate=SHORT,
    )(w)


def fold(values):
    rows, cols = values.shape
    total = values[:, :128]
    for k in range(1, cols // 128):
        total = total + values[:, 128 * k : 128 * (k + 1)]
    out = total[:8]
    for k in range(1, rows // 8):
        out = out + total[8 * k : 8 * (k + 1)]
    return out


def adam_step(first, grad, w_ref, m_ref, v_ref, grad_ref, nm_ref, nv_ref, dir_ref, sum_ref):
    weight = w_ref[...]
    new_m, new_v, direction = adam_direction(weight, grad, m_ref[...], v_ref[...])
    grad_ref[...] = grad
    nm_ref[...] = new_m
    nv_ref[...] = new_v
    dir_ref[...] = direction

    @pl.when(first)
    def _():
        sum_ref[...] = jnp.zeros_like(sum_ref)

    sum_ref[0, 0] += fold(weight * weight)
    sum_ref[0, 1] += fold(direction * direction)


def adam_gate_kernel(w_ref, m_ref, v_ref, got_ref, *refs):
    grad = jnp.concatenate([got_ref[h, 0] for h in range(got_ref.shape[0])], 1).astype(WIDE)
    adam_step(pl.program_id(0) == 0, grad, w_ref, m_ref, v_ref, *refs[-5:])


def adam_gate(sizes, w, m, v, got, kind, done=()):
    ny, nc, nh, _ = sizes
    rows = w.shape[0]
    part = got.shape[2] // (2 * ny)
    width = nh * part
    first = 4 * D + kind * FF
    column = pl.BlockSpec((rows, width), lambda b: (0, first // width + b))
    like = jax.ShapeDtypeStruct(w.shape, WIDE)
    return pl.pallas_call(
        adam_gate_kernel,
        grid=(ny * nc,),
        in_specs=[column] * 3
        + [pl.BlockSpec((nh, 1, rows, part), lambda b: (0, b % nc, 0, kind * ny + b // nc))]
        + [pl.BlockSpec(memory_space=pl.ANY) for _ in done],
        out_specs=[column] * 4 + [pl.BlockSpec((1, 2, 8, 128), lambda b: (0, 0, 0, 0))],
        out_shape=[like] * 4 + [jax.ShapeDtypeStruct((1, 2, 8, 128), WIDE)],
        input_output_aliases={4 + k: k for k in range(len(done))},
        compiler_params=pltpu.CompilerParams(vmem_limit_bytes=ROOM),
        cost_estimate=SHORT,
    )(w, m, v, got.reshape(nh, nc, rows, -1), *done)


def adam_plain_kernel(w_ref, m_ref, v_ref, g_ref, *refs):
    adam_step(pl.program_id(1) == 0, g_ref[...], w_ref, m_ref, v_ref, *refs[-5:])


def adam_columns(w, m, v, grad, first, kinds, done=()):
    rows = w.shape[0]
    width = 1024
    blocks = grad.shape[1] // (kinds * width)
    column = pl.BlockSpec((rows, width), lambda k, b: (0, first // width + k * blocks + b))
    like = jax.ShapeDtypeStruct(w.shape, WIDE)
    return pl.pallas_call(
        adam_plain_kernel,
        grid=(kinds, blocks),
        in_specs=[column] * 3
        + [pl.BlockSpec((rows, width), lambda k, b: (0, k * blocks + b))]
        + [pl.BlockSpec(memory_space=pl.ANY) for _ in done],
        out_specs=[column] * 4 + [pl.BlockSpec((1, 2, 8, 128), lambda k, b: (k, 0, 0, 0))],
        out_shape=[like] * 4 + [jax.ShapeDtypeStruct((kinds, 2, 8, 128), WIDE)],
        input_output_aliases={4 + k: k for k in range(len(done))},
        compiler_params=pltpu.CompilerParams(vmem_limit_bytes=ROOM),
        cost_estimate=SHORT,
    )(w, m, v, grad, *done)


def adam_down(w, m, v, grad):
    rows = 64
    block = pl.BlockSpec((rows, D), lambda k, i: (i, 0))
    like = jax.ShapeDtypeStruct(w.shape, WIDE)
    return pl.pallas_call(
        adam_plain_kernel,
        grid=(1, w.shape[0] // rows),
        in_specs=[block] * 4,
        out_specs=[block] * 4 + [pl.BlockSpec((1, 2, 8, 128), lambda k, i: (0, 0, 0, 0))],
        out_shape=[like] * 4 + [jax.ShapeDtypeStruct((1, 2, 8, 128), WIDE)],
        compiler_params=pltpu.CompilerParams(vmem_limit_bytes=ROOM),
        cost_estimate=SHORT,
    )(w, m, v, grad)


def adam_first_kernel(sizes, w_ref, m_ref, v_ref, got_ref, *refs):
    ny, nc, nh, nl = sizes
    rows = w_ref.shape[0]
    parts = []
    for yc in range(ny * nc):
        for h in range(nh):
            for k in range(nl):
                parts.append(got_ref[yc * nl + k, 0, :, h * rows : (h + 1) * rows])
    grad = jnp.concatenate(parts, 1).astype(WIDE)
    adam_step(pl.program_id(0) == 0, grad, w_ref, m_ref, v_ref, *refs[-5:])


def adam_first(sizes, w, m, v, got):
    rows = w.shape[0]
    column = pl.BlockSpec((rows, D), lambda i: (0, i))
    like = jax.ShapeDtypeStruct(w.shape, WIDE)
    return pl.pallas_call(
        functools.partial(adam_first_kernel, sizes),
        grid=(3,),
        in_specs=[column] * 3
        + [pl.BlockSpec((got.shape[0], 1) + got.shape[2:], lambda i: (0, i, 0, 0))],
        out_specs=[column] * 4 + [pl.BlockSpec((1, 2, 8, 128), lambda i: (0, 0, 0, 0))],
        out_shape=[like] * 4 + [jax.ShapeDtypeStruct((1, 2, 8, 128), WIDE)],
        compiler_params=pltpu.CompilerParams(vmem_limit_bytes=ROOM),
        cost_estimate=SHORT,
    )(w, m, v, got)


def step_kernel(ratio_ref, w_ref, dir_ref, *refs):
    refs[-1][...] = w_ref[...] + dir_ref[...] * ratio_ref[pl.program_id(0)]


def stepped(ratio, w, direction, first, kinds, blocks, width, done=None):
    rows = w.shape[0]
    column = pl.BlockSpec((rows, width), lambda k, b, r: (0, first + k * blocks + b))
    more = () if done is None else (done,)
    return pl.pallas_call(
        step_kernel,
        grid_spec=pltpu.PrefetchScalarGridSpec(
            num_scalar_prefetch=1,
            grid=(kinds, blocks),
            in_specs=[column] * 2 + [pl.BlockSpec(memory_space=pl.ANY) for _ in more],
            out_specs=column,
        ),
        out_shape=jax.ShapeDtypeStruct(w.shape, WIDE),
        input_output_aliases={3: 0} if more else {},
        compiler_params=pltpu.CompilerParams(vmem_limit_bytes=ROOM),
        cost_estimate=SHORT,
    )(ratio, w, direction, *more)


def local(
    inputs,
    out_grad,
    segments,
    w_in,
    w_down,
    conv_taps,
    norm_gains,
    m_in,
    m_down,
    m_taps,
    m_gains,
    v_in,
    v_down,
    v_taps,
    v_gains,
):
    sizes = tuple(lax.axis_size(a) for a in AXES)
    ny, nc, nh, nl = sizes
    yi, ci, hi, li = (lax.axis_index(a) for a in AXES)
    own = inputs.shape[0] * inputs.shape[1]
    rows = w_in.shape[0]
    wide_rows = w_down.shape[0]
    channels = nh * rows
    span = ny * nc * own
    conv_total = nl * span

    def feed_order(a):
        return a.reshape(own, ny, nc, nh, nl, rows).transpose(0, 1, 4, 3, 2, 5).reshape(own, D)

    def from_feed_order(a):
        return a.reshape(own, ny, nl, nh, nc, rows).transpose(0, 1, 4, 3, 2, 5).reshape(own, D)

    def conv_order(a):
        return rolled(a.reshape(own, ny * nc, nh, -1).swapaxes(1, 2), "h", 1, 1).reshape(own, D)

    def from_conv_order(a):
        return rolled(a.reshape(own, nh, ny * nc, -1), "h", 1, -1).swapaxes(1, 2).reshape(own, D)

    def near(value, axes, first=1, last=None):
        last = lax.axis_size(axes) if last is None else last
        return [turned(value, axes, -k) for k in range(first, last)]

    def ring(value, axis):
        pieces = [value]
        for _ in range(1, lax.axis_size(axis)):
            pieces.append(turned(pieces[-1], axis, -1))
        return pieces

    def ring_sum(blocks, axis):
        n = lax.axis_size(axis)
        passed = blocks[n - 1]
        for k in range(n - 2, -1, -1):
            passed = turned(passed.astype(LOW), axis, 1).astype(WIDE) + blocks[k].astype(WIDE)
        return passed

    def with_core(pieces):
        mine = jnp.concatenate(pieces, 0)
        return mine, turned(mine, "c", 1)

    def scatter(other, mine, axes):
        both = turned(other, "c", 1)
        both = (mine() + both.astype(WIDE)).reshape(-1, own, D)
        sent = [turned(both[k].astype(LOW), axes, k) for k in range(1, both.shape[0])]
        return both[0], sent

    def total(first, sent):
        for s in sent:
            first = first + s.astype(WIDE)
        return first

    def out_order(a):
        return rolled(a, "h", 0, -1)

    note = jnp.concatenate(
        [norm_gains.reshape(-1), conv_taps.reshape(-1), segments.reshape(-1).astype(WIDE)]
    )
    low_o = w_in[:, 3 * D : 4 * D].astype(LOW)
    notes, p_cols = tied(spread_to(note, AXES), prep_conv(sizes, w_in))
    o_pieces = [low_o] + near(low_o, "h")
    notes = notes.reshape(sizes + (-1,))
    gains = notes[..., : 2 * rows].reshape(D, 2).astype(LOW).astype(WIDE)
    gain_one = gains[:, 0]
    gain_two = gains[:, 1]
    of_group = picked(picked(picked(notes, li, 3), ci, 1), yi, 0)
    taps = of_group[:, 2 * rows : 5 * rows].reshape(channels, TAPS).astype(LOW).astype(WIDE)
    ids = picked(notes[..., 5 * rows :], hi, 2).transpose(2, 0, 1, 3).reshape(nl, span)

    def as_rows(a):
        return a.reshape(-1, a.shape[-1])

    grad_low = out_grad.reshape(own, D)
    grad_top = grad_low.astype(WIDE)
    e_all = lax.all_gather(grad_low, FEED, axis=0)
    down = lax.all_gather(w_down.astype(LOW), FEED_COPIES, axis=0, tiled=True)
    values = inputs.reshape(own, D).astype(WIDE)
    norm_one, scale_one = norm_forward(values, gain_one)
    low_one = conv_order(norm_one.astype(LOW))
    mine, other = with_core([low_one] + near(low_one, LINES))
    cols_p, gate_cols, *o_pieces = tied(
        exchanged(p_cols, CONV), prep_feed(sizes, w_in, 4 * D), *o_pieces
    )
    gate_cols, cols_p, mine, other = tied(exchanged(gate_cols, FEED), cols_p, mine, other)
    gate_w = lax.all_gather(as_rows(gate_cols), FEED_COPIES, axis=0, tiled=True)
    o_w = placed(o_pieces, "h").reshape(channels, D)
    pieces = ring(cols_p.swapaxes(1, 2).reshape(-1, 3 * channels), "h")
    pieces[-1], up_cols = tied(pieces[-1], prep_feed(sizes, w_in, 4 * D + FF))
    up_cols = exchanged(up_cols, FEED)
    p_w = jnp.concatenate(pieces, 0)

    h_one = jnp.zeros((ny * nl, nc, own, D), LOW)
    for k, part in enumerate((mine, other)):
        part = rolled(part.reshape(-1, 1, own, D), LINES, 0, -1)
        h_one = lax.dynamic_update_slice(h_one, part, (0, (ci + k) % nc, 0, 0))
    h_one = h_one.reshape(conv_total, D)
    bcx = times(h_one, p_w).reshape(nl, span, 3 * channels)
    b_part = bcx[:, :, :channels]
    c_part = bcx[:, :, channels : 2 * channels]
    x_part = bcx[:, :, 2 * channels :]
    mixed_in = b_part * x_part
    extended = jnp.pad(mixed_in, ((0, 0), (2, 0), (0, 0)))
    ext_ids = jnp.pad(ids, ((0, 0), (2, 0)), constant_values=-1.0)
    keeps = []
    conv = jnp.zeros((nl, span, channels), WIDE)
    for lag in range(TAPS):
        keep = (ext_ids[:, 2 - lag : 2 - lag + span] == ids).astype(WIDE)[:, :, None]
        keeps.append(keep)
        conv = conv + taps[:, lag] * extended[:, 2 - lag : 2 - lag + span] * keep
    y_mix = (c_part * conv).astype(LOW)

    def by_core(value):
        parts = rolled(value.reshape(ny * nl, nc, own, -1), LINES, 0, 1)
        return [picked(parts, (ci + k) % nc, 1).reshape(ny * nl * own, -1) for k in range(nc)]

    y_mine, y_other = by_core(y_mix)
    both, sent = scatter(times(y_other, o_w).astype(LOW), lambda: times(y_mine, o_w), LINES)
    both, up_cols = tied(both, up_cols)
    up_w = lax.all_gather(as_rows(up_cols), FEED_COPIES, axis=0, tiled=True)
    *sent, e_all = tied(*sent, e_all)
    middle = values + total(both, sent)
    e_all = e_all.reshape(nh, nc, own, D)
    e_mine, e_other = (picked(e_all, (ci + k) % nc, 1).reshape(-1, D) for k in range(nc))

    norm_two, scale_two = norm_forward(middle, gain_two)
    low_two = feed_order(norm_two.astype(LOW))
    h_mine = placed([low_two] + near(low_two, "h"), "h").reshape(-1, D)
    h_other = turned(h_mine, "c", 1)
    hid_mine, dg_mine, du_mine = feed(h_mine, e_mine, gate_w, up_w, down)
    hid_other, dg_other, du_other = feed(h_other, e_other, gate_w, up_w, down)
    core = ci.reshape(1).astype(jnp.int32)

    def summed(part, axes):
        return lax.psum_scatter(part, axes, scatter_dimension=0, tiled=True)

    d_h_two = both_cores(core, [dg_mine, du_mine], [dg_other, du_other], [gate_w, up_w], own, True)
    d_h_two, h_mine = tied(d_h_two, h_mine)
    d_h_two = summed(d_h_two.reshape(-1, D), FEED).astype(WIDE)
    part_feed = weight_grads([h_mine, h_other], [[dg_mine, du_mine], [dg_other, du_other]])
    part_feed, hid_mine = tied(part_feed, hid_mine)
    part_down = weight_grads([hid_mine, hid_other], [[e_mine], [e_other]])
    out_part = both_cores(core, [hid_mine], [hid_other], [down], own, False)
    d_h_two, part_down, part_feed, out_part = tied(d_h_two, part_down, part_feed, out_part)
    out_sum = summed(out_part.reshape(-1, D), FEED)
    d_middle, d_gain_two = norm_backward(middle, scale_two, gain_two, from_feed_order(d_h_two))
    d_middle = d_middle + grad_top

    low_branch = d_middle.astype(LOW)
    do_mine, do_other = with_core([low_branch] + near(low_branch, LINES))
    do_mine, do_other, part_feed = tied(do_mine, do_other, part_feed)
    got_feed = summed(part_feed, FEED_COPIES)
    part_o = over_tokens(y_mine, do_mine) + over_tokens(y_other, do_other)
    part_o = rolled(part_o.reshape(nh, rows, D), "h", 0, 1)
    sent_o = [turned(part_o[k].astype(LOW), "h", k) for k in range(1, nh)]
    d_mix = jnp.zeros((ny * nl, nc, own, channels), WIDE)
    for k, part in enumerate((do_mine, do_other)):
        part = rolled(times_wide(part, o_w).reshape(-1, 1, own, channels), LINES, 0, -1)
        d_mix = lax.dynamic_update_slice(d_mix, part, (0, (ci + k) % nc, 0, 0))
    d_mix = d_mix.reshape(nl, span, channels)
    d_c = d_mix * conv
    d_conv = d_mix * c_part
    d_extended = jnp.zeros((nl, span + 2, channels), WIDE)
    tap_grads = []
    for lag in range(TAPS):
        counted = d_conv * keeps[lag]
        tap_grads.append(jnp.sum(counted * extended[:, 2 - lag : 2 - lag + span], axis=(0, 1)))
        d_extended = d_extended + jnp.pad(taps[:, lag] * counted, ((0, 0), (2 - lag, lag), (0, 0)))
    d_mixed_in = d_extended[:, 2:]
    d_bcx = jnp.concatenate([d_mixed_in * x_part, d_c, d_mixed_in * b_part], 2).astype(LOW)

    part_p = weight_grads([h_one], [[d_bcx.reshape(conv_total, -1)]]).reshape(nh, -1, 3 * channels)
    part_p, d_bcx, part_down, out_sum, *sent_o = tied(part_p, d_bcx, part_down, out_sum, *sent_o)
    grad_o = total(part_o[0], sent_o)
    grad_down = summed(part_down, FEED_COPIES)
    part_p = ring_sum(list(part_p), "h").astype(LOW)
    db_mine, db_other = by_core(d_bcx)
    other = back([db_other], p_w, LOW)
    other, db_mine = tied(other, db_mine)
    both, sent = scatter(other, lambda: back([db_mine], p_w, WIDE), LINES)
    got_feed, part_p = tied(got_feed, part_p)
    got_feed, part_p, both = tied(exchanged(got_feed.reshape(nh * nc, rows, -1), FEED), part_p, both)
    got_p = exchanged(part_p.reshape(ny * nc * nl, rows, 3, channels).swapaxes(1, 2), CONV)
    d_h_one = total(both, sent)
    d_values, d_gain_one = norm_backward(values, scale_one, gain_one, from_conv_order(d_h_one))
    input_grad = (d_values + d_middle).reshape(inputs.shape)

    tap_terms = jnp.stack(tap_grads, 1).reshape(1, 1, nh, 1, rows, TAPS)
    tap_terms = lax.dynamic_update_slice(
        jnp.zeros(sizes + (rows, TAPS), WIDE), tap_terms, (yi, ci, 0, li, 0, 0)
    )
    gain_terms = jnp.stack([d_gain_one, d_gain_two], 1).reshape(sizes + (rows, 2))
    terms = jnp.concatenate([tap_terms, gain_terms], -1).reshape(-1, rows, TAPS + 2)
    got_p, terms = tied(got_p, terms)
    terms = exchanged(terms, AXES)
    *done, sums_p = adam_first(sizes, w_in, m_in, v_in, got_p)
    *done, sums_o = adam_columns(w_in, m_in, v_in, grad_o, 3 * D, 1, done)
    *done, sums_gate = adam_gate(sizes, w_in, m_in, v_in, got_feed, 0, done)
    *done, sums_up = adam_gate(sizes, w_in, m_in, v_in, got_feed, 1, done)
    grad_down, sums_up = tied(grad_down, sums_up)
    grad_down = grad_down.astype(WIDE)
    grad_down, new_m_down, new_v_down, dir_down, sums_down = adam_down(w_down, m_down, v_down, grad_down)
    grad_in, new_m_in, new_v_in, dir_in = done
    block_out = (middle + out_sum.astype(WIDE)).astype(LOW).reshape(inputs.shape)
    terms = jnp.sum(terms, axis=0)
    grad_taps, grad_gains = terms[:, :TAPS], terms[:, TAPS:]
    new_m_taps, new_v_taps, dir_taps = adam_direction(conv_taps, grad_taps, m_taps, v_taps)
    new_m_gains, new_v_gains, dir_gains = adam_direction(norm_gains, grad_gains, m_gains, v_gains)

    def lanes(a):
        return jnp.pad(jnp.sum(a * a, axis=0), (0, 128 - a.shape[1]))

    def small(taps_like, gains_like):
        return jnp.stack(
            [lanes(taps_like), lanes(gains_like[:, :1]), lanes(gains_like[:, 1:])], 0
        )

    sums = jnp.concatenate(
        [
            jnp.sum(jnp.concatenate([sums_p, sums_o, sums_gate, sums_up, sums_down], 0), axis=2),
            jnp.stack([small(conv_taps, norm_gains), small(dir_taps, dir_gains)], 1),
        ],
        0,
    )
    lamb_norms = jnp.sqrt(jnp.sum(spread_to(sums, AXES), axis=(0, 3)).T)
    ratio = -RATE * lamb_norms[0] / (lamb_norms[1] + 1e-06)
    width = 2048
    new_w_down = w_down + dir_down * ratio[4]
    new_w_in = stepped(ratio[:1], w_in, dir_in, 0, 1, 3 * D // width, width)
    new_w_in = stepped(ratio[1:2], w_in, dir_in, 3 * D // width, 1, D // width, width, new_w_in)
    new_w_in = stepped(ratio[2:4], w_in, dir_in, 4 * D // width, 2, FF // width, width, new_w_in)
    new_w_taps = conv_taps + dir_taps * ratio[5]
    new_w_gains = norm_gains + dir_gains * ratio[6:][None, :]
    return (
        block_out,
        input_grad,
        grad_in,
        grad_down,
        grad_taps,
        grad_gains,
        new_m_in,
        new_m_down,
        new_m_taps,
        new_m_gains,
        new_v_in,
        new_v_down,
        new_v_taps,
        new_v_gains,
        new_w_in,
        new_w_down,
        new_w_taps,
        new_w_gains,
        lamb_norms,
    )


def solution(mesh):
    seq, shard = mesh.shape["seq"], mesh.shape["shard"]
    grid = Mesh(mesh.devices.reshape(seq // 2, 2, 4, shard // 4), AXES)
    tokens = P(("h", "l"), ("y", "c"), None)
    weights = P(AXES, None)
    return jax.shard_map(
        local,
        mesh=grid,
        in_specs=(tokens, tokens, P(("h", "l"), ("y", "c"))) + (weights,) * 12,
        out_specs=(tokens, tokens) + (weights,) * 16 + (P(),),
        check_vma=False,
    )
```

time: 1030 us -> 736 us (0.71); the launches traced: 1010 us -> 727 us
  local copies, waits for them, and re-layouts: 231 us -> 58 us
  Pallas kernels: 0 us -> 148 us
  waiting for transfers between devices: 446 us -> 350 us
  other arithmetic: 128 us -> 50.8 us
  matrix products: 90.5 us -> 15.5 us
    ppermute x47 -> x32, waiting for transfers between devices: 387 us -> 211 us  [turned(): return lax.ppermute(value, ordered if len(names) > 1 else axes, pairs)]
    pallas_call x0 -> x20, Pallas kernels: none -> 148 us  [the longest x3 29.7 us: weight_grads(): pl.pallas_call(functools.partial(weight_kernel, parts, outs), grid=(rows...]
    convert_element_type x43 -> x3, local copies, waits for them, and re-layouts: 80 us -> 1.3 us  [the longest x1 0.89 us: local(): sent_o = [turned(part_o[k].astype(LOW), 'h', k) for k in range(1, nh)]]
    add x28 -> x3, other arithmetic: 46 us -> 4.82 us  [the longest x2 4.19 us: total(): first = first + s.astype(WIDE)]
    all_to_all x10 -> x8, waiting for transfers between devices: 58.9 us -> 95.7 us  [exchanged(): return lax.all_to_all(value, axes, 0, 0, tiled=True)]
    dot_general x5 -> x2, matrix products: 36.2 us -> 3.23 us  [times_wide(): lax.dot_general(left, right, (((1,), (1,)), ((), ())), preferred_element_...]
    reshape x16 -> x7, local copies, waits for them, and re-layouts: 35.7 us -> 6.6 us  [the longest x2 3.74 us: local(): part_p.reshape(ny * nc * nl, rows, 3, channels).swapaxes(1, 2)]
    unnamed x4 -> x9, waiting for transfers between devices: 0.07 us -> 25.7 us
  transfers between devices with their start and end apart: 61 -> 48, of which waited for: 30 -> 29; matrix products, arithmetic and copies ran while one was open for 31% -> 15% of each run, Pallas kernels for 0% -> 14%
where the time goes in v2:
time: 736 us; the launch traced here: 727 us
  waiting for transfers between devices  350 us (48%)
  Pallas kernels  148 us (20%)
  starting transfers between devices  89 us (12%)
  local copies, waits for them, and re-layouts  58 us (8%)
  other arithmetic  50.8 us (7%)
  between operations  15.8 us (2%)
  matrix products  15.5 us (2%)
    ppermute x32, waiting for transfers between devices, turned(): return lax.ppermute(value, ordered if len(names) > 1 else axes, pairs)  211 us
    all_to_all x8, waiting for transfers between devices, exchanged(): return lax.all_to_all(value, axes, 0, 0, tiled=True)  95.7 us
    all_to_all x8, starting transfers between devices, exchanged(): return lax.all_to_all(value, axes, 0, 0, tiled=True)  48.8 us
    ppermute x32, starting transfers between devices, turned(): return lax.ppermute(value, ordered if len(names) > 1 else axes, pairs)  39.7 us
    pallas_call x3, Pallas kernels, weight_grads(): pl.pallas_call(functools.partial(weight_kernel, parts, outs), grid=(rows...  29.7 us
    pallas_call x2, Pallas kernels, both_cores(): pl.pallas_call(functools.partial(both_kernel, len(mine), wide), grid_spec...  26.5 us
    unnamed x9, waiting for transfers between devices  25.7 us
    pallas_call x2, Pallas kernels, feed(): pl.pallas_call(feed_kernel, grid=(features // tile,), in_specs=[whole, wh...  24.5 us
  transfers between devices with their start and end apart: 48, of which 29 were waited for; matrix products, arithmetic and copies ran while one was open for 15% of the time, Pallas kernels for 14%

profile of v2, /device:TPU:0, one launch (start us, length us, event | category | flops | bytes accessed | tf_op | source)
XLA Modules:
  0.0 727.3 jit_solution(7755861319115053515)
XLA Ops:
  12.1 7.3 %all-to-all-start = ((f32[32,1,448]{2,1,0:T(1,128)}), f32[32,1,448]{2,1,0:T(1,128)S(1)}, u32[]{:S(2)}, u32[]{:S(2)}) async-start(f32[32,1,448]{2,1,0:T(1,128)} %broadcast_in_dim.57), calls=%async_computation | async-start | bytes 131072 | tf_op jit(solution)/shard_map/all_to_all | solution.py:55
  38.4 3.7 all-to-all-start.1
  47.2 9.8 %collective-permute-done.4 = bf16[128,2048]{1,0:T(8,128)(2,1)S(1)} collective-permute-done((bf16[128,2048]{1,0:T(8,128)(2,1)S(1)}, bf16[128,2048]{1,0:T(8,128)(2,1)S(1)}, u32[]{:S(2)}, u32[]{:S(2)}) %collective-permute-start.4) | collective-permute-done | bytes 524320 | tf_op jit(solution)/shard_map/ppermute | solution.py:43
  62.2 5.6 collective-permute-done.1
  68.7 14.9 %all-to-all-start.2 = ((bf16[8,64,1024]{2,1,0:T(8,128)(2,1)}), bf16[8,64,1024]{2,1,0:T(8,128)(2,1)S(1)}, u32[]{:S(2)}, u32[]{:S(2)}) async-start(bf16[8,64,1024]{2,1,0:T(8,128)(2,1)} %shard_map.295), calls=%async_computation.2 | async-start | bytes 2097152 | tf_op jit(solution)/shard_map/all_to_all | solution.py:55
  86.7 23.5 %all-to-all-done.2 = bf16[8,64,1024]{2,1,0:T(8,128)(2,1)S(1)} async-done(((bf16[8,64,1024]{2,1,0:T(8,128)(2,1)}), bf16[8,64,1024]{2,1,0:T(8,128)(2,1)S(1)}, u32[]{:S(2)}, u32[]{:S(2)}) %all-to-all-start.2) | async-done | bytes 1048608 | tf_op jit(solution)/shard_map/all_to_all | solution.py:55
  113.5 16.8 %collective-permute-done.7 = bf16[512,768]{1,0:T(8,128)(2,1)} collective-permute-done((bf16[512,768]{1,0:T(8,128)(2,1)S(1)}, bf16[512,768]{1,0:T(8,128)(2,1)}, u32[]{:S(2)}, u32[]{:S(2)}) %collective-permute-start.7) | collective-permute-done | bytes 786464 | tf_op jit(solution)/shard_map/ppermute | solution.py:43
  135.8 14.5 %collective-permute-done.8 = bf16[512,768]{1,0:T(8,128)(2,1)S(1)} collective-permute-done((bf16[512,768]{1,0:T(8,128)(2,1)}, bf16[512,768]{1,0:T(8,128)(2,1)S(1)}, u32[]{:S(2)}, u32[]{:S(2)}) %collective-permute-start.8) | collective-permute-done | bytes 786464 | tf_op jit(solution)/shard_map/ppermute | solution.py:43
  150.3 4.6 collective-permute-start.9
  162.5 7.6 %collective-permute-done.9 = bf16[512,768]{1,0:T(8,128)(2,1)S(1)} collective-permute-done((bf16[512,768]{1,0:T(8,128)(2,1)S(1)}, bf16[512,768]{1,0:T(8,128)(2,1)S(1)}, u32[]{:S(2)}, u32[]{:S(2)}) %collective-permute-start.9) | collective-permute-done | bytes 786464 | tf_op jit(solution)/shard_map/ppermute | solution.py:43
  178.0 5.7 all-to-all-start.3
  188.4 22.0 %all-to-all-done.3 = bf16[8,64,1024]{2,1,0:T(8,128)(2,1)} async-done(((bf16[8,64,1024]{2,1,0:T(8,128)(2,1)}), bf16[8,64,1024]{2,1,0:T(8,128)(2,1)}, u32[]{:S(2)}, u32[]{:S(2)}) %all-to-all-start.3) | async-done | bytes 1048608 | tf_op jit(solution)/shard_map/all_to_all | solution.py:55
  215.3 20.4 %collective-permute-done.13 = bf16[128,2048]{1,0:T(8,128)(2,1)S(1)} collective-permute-done((bf16[128,2048]{1,0:T(8,128)(2,1)}, bf16[128,2048]{1,0:T(8,128)(2,1)S(1)}, u32[]{:S(2)}, u32[]{:S(2)}) %collective-permute-start.13) | collective-permute-done | bytes 524320 | tf_op jit(solution)/shard_map/ppermute | solution.py:43
  235.7 13.2 %collective-permute-done.12 = bf16[128,2048]{1,0:T(8,128)(2,1)S(1)} collective-permute-done((bf16[128,2048]{1,0:T(8,128)(2,1)}, bf16[128,2048]{1,0:T(8,128)(2,1)S(1)}, u32[]{:S(2)}, u32[]{:S(2)}) %collective-permute-start.12) | collective-permute-done | bytes 524320 | tf_op jit(solution)/shard_map/ppermute | solution.py:43
  259.2 9.9 %collective-permute-done.16 = bf16[128,2048]{0,1:T(8,128)(2,1)} collective-permute-done((bf16[128,2048]{0,1:T(8,128)(2,1)}, bf16[128,2048]{0,1:T(8,128)(2,1)}, u32[]{:S(2)}, u32[]{:S(2)}) %collective-permute-start.16) | collective-permute-done | bytes 524320 | tf_op jit(solution)/shard_map/ppermute | solution.py:43
  271.1 18.3 %collective-permute-done.15 = bf16[128,2048]{0,1:T(8,128)(2,1)} collective-permute-done((bf16[128,2048]{0,1:T(8,128)(2,1)}, bf16[128,2048]{0,1:T(8,128)(2,1)}, u32[]{:S(2)}, u32[]{:S(2)}) %collective-permute-start.15) | collective-permute-done | bytes 524320 | tf_op jit(solution)/shard_map/ppermute | solution.py:43
  295.9 5.5 constant_dynamic-slice_fusion
  301.4 12.2 %shard_map.297 = (bf16[512,1024]{1,0:T(8,128)(2,1)}, bf16[512,1024]{1,0:T(8,128)(2,1)}, bf16[512,1024]{1,0:T(8,128)(2,1)}) custom-call(bf16[512,2048]{1,0:T(8,128)(2,1)} %bitcast.203, bf16[512,2048]{1,0:T(8,128)(2,1)} %bitcast.200, bf16[2048,1024]{1,0:T(8,128)(2,1)} %all-gather.7.cloned.1.call-done.g_ref.refs_4_, ...), custom_call_target="tpu_custom_call" | custom-call | flops 1024 | bytes 1024 | tf_op jit(solution)/shard_map/pallas_call | solution.py:135
  313.7 12.3 %shard_map.298 = (bf16[512,1024]{1,0:T(8,128)(2,1)}, bf16[512,1024]{1,0:T(8,128)(2,1)}, bf16[512,1024]{1,0:T(8,128)(2,1)}) custom-call(bf16[512,2048]{1,0:T(8,128)(2,1)} %collective-permute-done.17.h_ref.refs_1_, bf16[512,2048]{1,0:T(8,128)(2,1)} %bitcast.198, bf16[2048,1024]{1,0:T(8,128)(2,1)} %all-gather.7.cloned.1.call-done.g_ref.refs_4_, ...), custom_call_target="tpu_custom_call" | custom-call | flops 1024 | bytes 1024 | tf_op jit(solution)/shard_map/pallas_call | solution.py:135
  325.9 15.6 %shard_map.299 = bf16[4,2,128,2048]{3,2,1,0:T(8,128)(2,1)} custom-call(s32[1]{0:T(128)} %bitcast.22.c_ref, bf16[512,1024]{1,0:T(8,128)(2,1)} %get-tuple-element.119.refs_0_.refs_2_, bf16[512,1024]{1,0:T(8,128)(2,1)} %get-tuple-element.120.refs_1_.refs_3_, bf16[512,1024]{1,0:T(8,128)(2,1)} %get-tuple-element.121.refs_2_.refs_4_, ...), custom_call_target="tpu_custom_call" | custom-call | flops 1024 | bytes 1024 | tf_op jit(solution)/shard_map/pallas_call | solution.py:206
  341.6 13.4 %shard_map.300 = bf16[2048,2048]{1,0:T(8,128)(2,1)} custom-call(bf16[512,2048]{1,0:T(8,128)(2,1)} %bitcast.204, bf16[512,2048]{1,0:T(8,128)(2,1)} %collective-permute-done.17.h_ref.refs_1_, bf16[512,1024]{1,0:T(8,128)(2,1)} %get-tuple-element.119.refs_0_.refs_2_, bf16[512,1024]{1,0:T(8,128)(2,1)} %get-tuple-element.120.refs_1_.refs_3_, ...), custom_call_target="tpu_custom_call" | custom-call | flops 1024 | bytes 1024 | tf_op jit(solution)/shard_map/pallas_call | solution.py:242
  355.0 9.0 %shard_map.301 = bf16[1024,2048]{1,0:T(8,128)(2,1)} custom-call(bf16[512,1024]{1,0:T(8,128)(2,1)} %get-tuple-element.126.refs_0_, bf16[512,1024]{1,0:T(8,128)(2,1)} %get-tuple-element.127.refs_1_, bf16[512,2048]{1,0:T(8,128)(2,1)} %bitcast.201, bf16[512,2048]{1,0:T(8,128)(2,1)} %bitcast.199), custom_call_target="tpu_custom_call" | custom-call | flops 1024 | bytes 1024 | tf_op jit(solution)/shard_map/pallas_call | solution.py:242
  364.0 10.9 %shard_map.302 = bf16[4,2,128,2048]{3,2,1,0:T(8,128)(2,1)} custom-call(s32[1]{0:T(128)} %bitcast.22.c_ref, bf16[512,1024]{1,0:T(8,128)(2,1)} %get-tuple-element.126.refs_0_, bf16[512,1024]{1,0:T(8,128)(2,1)} %get-tuple-element.127.refs_1_, bf16[1024,2048]{1,0:T(8,128)(2,1)} %all-gather.11.cloned.1.call-done.d_ref.refs_2_), custom_call_target="tpu_custom_call" | custom-call | flops 1024 | bytes 1024 | tf_op jit(solution)/shard_map/pallas_call | solution.py:206
  374.9 24.9 %reduce-scatter.13.cloned.1.call-done = bf16[128,2048]{1,0:T(8,128)(2,1)} async-done(((bf16[1024,2048]{1,0:T(8,128)(2,1)}), bf16[128,2048]{1,0:T(8,128)(2,1)}) %reduce-scatter.13.cloned.1.call-update) | async-done | bytes 524304
  408.7 11.4 %collective-permute-done.20 = bf16[128,2048]{1,0:T(8,128)(2,1)S(1)} collective-permute-done((bf16[128,2048]{1,0:T(8,128)(2,1)S(1)}, bf16[128,2048]{1,0:T(8,128)(2,1)S(1)}, u32[]{:S(2)}, u32[]{:S(2)}) %collective-permute-start.20) | collective-permute-done | bytes 524320 | tf_op jit(solution)/shard_map/ppermute | solution.py:43
  420.7 7.3 %collective-permute-done.18 = bf16[128,2048]{1,0:T(8,128)(2,1)S(1)} collective-permute-done((bf16[128,2048]{1,0:T(8,128)(2,1)S(1)}, bf16[128,2048]{1,0:T(8,128)(2,1)S(1)}, u32[]{:S(2)}, u32[]{:S(2)}) %collective-permute-start.18) | collective-permute-done | bytes 524320 | tf_op jit(solution)/shard_map/ppermute | solution.py:43
  428.3 4.2 collective-permute-done.21
  450.3 7.3 %shard_map.303 = bf16[2048,768]{1,0:T(8,128)(2,1)} custom-call(bf16[1024,2048]{1,0:T(8,128)(2,1)} %bitcast.208, bf16[1024,768]{1,0:T(8,128)(2,1)} %pad_maximum_fusion.1.refs_1_), custom_call_target="tpu_custom_call" | custom-call | flops 1024 | bytes 1024 | tf_op jit(solution)/shard_map/pallas_call | solution.py:242
  457.7 14.2 %collective-permute-done.23 = bf16[64,2048]{1,0:T(8,128)(2,1)} collective-permute-done((bf16[64,2048]{1,0:T(8,128)(2,1)}, bf16[64,2048]{1,0:T(8,128)(2,1)}, u32[]{:S(2)}, u32[]{:S(2)}) %collective-permute-start.23) | collective-permute-done | bytes 262176 | tf_op jit(solution)/shard_map/ppermute | solution.py:43
  473.4 21.3 %collective-permute-done.25 = bf16[512,768]{1,0:T(8,128)(2,1)S(1)} collective-permute-done((bf16[512,768]{1,0:T(8,128)(2,1)S(1)}, bf16[512,768]{1,0:T(8,128)(2,1)S(1)}, u32[]{:S(2)}, u32[]{:S(2)}) %collective-permute-start.25) | collective-permute-done | bytes 786464 | tf_op jit(solution)/shard_map/ppermute | solution.py:43
  496.1 20.4 %collective-permute-done.26 = bf16[512,768]{1,0:T(8,128)(2,1)S(1)} collective-permute-done((bf16[512,768]{1,0:T(8,128)(2,1)S(1)}, bf16[512,768]{1,0:T(8,128)(2,1)S(1)}, u32[]{:S(2)}, u32[]{:S(2)}) %collective-permute-start.26) | collective-permute-done | bytes 786464 | tf_op jit(solution)/shard_map/ppermute | solution.py:43
  518.4 5.4 shard_map.304
  523.8 12.4 %collective-permute-done.27 = bf16[512,768]{1,0:T(8,128)(2,1)S(1)} collective-permute-done((bf16[512,768]{1,0:T(8,128)(2,1)S(1)}, bf16[512,768]{1,0:T(8,128)(2,1)S(1)}, u32[]{:S(2)}, u32[]{:S(2)}) %collective-permute-start.27) | collective-permute-done | bytes 786464 | tf_op jit(solution)/shard_map/ppermute | solution.py:43
  537.3 17.7 %reduce-scatter.9.cloned.1.call-done = bf16[512,2048]{1,0:T(8,128)(2,1)} async-done(((bf16[2048,2048]{1,0:T(8,128)(2,1)}), bf16[512,2048]{1,0:T(8,128)(2,1)}) %reduce-scatter.9.cloned.1.call-update) | async-done | bytes 2097168 | tf_op jit(solution)/shard_map/reduce_scatter | solution.py:599
  555.0 4.6 all-to-all-start.4
  561.9 5.9 shard_map.305
  581.6 27.1 %all-to-all-done.4 = bf16[8,64,2048]{2,1,0:T(8,128)(2,1)S(1)} async-done(((bf16[8,64,2048]{2,1,0:T(8,128)(2,1)}), bf16[8,64,2048]{2,1,0:T(8,128)(2,1)S(1)}, u32[]{:S(2)}, u32[]{:S(2)}) %all-to-all-start.4) | async-done | bytes 2097184 | tf_op jit(solution)/shard_map/all_to_all | solution.py:55
  612.4 4.2 all-to-all-start.5
  622.9 13.1 %all-to-all-done.5.got_ref = bf16[8,3,64,256]{3,2,1,0:T(8,128)(2,1)} async-done(((bf16[8,3,64,256]{3,2,1,0:T(8,128)(2,1)}), bf16[8,3,64,256]{3,2,1,0:T(8,128)(2,1)}, u32[]{:S(2)}, u32[]{:S(2)}) %all-to-all-start.5) | async-done | bytes 786464 | tf_op jit(solution)/shard_map/all_to_all | solution.py:55
  639.3 6.8 shard_map.306
  648.9 7.6 %shard_map.308 = (f32[64,24576]{1,0:T(8,128)}, f32[64,24576]{1,0:T(8,128)}, f32[64,24576]{1,0:T(8,128)}, f32[64,24576]{1,0:T(8,128)}, f32[1,2,8,128]{3,2,1,0:T(8,128)}) custom-call(f32[64,24576]{1,0:T(8,128)} %w_ref.21, f32[64,24576]{1,0:T(8,128)} %m_ref.8, ...), custom_call_target="tpu_custom_call", output_to_operand_aliasing={{0}: (4, {}), {1}: (5, {}), {2}: (6, {}), {3}: (7, {})} | custom-call | flops 1024 | bytes 1024 | tf_op jit(solution)/shard_map/pallas_call | solution.py:343
  656.5 7.6 %shard_map.309 = (f32[64,24576]{1,0:T(8,128)}, f32[64,24576]{1,0:T(8,128)}, f32[64,24576]{1,0:T(8,128)}, f32[64,24576]{1,0:T(8,128)}, f32[1,2,8,128]{3,2,1,0:T(8,128)}) custom-call(f32[64,24576]{1,0:T(8,128)} %w_ref.21, f32[64,24576]{1,0:T(8,128)} %m_ref.8, ...), custom_call_target="tpu_custom_call", output_to_operand_aliasing={{0}: (4, {}), {1}: (5, {}), {2}: (6, {}), {3}: (7, {})} | custom-call | flops 1024 | bytes 1024 | tf_op jit(solution)/shard_map/pallas_call | solution.py:343
  667.0 7.8 %shard_map.310 = (f32[256,2048]{1,0:T(8,128)}, f32[256,2048]{1,0:T(8,128)}, f32[256,2048]{1,0:T(8,128)}, f32[256,2048]{1,0:T(8,128)}, f32[1,2,8,128]{3,2,1,0:T(8,128)}) custom-call(f32[256,2048]{1,0:T(8,128)} %w_ref.18, f32[256,2048]{1,0:T(8,128)} %m_ref.9, f32[256,2048]{1,0:T(8,128)} %v_ref.9, f32[256,2048]{1,0:T(8,128)} %convert_element_type.241.g_ref), custom_call_target="tpu_custom_call" | custom-call | flops 1024 | bytes 1024 | tf_op jit(solution)/shard_map/pallas_call | solution.py:385
  681.1 5.8 all-to-all-start.7
  690.1 7.5 %all-to-all-done.7 = f32[32,8,2,128]{3,1,2,0:T(8,128)S(1)} async-done(((f32[32,8,2,128]{3,1,2,0:T(8,128)}), f32[32,8,2,128]{3,1,2,0:T(8,128)S(1)}, u32[]{:S(2)}, u32[]{:S(2)}) %all-to-all-start.7) | async-done | bytes 262176 | tf_op jit(solution)/shard_map/all_to_all | solution.py:55
  700.9 3.8 multiply_add_fusion
  704.7 4.4 shard_map.311.refs_0_
  711.8 8.3 %shard_map.313 = f32[64,24576]{1,0:T(8,128)} custom-call(f32[2]{0:T(128)} %get-tuple-element.244.ratio_ref, f32[64,24576]{1,0:T(8,128)} %w_ref.21, f32[64,24576]{1,0:T(8,128)} %get-tuple-element.177.dir_ref, f32[64,24576]{1,0:T(8,128)} %shard_map.312.refs_0_), custom_call_target="tpu_custom_call", output_to_operand_aliasing={{}: (3, {})} | custom-call | flops 1024 | bytes 1024 | tf_op jit(solution)/shard_map/pallas_call | solution.py:432
  (318 shorter events, 174.0 us)
Async XLA Ops:
  7.2 208.1 %all-gather.5.cloned.1.call-start = ((), (), s32[]{:S(2)}) async-start(), calls=%async_computation.12 | async-start | bytes 4718592 | tf_op jit(solution)/shard_map/all_gather | solution.py:540
  8.0 293.4 %all-gather.11.cloned.1.call-start = ((), (), s32[]{:S(2)}) async-start(), calls=%async_computation.15 | async-start | bytes 5242880 | tf_op jit(solution)/shard_map/all_gather | solution.py:541
  12.1 14.7 %all-to-all-start = ((f32[32,1,448]{2,1,0:T(1,128)}), f32[32,1,448]{2,1,0:T(1,128)S(1)}, u32[]{:S(2)}, u32[]{:S(2)}) async-start(f32[32,1,448]{2,1,0:T(1,128)} %broadcast_in_dim.57), calls=%async_computation | async-start | bytes 131072 | tf_op jit(solution)/shard_map/all_to_all | solution.py:55
  30.2 14.1 %collective-permute-start.3 = (bf16[128,2048]{1,0:T(8,128)(2,1)S(1)}, bf16[128,2048]{1,0:T(8,128)(2,1)S(1)}, u32[]{:S(2)}, u32[]{:S(2)}) collective-permute-start(bf16[128,2048]{1,0:T(8,128)(2,1)S(1)} %reshape.356), channel_id=1, source_target_pairs={{0,17},{16,0},{1,16},{17,1},{2,19},{18,2},{3,18},{19,3},{4,21},{20... | collective-permute-start | bytes 1572872 | tf_op jit(solution)/shard_map/ppermute | solution.py:43
  32.0 25.0 %collective-permute-start.4 = (bf16[128,2048]{1,0:T(8,128)(2,1)S(1)}, bf16[128,2048]{1,0:T(8,128)(2,1)S(1)}, u32[]{:S(2)}, u32[]{:S(2)}) collective-permute-start(bf16[128,2048]{1,0:T(8,128)(2,1)S(1)} %reshape.356), channel_id=1, source_target_pairs={{0,1},{16,17},{1,0},{17,16},{2,3},{18,19},{3,2},{19,18},{4,5},{20,... | collective-permute-start | bytes 1572872 | tf_op jit(solution)/shard_map/ppermute | solution.py:43
  34.0 28.3 %collective-permute-start.2 = (bf16[64,2048]{1,0:T(8,128)(2,1)S(1)}, bf16[64,2048]{1,0:T(8,128)(2,1)S(1)}, u32[]{:S(2)}, u32[]{:S(2)}) collective-permute-start(bf16[64,2048]{1,0:T(8,128)(2,1)S(1)} %slice.292), channel_id=1, source_target_pairs={{0,2},{2,4},{4,6},{6,0},{1,3},{3,5},{5,7},{7,1},{8,10},{10,12},{12... | collective-permute-start | bytes 786440 | tf_op jit(solution)/shard_map/ppermute | solution.py:43
  34.0 33.8 %collective-permute-start.1 = (bf16[64,2048]{1,0:T(8,128)(2,1)S(1)}, bf16[64,2048]{1,0:T(8,128)(2,1)}, u32[]{:S(2)}, u32[]{:S(2)}) collective-permute-start(bf16[64,2048]{1,0:T(8,128)(2,1)S(1)} %slice.292), channel_id=1, source_target_pairs={{0,4},{2,6},{4,0},{6,2},{1,5},{3,7},{5,1},{7,3},{8,12},{10,14},{12... | collective-permute-start | bytes 786440 | tf_op jit(solution)/shard_map/ppermute | solution.py:43
  37.1 20.9 %collective-permute-start.5 = (bf16[128,2048]{1,0:T(8,128)(2,1)S(1)}, bf16[128,2048]{1,0:T(8,128)(2,1)}, u32[]{:S(2)}, u32[]{:S(2)}) collective-permute-start(bf16[128,2048]{1,0:T(8,128)(2,1)S(1)} %reshape.356), channel_id=1, source_target_pairs={{0,16},{16,1},{1,17},{17,0},{2,18},{18,3},{3,19},{19,2},{4,20},{20... | collective-permute-start | bytes 1572872 | tf_op jit(solution)/shard_map/ppermute | solution.py:43
  38.4 30.3 %all-to-all-start.1 = ((bf16[8,3,64,256]{3,2,1,0:T(8,128)(2,1)}), bf16[8,3,64,256]{3,2,1,0:T(8,128)(2,1)S(1)}, u32[]{:S(2)}, u32[]{:S(2)}) async-start(bf16[8,3,64,256]{3,2,1,0:T(8,128)(2,1)} %shard_map.294), calls=%async_computation.1 | async-start | bytes 1572864 | tf_op jit(solution)/shard_map/all_to_all | solution.py:55
  44.3 24.4 %collective-permute-start = (bf16[64,2048]{1,0:T(8,128)(2,1)S(1)}, bf16[64,2048]{1,0:T(8,128)(2,1)}, u32[]{:S(2)}, u32[]{:S(2)}) collective-permute-start(bf16[64,2048]{1,0:T(8,128)(2,1)S(1)} %slice.292), channel_id=1, source_target_pairs={{0,6},{2,0},{4,2},{6,4},{1,7},{3,1},{5,3},{7,5},{8,14},{10,8},{12,... | collective-permute-start | bytes 786440 | tf_op jit(solution)/shard_map/ppermute | solution.py:43
  59.8 50.3 %collective-permute-start.6 = (bf16[512,2048]{1,0:T(8,128)(2,1)}, bf16[512,2048]{1,0:T(8,128)(2,1)}, u32[]{:S(2)}, u32[]{:S(2)}) collective-permute-start(bf16[512,2048]{1,0:T(8,128)(2,1)} %constant_dynamic-update-slice_fusion), channel_id=1, source_target_pairs={{0,8},{8,0},{1,9},{9,1},{2,10},{10,2},{3,11},{11,3},{4,12},{12,4},... | collective-permute-start | bytes 6291464 | tf_op jit(solution)/shard_map/ppermute | solution.py:43
  68.7 41.5 %all-to-all-start.2 = ((bf16[8,64,1024]{2,1,0:T(8,128)(2,1)}), bf16[8,64,1024]{2,1,0:T(8,128)(2,1)S(1)}, u32[]{:S(2)}, u32[]{:S(2)}) async-start(bf16[8,64,1024]{2,1,0:T(8,128)(2,1)} %shard_map.295), calls=%async_computation.2 | async-start | bytes 2097152 | tf_op jit(solution)/shard_map/all_to_all | solution.py:55
  83.6 217.8 %all-gather.7.cloned.1.call-start = ((), (), s32[]{:S(2)}) async-start(), calls=%async_computation.13 | async-start | bytes 5242880 | tf_op jit(solution)/shard_map/all_gather | solution.py:550
  111.0 19.2 %collective-permute-start.7 = (bf16[512,768]{1,0:T(8,128)(2,1)S(1)}, bf16[512,768]{1,0:T(8,128)(2,1)}, u32[]{:S(2)}, u32[]{:S(2)}) collective-permute-start(bf16[512,768]{1,0:T(8,128)(2,1)S(1)} %bitcast.231), channel_id=1, source_target_pairs={{0,6},{2,0},{4,2},{6,4},{1,7},{3,1},{5,3},{7,5},{8,14},{10,8},{12,... | collective-permute-start | bytes 2359304 | tf_op jit(solution)/shard_map/ppermute | solution.py:43
  130.3 20.0 %collective-permute-start.8 = (bf16[512,768]{1,0:T(8,128)(2,1)}, bf16[512,768]{1,0:T(8,128)(2,1)S(1)}, u32[]{:S(2)}, u32[]{:S(2)}) collective-permute-start(bf16[512,768]{1,0:T(8,128)(2,1)} %collective-permute-done.7), channel_id=1, source_target_pairs={{0,6},{2,0},{4,2},{6,4},{1,7},{3,1},{5,3},{7,5},{8,14},{10,8},{12,... | collective-permute-start | bytes 2359304 | tf_op jit(solution)/shard_map/ppermute | solution.py:43
  150.3 19.9 %collective-permute-start.9 = (bf16[512,768]{1,0:T(8,128)(2,1)S(1)}, bf16[512,768]{1,0:T(8,128)(2,1)S(1)}, u32[]{:S(2)}, u32[]{:S(2)}) collective-permute-start(bf16[512,768]{1,0:T(8,128)(2,1)S(1)} %collective-permute-done.8), channel_id=1, source_target_pairs={{0,6},{2,0},{4,2},{6,4},{1,7},{3,1},{5,3},{7,5},{8,14},{10,8},{12,... | collective-permute-start | bytes 2359304 | tf_op jit(solution)/shard_map/ppermute | solution.py:43
  178.0 5.7 collective-permute-start.10
  178.0 32.4 %all-to-all-start.3 = ((bf16[8,64,1024]{2,1,0:T(8,128)(2,1)}), bf16[8,64,1024]{2,1,0:T(8,128)(2,1)}, u32[]{:S(2)}, u32[]{:S(2)}) async-start(bf16[8,64,1024]{2,1,0:T(8,128)(2,1)} %shard_map.296), calls=%async_computation.3 | async-start | bytes 2097152 | tf_op jit(solution)/shard_map/all_to_all | solution.py:55
  183.7 117.7 %all-gather.9.cloned.1.call-start = ((), (), s32[]{:S(2)}) async-start(), calls=%async_computation.14 | async-start | bytes 5242880 | tf_op jit(solution)/shard_map/all_gather | solution.py:584
  210.4 189.4 %reduce-scatter.13.cloned.1.call-start = ((), (), s32[]{:S(2)}) async-start(), calls=%async_computation.19 | async-start | bytes 4718592
  211.7 24.0 %collective-permute-start.13 = (bf16[128,2048]{1,0:T(8,128)(2,1)}, bf16[128,2048]{1,0:T(8,128)(2,1)S(1)}, u32[]{:S(2)}, u32[]{:S(2)}) collective-permute-start(bf16[128,2048]{1,0:T(8,128)(2,1)} %get-tuple-element.225), channel_id=1, source_target_pairs={{0,17},{16,0},{1,16},{17,1},{2,19},{18,2},{3,18},{19,3},{4,21},{20... | collective-permute-start | bytes 1572872 | tf_op jit(solution)/shard_map/ppermute | solution.py:43
  214.2 34.7 %collective-permute-start.12 = (bf16[128,2048]{1,0:T(8,128)(2,1)}, bf16[128,2048]{1,0:T(8,128)(2,1)S(1)}, u32[]{:S(2)}, u32[]{:S(2)}) collective-permute-start(bf16[128,2048]{1,0:T(8,128)(2,1)} %get-tuple-element.226), channel_id=1, source_target_pairs={{0,1},{16,17},{1,0},{17,16},{2,3},{18,19},{3,2},{19,18},{4,5},{20,... | collective-permute-start | bytes 1572872 | tf_op jit(solution)/shard_map/ppermute | solution.py:43
  214.7 34.3 %collective-permute-start.11 = (bf16[128,2048]{1,0:T(8,128)(2,1)}, bf16[128,2048]{1,0:T(8,128)(2,1)S(1)}, u32[]{:S(2)}, u32[]{:S(2)}) collective-permute-start(bf16[128,2048]{1,0:T(8,128)(2,1)} %get-tuple-element.227), channel_id=1, source_target_pairs={{0,16},{16,1},{1,17},{17,0},{2,18},{18,3},{3,19},{19,2},{4,20},{20... | collective-permute-start | bytes 1572872 | tf_op jit(solution)/shard_map/ppermute | solution.py:43
  252.0 17.1 %collective-permute-start.16 = (bf16[128,2048]{0,1:T(8,128)(2,1)}, bf16[128,2048]{0,1:T(8,128)(2,1)}, u32[]{:S(2)}, u32[]{:S(2)}) collective-permute-start(bf16[128,2048]{0,1:T(8,128)(2,1)} %bitcast.27), channel_id=1, source_target_pairs={{0,2},{2,4},{4,6},{6,0},{1,3},{3,5},{5,7},{7,1},{8,10},{10,12},{12... | collective-permute-start | bytes 1572872 | tf_op jit(solution)/shard_map/ppermute | solution.py:43
  252.0 37.4 %collective-permute-start.15 = (bf16[128,2048]{0,1:T(8,128)(2,1)}, bf16[128,2048]{0,1:T(8,128)(2,1)}, u32[]{:S(2)}, u32[]{:S(2)}) collective-permute-start(bf16[128,2048]{0,1:T(8,128)(2,1)} %bitcast.27), channel_id=1, source_target_pairs={{0,4},{2,6},{4,0},{6,2},{1,5},{3,7},{5,1},{7,3},{8,12},{10,14},{12... | collective-permute-start | bytes 1572872 | tf_op jit(solution)/shard_map/ppermute | solution.py:43
  254.3 37.2 %collective-permute-start.14 = (bf16[128,2048]{0,1:T(8,128)(2,1)}, bf16[128,2048]{0,1:T(8,128)(2,1)}, u32[]{:S(2)}, u32[]{:S(2)}) collective-permute-start(bf16[128,2048]{0,1:T(8,128)(2,1)} %bitcast.27), channel_id=1, source_target_pairs={{0,6},{2,0},{4,2},{6,4},{1,7},{3,1},{5,3},{7,5},{8,14},{10,8},{12,... | collective-permute-start | bytes 1572872 | tf_op jit(solution)/shard_map/ppermute | solution.py:43
  295.8 17.9 %collective-permute-start.17 = (bf16[512,2048]{1,0:T(8,128)(2,1)S(1)}, bf16[512,2048]{1,0:T(8,128)(2,1)}, u32[]{:S(2)}, u32[]{:S(2)}) collective-permute-start(bf16[512,2048]{1,0:T(8,128)(2,1)S(1)} %bitcast.202), channel_id=1, source_target_pairs={{0,8},{8,0},{1,9},{9,1},{2,10},{10,2},{3,11},{11,3},{4,12},{12,4},... | collective-permute-start | bytes 6291464 | tf_op jit(solution)/shard_map/ppermute | solution.py:43
  341.6 130.4 %reduce-scatter.7.cloned.1.call-start = ((), (), s32[]{:S(2)}) async-start(), calls=%async_computation.16 | async-start | bytes 4718592 | tf_op jit(solution)/shard_map/reduce_scatter | solution.py:599
  401.2 153.8 %reduce-scatter.9.cloned.1.call-start = ((), (), s32[]{:S(2)}) async-start(), calls=%async_computation.17 | async-start | bytes 10485760 | tf_op jit(solution)/shard_map/reduce_scatter | solution.py:599
  404.3 15.8 %collective-permute-start.20 = (bf16[128,2048]{1,0:T(8,128)(2,1)S(1)}, bf16[128,2048]{1,0:T(8,128)(2,1)S(1)}, u32[]{:S(2)}, u32[]{:S(2)}) collective-permute-start(bf16[128,2048]{1,0:T(8,128)(2,1)S(1)} %get-tuple-element.210), channel_id=1, source_target_pairs={{0,16},{16,1},{1,17},{17,0},{2,18},{18,3},{3,19},{19,2},{4,20},{20... | collective-permute-start | bytes 1572872 | tf_op jit(solution)/shard_map/ppermute | solution.py:43
  405.8 14.9 %collective-permute-start.19 = (bf16[128,2048]{1,0:T(8,128)(2,1)S(1)}, bf16[128,2048]{1,0:T(8,128)(2,1)S(1)}, u32[]{:S(2)}, u32[]{:S(2)}) collective-permute-start(bf16[128,2048]{1,0:T(8,128)(2,1)S(1)} %get-tuple-element.210), channel_id=1, source_target_pairs={{0,1},{16,17},{1,0},{17,16},{2,3},{18,19},{3,2},{19,18},{4,5},{20,... | collective-permute-start | bytes 1572872 | tf_op jit(solution)/shard_map/ppermute | solution.py:43
  407.3 20.7 %collective-permute-start.18 = (bf16[128,2048]{1,0:T(8,128)(2,1)S(1)}, bf16[128,2048]{1,0:T(8,128)(2,1)S(1)}, u32[]{:S(2)}, u32[]{:S(2)}) collective-permute-start(bf16[128,2048]{1,0:T(8,128)(2,1)S(1)} %get-tuple-element.210), channel_id=1, source_target_pairs={{0,17},{16,0},{1,16},{17,1},{2,19},{18,2},{3,18},{19,3},{4,21},{20... | collective-permute-start | bytes 1572872 | tf_op jit(solution)/shard_map/ppermute | solution.py:43
  428.2 4.4 collective-permute-start.21
  432.5 231.5 %reduce-scatter.11.cloned.1.call-start = ((), (), s32[]{:S(2)}) async-start(), calls=%async_computation.18 | async-start | bytes 5242880 | tf_op jit(solution)/shard_map/reduce_scatter | solution.py:599
  438.5 19.2 %collective-permute-start.24 = (bf16[64,2048]{1,0:T(8,128)(2,1)}, bf16[64,2048]{1,0:T(8,128)(2,1)S(1)}, u32[]{:S(2)}, u32[]{:S(2)}) collective-permute-start(bf16[64,2048]{1,0:T(8,128)(2,1)} %get-tuple-element.230), channel_id=1, source_target_pairs={{0,6},{2,0},{4,2},{6,4},{1,7},{3,1},{5,3},{7,5},{8,14},{10,8},{12,... | collective-permute-start | bytes 786440 | tf_op jit(solution)/shard_map/ppermute | solution.py:43
  441.4 30.5 %collective-permute-start.23 = (bf16[64,2048]{1,0:T(8,128)(2,1)}, bf16[64,2048]{1,0:T(8,128)(2,1)}, u32[]{:S(2)}, u32[]{:S(2)}) collective-permute-start(bf16[64,2048]{1,0:T(8,128)(2,1)} %get-tuple-element.231), channel_id=1, source_target_pairs={{0,4},{2,6},{4,0},{6,2},{1,5},{3,7},{5,1},{7,3},{8,12},{10,14},{12... | collective-permute-start | bytes 786440 | tf_op jit(solution)/shard_map/ppermute | solution.py:43
  441.4 30.5 %collective-permute-start.22 = (bf16[64,2048]{1,0:T(8,128)(2,1)}, bf16[64,2048]{1,0:T(8,128)(2,1)}, u32[]{:S(2)}, u32[]{:S(2)}) collective-permute-start(bf16[64,2048]{1,0:T(8,128)(2,1)} %get-tuple-element.232), channel_id=1, source_target_pairs={{0,2},{2,4},{4,6},{6,0},{1,3},{3,5},{5,7},{7,1},{8,10},{10,12},{12... | collective-permute-start | bytes 786440 | tf_op jit(solution)/shard_map/ppermute | solution.py:43
  473.3 21.3 %collective-permute-start.25 = (bf16[512,768]{1,0:T(8,128)(2,1)S(1)}, bf16[512,768]{1,0:T(8,128)(2,1)S(1)}, u32[]{:S(2)}, u32[]{:S(2)}) collective-permute-start(bf16[512,768]{1,0:T(8,128)(2,1)S(1)} %slice_bitcast_fusion), channel_id=1, source_target_pairs={{0,2},{2,4},{4,6},{6,0},{1,3},{3,5},{5,7},{7,1},{8,10},{10,12},{12... | collective-permute-start | bytes 2359304 | tf_op jit(solution)/shard_map/ppermute | solution.py:43
  496.0 20.5 %collective-permute-start.26 = (bf16[512,768]{1,0:T(8,128)(2,1)S(1)}, bf16[512,768]{1,0:T(8,128)(2,1)S(1)}, u32[]{:S(2)}, u32[]{:S(2)}) collective-permute-start(bf16[512,768]{1,0:T(8,128)(2,1)S(1)} %fusion.9), channel_id=1, source_target_pairs={{0,2},{2,4},{4,6},{6,0},{1,3},{3,5},{5,7},{7,1},{8,10},{10,12},{12... | collective-permute-start | bytes 2359304 | tf_op jit(solution)/shard_map/ppermute | solution.py:43
  516.7 19.6 %collective-permute-start.27 = (bf16[512,768]{1,0:T(8,128)(2,1)S(1)}, bf16[512,768]{1,0:T(8,128)(2,1)S(1)}, u32[]{:S(2)}, u32[]{:S(2)}) collective-permute-start(bf16[512,768]{1,0:T(8,128)(2,1)S(1)} %fusion.8), channel_id=1, source_target_pairs={{0,2},{2,4},{4,6},{6,0},{1,3},{3,5},{5,7},{7,1},{8,10},{10,12},{12... | collective-permute-start | bytes 2359304 | tf_op jit(solution)/shard_map/ppermute | solution.py:43
  523.8 44.0 %collective-permute-start.28 = (bf16[512,2048]{1,0:T(8,128)(2,1)}, bf16[512,2048]{1,0:T(8,128)(2,1)}, u32[]{:S(2)}, u32[]{:S(2)}) collective-permute-start(bf16[512,2048]{1,0:T(8,128)(2,1)} %shard_map.304), channel_id=1, source_target_pairs={{0,8},{8,0},{1,9},{9,1},{2,10},{10,2},{3,11},{11,3},{4,12},{12,4},... | collective-permute-start | bytes 6291464 | tf_op jit(solution)/shard_map/ppermute | solution.py:43
  555.0 53.7 %all-to-all-start.4 = ((bf16[8,64,2048]{2,1,0:T(8,128)(2,1)}), bf16[8,64,2048]{2,1,0:T(8,128)(2,1)S(1)}, u32[]{:S(2)}, u32[]{:S(2)}) async-start(bf16[8,64,2048]{2,1,0:T(8,128)(2,1)} %bitcast.239), calls=%async_computation.6 | async-start | bytes 4194304 | tf_op jit(solution)/shard_map/all_to_all | solution.py:55
  572.8 43.9 %collective-permute-start.29 = (bf16[128,2048]{1,0:T(8,128)(2,1)}, bf16[128,2048]{1,0:T(8,128)(2,1)}, u32[]{:S(2)}, u32[]{:S(2)}) collective-permute-start(bf16[128,2048]{1,0:T(8,128)(2,1)} %get-tuple-element.222), channel_id=1, source_target_pairs={{0,16},{16,1},{1,17},{17,0},{2,18},{18,3},{3,19},{19,2},{4,20},{20... | collective-permute-start | bytes 1572872 | tf_op jit(solution)/shard_map/ppermute | solution.py:43
  574.3 42.4 %collective-permute-start.31 = (bf16[128,2048]{1,0:T(8,128)(2,1)}, bf16[128,2048]{1,0:T(8,128)(2,1)}, u32[]{:S(2)}, u32[]{:S(2)}) collective-permute-start(bf16[128,2048]{1,0:T(8,128)(2,1)} %get-tuple-element.223), channel_id=1, source_target_pairs={{0,17},{16,0},{1,16},{17,1},{2,19},{18,2},{3,18},{19,3},{4,21},{20... | collective-permute-start | bytes 1572872 | tf_op jit(solution)/shard_map/ppermute | solution.py:43
  575.9 40.8 %collective-permute-start.30 = (bf16[128,2048]{1,0:T(8,128)(2,1)}, bf16[128,2048]{1,0:T(8,128)(2,1)}, u32[]{:S(2)}, u32[]{:S(2)}) collective-permute-start(bf16[128,2048]{1,0:T(8,128)(2,1)} %get-tuple-element.224), channel_id=1, source_target_pairs={{0,1},{16,17},{1,0},{17,16},{2,3},{18,19},{3,2},{19,18},{4,5},{20,... | collective-permute-start | bytes 1572872 | tf_op jit(solution)/shard_map/ppermute | solution.py:43
  612.4 23.5 %all-to-all-start.5 = ((bf16[8,3,64,256]{3,2,1,0:T(8,128)(2,1)}), bf16[8,3,64,256]{3,2,1,0:T(8,128)(2,1)}, u32[]{:S(2)}, u32[]{:S(2)}) async-start(bf16[8,3,64,256]{3,2,1,0:T(8,128)(2,1)} %bitcast.230), calls=%async_computation.7 | async-start | bytes 1572864 | tf_op jit(solution)/shard_map/all_to_all | solution.py:55
  636.7 38.9 %all-to-all-start.6 = ((f32[32,1,320]{2,1,0:T(1,128)}), f32[32,1,320]{2,1,0:T(1,128)S(1)}, u32[]{:S(2)}, u32[]{:S(2)}) async-start(f32[32,1,320]{2,1,0:T(1,128)} %reshape.412), calls=%async_computation.9 | async-start | bytes 98304 | tf_op jit(solution)/shard_map/all_to_all | solution.py:55
  681.1 16.5 %all-to-all-start.7 = ((f32[32,8,2,128]{3,1,2,0:T(8,128)}), f32[32,8,2,128]{3,1,2,0:T(8,128)S(1)}, u32[]{:S(2)}, u32[]{:S(2)}) async-start(f32[32,8,2,128]{3,1,2,0:T(8,128)} %broadcast_in_dim.69), calls=%async_computation.10 | async-start | bytes 524288 | tf_op jit(solution)/shard_map/all_to_all | solution.py:55
  (43 other events, 409.1 us)
Sparse Core Ops, SparseCore 0:
  9.6 72.3 all-gather.4
  84.4 52.1 all-gather.10
  139.0 52.6 all-gather.6
  210.6 67.9 all-gather.8
  341.7 58.0 reduce-scatter.12
  402.5 53.6 reduce-scatter.6
  459.2 95.7 reduce-scatter.8
  558.2 82.7 reduce-scatter.10

commit v3 on v2

--- a/solution.py
+++ b/solution.py
@@ -113,13 +113,57 @@
     return (new_first, new_second, direction)
 
 
-def feed_kernel(h_ref, e_ref, g_ref, u_ref, d_ref, hid_ref, dg_ref, du_ref):
+def assembled_kernel(me_ref, *refs):
+    out_ref, n = refs[-1], len(refs) - 1
+    for k in range(n):
+        out_ref[pl.ds((me_ref[0] + k) % n, 1)] = refs[k][...][None]
+
+
+def assembled(me, pieces):
+    rows, cols = pieces[0].shape
+    n = len(pieces)
+    out = pl.pallas_call(
+        assembled_kernel,
+        in_specs=[pl.BlockSpec(memory_space=pltpu.SMEM)]
+        + [pl.BlockSpec(memory_space=pltpu.VMEM) for _ in pieces],
+        out_specs=pl.BlockSpec(memory_space=pltpu.VMEM),
+        out_shape=jax.ShapeDtypeStruct((n, rows, cols), LOW),
+        compiler_params=pltpu.CompilerParams(vmem_limit_bytes=ROOM),
+        cost_estimate=SHORT,
+    )(me.reshape(1).astype(jnp.int32), *pieces)
+    return out.reshape(n * rows, cols)
+
+
+def interleaved_kernel(place_ref, mine_ref, other_ref, out_ref):
+    out_ref[0, pl.ds(place_ref[1], 1)] = mine_ref[...][None]
+    out_ref[0, pl.ds(1 - place_ref[1], 1)] = other_ref[...][None]
+
+
+def interleaved(place, mine, other, own):
+    n, cols = mine.shape[0] // own, mine.shape[1]
+    block = pl.BlockSpec((own, cols), lambda i, p: (i, 0))
+    return pl.pallas_call(
+        interleaved_kernel,
+        grid_spec=pltpu.PrefetchScalarGridSpec(
+            num_scalar_prefetch=1,
+            grid=(n,),
+            in_specs=[block, block],
+            out_specs=pl.BlockSpec((1, 2, own, cols), lambda i, p: ((p[0] + i) % n, 0, 0, 0)),
+        ),
+        out_shape=jax.ShapeDtypeStruct((n, 2, own, cols), mine.dtype),
+        compiler_params=pltpu.CompilerParams(vmem_limit_bytes=ROOM),
+        cost_estimate=SHORT,
+    )(place.astype(jnp.int32), mine, other)
+
+
+def feed_kernel(c_ref, h_ref, e_ref, g_ref, u_ref, d_ref, hid_ref, dg_ref, du_ref):
     step = 256
+    grads = e_ref[...].reshape(h_ref.shape)
     for j in range(h_ref.shape[0] // step):
         at = slice(j * step, (j + 1) * step)
         gate = times(h_ref[at, :], g_ref[...])
         up = times(h_ref[at, :], u_ref[...])
-        d_hidden = times_wide(e_ref[at, :], d_ref[...])
+        d_hidden = times_wide(grads[at, :], d_ref[...])
         sig = jax.nn.sigmoid(gate)
         activated = gate * sig
         hid_ref[at, :] = (activated * up).astype(LOW)
@@ -127,26 +171,62 @@
         du_ref[at, :] = (d_hidden * activated).astype(LOW)
 
 
-def feed(h, e, gate, up, down):
+def feed(core, h, e, gate, up, down):
     count, features = h.shape[0], down.shape[0]
     tile = 256
-    whole = pl.BlockSpec((count, D), lambda i: (0, 0), pipeline_mode=pl.Buffered(1))
-    made = pl.BlockSpec((count, tile), lambda i: (0, i))
+    made = pl.BlockSpec((count, tile), lambda i, c: (0, i))
     return pl.pallas_call(
         feed_kernel,
-        grid=(features // tile,),
-        in_specs=[
-            whole,
-            whole,
-            pl.BlockSpec((D, tile), lambda i: (0, i)),
-            pl.BlockSpec((D, tile), lambda i: (0, i)),
-            pl.BlockSpec((tile, D), lambda i: (i, 0)),
-        ],
-        out_specs=[made] * 3,
+        grid_spec=pltpu.PrefetchScalarGridSpec(
+            num_scalar_prefetch=1,
+            grid=(features // tile,),
+            in_specs=[
+                pl.BlockSpec((count, D), lambda i, c: (0, 0), pipeline_mode=pl.Buffered(1)),
+                pl.BlockSpec(
+                    (e.shape[0], 1) + e.shape[2:],
+                    lambda i, c: (0, c[0], 0, 0),
+                    pipeline_mode=pl.Buffered(1),
+                ),
+                pl.BlockSpec((D, tile), lambda i, c: (0, i)),
+                pl.BlockSpec((D, tile), lambda i, c: (0, i)),
+                pl.BlockSpec((tile, D), lambda i, c: (i, 0)),
+            ],
+            out_specs=[made] * 3,
+        ),
         out_shape=[jax.ShapeDtypeStruct((count, features), LOW)] * 3,
         compiler_params=pltpu.CompilerParams(vmem_limit_bytes=ROOM),
         cost_estimate=SHORT,
-    )(h, e, gate, up, down)
+    )(core, h, e, gate, up, down)
+
+
+def down_kernel(c_ref, mine_ref, other_ref, mine_e_ref, other_e_ref, out_ref):
+    rows = mine_ref.shape[0]
+    total = over_tokens(mine_ref[...], mine_e_ref[...].reshape(rows, -1))
+    total += over_tokens(other_ref[...], other_e_ref[...].reshape(rows, -1))
+    out_ref[...] = total.astype(out_ref.dtype)
+
+
+def down_grads(core, mine, other, e):
+    count, features = mine.shape
+    tile = 512
+    side = (e.shape[0], 1) + e.shape[2:]
+    return pl.pallas_call(
+        down_kernel,
+        grid_spec=pltpu.PrefetchScalarGridSpec(
+            num_scalar_prefetch=1,
+            grid=(features // tile,),
+            in_specs=[
+                pl.BlockSpec((count, tile), lambda i, c: (0, i)),
+                pl.BlockSpec((count, tile), lambda i, c: (0, i)),
+                pl.BlockSpec(side, lambda i, c: (0, c[0], 0, 0), pipeline_mode=pl.Buffered(1)),
+                pl.BlockSpec(side, lambda i, c: (0, 1 - c[0], 0, 0), pipeline_mode=pl.Buffered(1)),
+            ],
+            out_specs=pl.BlockSpec((tile, D), lambda i, c: (i, 0)),
+        ),
+        out_shape=jax.ShapeDtypeStruct((features, D), LOW),
+        compiler_params=pltpu.CompilerParams(vmem_limit_bytes=ROOM),
+        cost_estimate=SHORT,
+    )(core, mine, other, e, e)
 
 
 def back_kernel(pairs, *refs):
@@ -355,7 +435,7 @@
 
 
 def adam_plain_kernel(w_ref, m_ref, v_ref, g_ref, *refs):
-    adam_step(pl.program_id(1) == 0, g_ref[...], w_ref, m_ref, v_ref, *refs[-5:])
+    adam_step(pl.program_id(1) == 0, g_ref[...].astype(WIDE), w_ref, m_ref, v_ref, *refs[-5:])
 
 
 def adam_columns(w, m, v, grad, first, kinds, done=()):
@@ -405,7 +485,7 @@
     adam_step(pl.program_id(0) == 0, grad, w_ref, m_ref, v_ref, *refs[-5:])
 
 
-def adam_first(sizes, w, m, v, got):
+def adam_first(sizes, w, m, v, got, done=()):
     rows = w.shape[0]
     column = pl.BlockSpec((rows, D), lambda i: (0, i))
     like = jax.ShapeDtypeStruct(w.shape, WIDE)
@@ -413,35 +493,34 @@
         functools.partial(adam_first_kernel, sizes),
         grid=(3,),
         in_specs=[column] * 3
-        + [pl.BlockSpec((got.shape[0], 1) + got.shape[2:], lambda i: (0, i, 0, 0))],
+        + [pl.BlockSpec((got.shape[0], 1) + got.shape[2:], lambda i: (0, i, 0, 0))]
+        + [pl.BlockSpec(memory_space=pl.ANY) for _ in done],
         out_specs=[column] * 4 + [pl.BlockSpec((1, 2, 8, 128), lambda i: (0, 0, 0, 0))],
         out_shape=[like] * 4 + [jax.ShapeDtypeStruct((1, 2, 8, 128), WIDE)],
-        compiler_params=pltpu.CompilerParams(vmem_limit_bytes=ROOM),
-        cost_estimate=SHORT,
-    )(w, m, v, got)
-
-
-def step_kernel(ratio_ref, w_ref, dir_ref, *refs):
-    refs[-1][...] = w_ref[...] + dir_ref[...] * ratio_ref[pl.program_id(0)]
-
-
-def stepped(ratio, w, direction, first, kinds, blocks, width, done=None):
-    rows = w.shape[0]
-    column = pl.BlockSpec((rows, width), lambda k, b, r: (0, first + k * blocks + b))
-    more = () if done is None else (done,)
+        input_output_aliases={4 + k: k for k in range(len(done))},
+        compiler_params=pltpu.CompilerParams(vmem_limit_bytes=ROOM),
+        cost_estimate=SHORT,
+    )(w, m, v, got, *done)
+
+
+def step_kernel(ratio_ref, w_ref, dir_ref, out_ref):
+    block = pl.program_id(0)
+    piece = jnp.where(block < 3, 0, jnp.where(block < 4, 1, jnp.where(block < 4 + FF // D, 2, 3)))
+    out_ref[...] = w_ref[...] + dir_ref[...] * ratio_ref[piece]
+
+
+def stepped(ratio, w, direction):
+    rows, cols = w.shape
+    column = pl.BlockSpec((rows, D), lambda b, r: (0, b))
     return pl.pallas_call(
         step_kernel,
         grid_spec=pltpu.PrefetchScalarGridSpec(
-            num_scalar_prefetch=1,
-            grid=(kinds, blocks),
-            in_specs=[column] * 2 + [pl.BlockSpec(memory_space=pl.ANY) for _ in more],
-            out_specs=column,
+            num_scalar_prefetch=1, grid=(cols // D,), in_specs=[column] * 2, out_specs=column
         ),
         out_shape=jax.ShapeDtypeStruct(w.shape, WIDE),
-        input_output_aliases={3: 0} if more else {},
-        compiler_params=pltpu.CompilerParams(vmem_limit_bytes=ROOM),
-        cost_estimate=SHORT,
-    )(ratio, w, direction, *more)
+        compiler_params=pltpu.CompilerParams(vmem_limit_bytes=ROOM),
+        cost_estimate=SHORT,
+    )(ratio, w, direction)
 
 
 def local(
@@ -522,7 +601,7 @@
         [norm_gains.reshape(-1), conv_taps.reshape(-1), segments.reshape(-1).astype(WIDE)]
     )
     low_o = w_in[:, 3 * D : 4 * D].astype(LOW)
-    notes, p_cols = tied(spread_to(note, AXES), prep_conv(sizes, w_in))
+    notes, p_cols, low_o = tied(spread_to(note, AXES), prep_conv(sizes, w_in), low_o)
     o_pieces = [low_o] + near(low_o, "h")
     notes = notes.reshape(sizes + (-1,))
     gains = notes[..., : 2 * rows].reshape(D, 2).astype(LOW).astype(WIDE)
@@ -537,28 +616,31 @@
 
     grad_low = out_grad.reshape(own, D)
     grad_top = grad_low.astype(WIDE)
-    e_all = lax.all_gather(grad_low, FEED, axis=0)
     down = lax.all_gather(w_down.astype(LOW), FEED_COPIES, axis=0, tiled=True)
     values = inputs.reshape(own, D).astype(WIDE)
     norm_one, scale_one = norm_forward(values, gain_one)
     low_one = conv_order(norm_one.astype(LOW))
-    mine, other = with_core([low_one] + near(low_one, LINES))
-    cols_p, gate_cols, *o_pieces = tied(
-        exchanged(p_cols, CONV), prep_feed(sizes, w_in, 4 * D), *o_pieces
+    cols_p, gate_cols, low_one, *o_pieces = tied(
+        exchanged(p_cols, CONV), prep_feed(sizes, w_in, 4 * D), low_one, *o_pieces
     )
-    gate_cols, cols_p, mine, other = tied(exchanged(gate_cols, FEED), cols_p, mine, other)
+    h_pieces = [low_one] + near(low_one, LINES)
+    gate_cols, up_cols, cols_p, down, h_pieces[1] = tied(
+        exchanged(gate_cols, FEED), prep_feed(sizes, w_in, 4 * D + FF), cols_p, down, h_pieces[1]
+    )
+    mine, other = with_core(h_pieces)
     gate_w = lax.all_gather(as_rows(gate_cols), FEED_COPIES, axis=0, tiled=True)
+    up_cols, cols_p = tied(exchanged(up_cols, FEED), cols_p)
+    up_w = lax.all_gather(as_rows(up_cols), FEED_COPIES, axis=0, tiled=True)
     o_w = placed(o_pieces, "h").reshape(channels, D)
-    pieces = ring(cols_p.swapaxes(1, 2).reshape(-1, 3 * channels), "h")
-    pieces[-1], up_cols = tied(pieces[-1], prep_feed(sizes, w_in, 4 * D + FF))
-    up_cols = exchanged(up_cols, FEED)
+    pieces = [cols_p.swapaxes(1, 2).reshape(-1, 3 * channels)]
+    for k in range(1, nh):
+        piece = turned(pieces[-1], "h", -1)
+        pieces.append(piece)
+    pieces[-1], gate_w = tied(pieces[-1], gate_w)
     p_w = jnp.concatenate(pieces, 0)
 
-    h_one = jnp.zeros((ny * nl, nc, own, D), LOW)
-    for k, part in enumerate((mine, other)):
-        part = rolled(part.reshape(-1, 1, own, D), LINES, 0, -1)
-        h_one = lax.dynamic_update_slice(h_one, part, (0, (ci + k) % nc, 0, 0))
-    h_one = h_one.reshape(conv_total, D)
+    line = li * ny + yi
+    h_one = interleaved(jnp.stack([line, ci]), mine, other, own).reshape(conv_total, D)
     bcx = times(h_one, p_w).reshape(nl, span, 3 * channels)
     b_part = bcx[:, :, :channels]
     c_part = bcx[:, :, channels : 2 * channels]
@@ -580,21 +662,18 @@
 
     y_mine, y_other = by_core(y_mix)
     both, sent = scatter(times(y_other, o_w).astype(LOW), lambda: times(y_mine, o_w), LINES)
-    both, up_cols = tied(both, up_cols)
-    up_w = lax.all_gather(as_rows(up_cols), FEED_COPIES, axis=0, tiled=True)
-    *sent, e_all = tied(*sent, e_all)
+    both, up_w, grad_low = tied(both, up_w, grad_low)
+    e_all = lax.all_gather(grad_low, FEED, axis=0)
     middle = values + total(both, sent)
-    e_all = e_all.reshape(nh, nc, own, D)
-    e_mine, e_other = (picked(e_all, (ci + k) % nc, 1).reshape(-1, D) for k in range(nc))
 
     norm_two, scale_two = norm_forward(middle, gain_two)
     low_two = feed_order(norm_two.astype(LOW))
-    h_mine = placed([low_two] + near(low_two, "h"), "h").reshape(-1, D)
+    h_mine = assembled(hi, [low_two] + near(low_two, "h"))
     h_other = turned(h_mine, "c", 1)
-    hid_mine, dg_mine, du_mine = feed(h_mine, e_mine, gate_w, up_w, down)
-    hid_other, dg_other, du_other = feed(h_other, e_other, gate_w, up_w, down)
+    e_all = e_all.reshape(nh, nc, own, D)
     core = ci.reshape(1).astype(jnp.int32)
-
+    hid_mine, dg_mine, du_mine = feed(core, h_mine, e_all, gate_w, up_w, down)
+    hid_other, dg_other, du_other = feed(1 - core, h_other, e_all, gate_w, up_w, down)
     def summed(part, axes):
         return lax.psum_scatter(part, axes, scatter_dimension=0, tiled=True)
 
@@ -603,7 +682,7 @@
     d_h_two = summed(d_h_two.reshape(-1, D), FEED).astype(WIDE)
     part_feed = weight_grads([h_mine, h_other], [[dg_mine, du_mine], [dg_other, du_other]])
     part_feed, hid_mine = tied(part_feed, hid_mine)
-    part_down = weight_grads([hid_mine, hid_other], [[e_mine], [e_other]])
+    part_down = down_grads(core, hid_mine, hid_other, e_all)
     out_part = both_cores(core, [hid_mine], [hid_other], [down], own, False)
     d_h_two, part_down, part_feed, out_part = tied(d_h_two, part_down, part_feed, out_part)
     out_sum = summed(out_part.reshape(-1, D), FEED)
@@ -616,7 +695,7 @@
     got_feed = summed(part_feed, FEED_COPIES)
     part_o = over_tokens(y_mine, do_mine) + over_tokens(y_other, do_other)
     part_o = rolled(part_o.reshape(nh, rows, D), "h", 0, 1)
-    sent_o = [turned(part_o[k].astype(LOW), "h", k) for k in range(1, nh)]
+    part_o = part_o.astype(LOW)
     d_mix = jnp.zeros((ny * nl, nc, own, channels), WIDE)
     for k, part in enumerate((do_mine, do_other)):
         part = rolled(times_wide(part, o_w).reshape(-1, 1, own, channels), LINES, 0, -1)
@@ -634,17 +713,30 @@
     d_bcx = jnp.concatenate([d_mixed_in * x_part, d_c, d_mixed_in * b_part], 2).astype(LOW)
 
     part_p = weight_grads([h_one], [[d_bcx.reshape(conv_total, -1)]]).reshape(nh, -1, 3 * channels)
-    part_p, d_bcx, part_down, out_sum, *sent_o = tied(part_p, d_bcx, part_down, out_sum, *sent_o)
-    grad_o = total(part_o[0], sent_o)
+    part_p, part_o, d_bcx, part_down, out_sum = tied(part_p, part_o, d_bcx, part_down, out_sum)
     grad_down = summed(part_down, FEED_COPIES)
-    part_p = ring_sum(list(part_p), "h").astype(LOW)
     db_mine, db_other = by_core(d_bcx)
-    other = back([db_other], p_w, LOW)
-    other, db_mine = tied(other, db_mine)
-    both, sent = scatter(other, lambda: back([db_mine], p_w, WIDE), LINES)
+    pass_p, pass_o = part_p[nh - 1], part_o[nh - 1]
+    for k in range(nh - 2, -1, -1):
+        pass_p, pass_o = turned(pass_p, "h", 1), turned(pass_o, "h", 1)
+        if k == nh - 2:
+            other = back([db_other], p_w, LOW)
+            other, db_mine = tied(other, db_mine)
+            both, sent = scatter(other, lambda: back([db_mine], p_w, WIDE), LINES)
+            pass_p, pass_o, both = tied(pass_p, pass_o, both)
+        if k == 0:
+            pass_p, pass_o = tied(pass_p, pass_o)
+        pass_p = pass_p.astype(WIDE) + part_p[k].astype(WIDE)
+        pass_o = pass_o.astype(WIDE) + part_o[k].astype(WIDE)
+        if k:
+            pass_p, pass_o = pass_p.astype(LOW), pass_o.astype(LOW)
+    grad_o = pass_o
+    part_p = pass_p.astype(LOW).reshape(ny * nc * nl, rows, 3, channels).swapaxes(1, 2)
     got_feed, part_p = tied(got_feed, part_p)
-    got_feed, part_p, both = tied(exchanged(got_feed.reshape(nh * nc, rows, -1), FEED), part_p, both)
-    got_p = exchanged(part_p.reshape(ny * nc * nl, rows, 3, channels).swapaxes(1, 2), CONV)
+    got_feed = exchanged(got_feed.reshape(nh * nc, rows, -1), FEED)
+    *done, sums_o = adam_columns(w_in, m_in, v_in, grad_o, 3 * D, 1)
+    got_feed, part_p, sums_o = tied(got_feed, part_p, sums_o)
+    got_p, *sent = tied(exchanged(part_p, CONV), *sent)
     d_h_one = total(both, sent)
     d_values, d_gain_one = norm_backward(values, scale_one, gain_one, from_conv_order(d_h_one))
     input_grad = (d_values + d_middle).reshape(inputs.shape)
@@ -655,14 +747,11 @@
     )
     gain_terms = jnp.stack([d_gain_one, d_gain_two], 1).reshape(sizes + (rows, 2))
     terms = jnp.concatenate([tap_terms, gain_terms], -1).reshape(-1, rows, TAPS + 2)
-    got_p, terms = tied(got_p, terms)
     terms = exchanged(terms, AXES)
-    *done, sums_p = adam_first(sizes, w_in, m_in, v_in, got_p)
-    *done, sums_o = adam_columns(w_in, m_in, v_in, grad_o, 3 * D, 1, done)
     *done, sums_gate = adam_gate(sizes, w_in, m_in, v_in, got_feed, 0, done)
     *done, sums_up = adam_gate(sizes, w_in, m_in, v_in, got_feed, 1, done)
+    *done, sums_p = adam_first(sizes, w_in, m_in, v_in, got_p, done)
     grad_down, sums_up = tied(grad_down, sums_up)
-    grad_down = grad_down.astype(WIDE)
     grad_down, new_m_down, new_v_down, dir_down, sums_down = adam_down(w_down, m_down, v_down, grad_down)
     grad_in, new_m_in, new_v_in, dir_in = done
     block_out = (middle + out_sum.astype(WIDE)).astype(LOW).reshape(inputs.shape)
@@ -688,11 +777,8 @@
     )
     lamb_norms = jnp.sqrt(jnp.sum(spread_to(sums, AXES), axis=(0, 3)).T)
     ratio = -RATE * lamb_norms[0] / (lamb_norms[1] + 1e-06)
-    width = 2048
+    new_w_in = stepped(ratio[:4], w_in, dir_in)
     new_w_down = w_down + dir_down * ratio[4]
-    new_w_in = stepped(ratio[:1], w_in, dir_in, 0, 1, 3 * D // width, width)
-    new_w_in = stepped(ratio[1:2], w_in, dir_in, 3 * D // width, 1, D // width, width, new_w_in)
-    new_w_in = stepped(ratio[2:4], w_in, dir_in, 4 * D // width, 2, FF // width, width, new_w_in)
     new_w_taps = conv_taps + dir_taps * ratio[5]
     new_w_gains = norm_gains + dir_gains * ratio[6:][None, :]
     return (

time: 736 us -> 698 us (0.948)
  waiting for transfers between devices: 350 us -> 332 us
  local copies, waits for them, and re-layouts: 58 us -> 47 us
  other arithmetic: 50.8 us -> 41.2 us
  starting transfers between devices: 89 us -> 81 us
    all_to_all x8, waiting for transfers between devices: 95.7 us -> 54.8 us  [exchanged(): return lax.all_to_all(value, axes, 0, 0, tiled=True)]
    ppermute x32, waiting for transfers between devices: 211 us -> 251 us  [turned(): return lax.ppermute(value, ordered if len(names) > 1 else axes, pairs)]
    reduce_scatter x3, waiting for transfers between devices: 17.7 us -> 0.01 us  [summed(): return lax.psum_scatter(part, axes, scatter_dimension=0, tiled=True)]
    pallas_call x2 -> x5, Pallas kernels: 24.5 us -> 41 us  [the longest x2 23.8 us: feed(): pl.pallas_call(feed_kernel, grid_spec=pltpu.PrefetchScalarGridSpec(num_sc...]
    all_to_all x8, starting transfers between devices: 48.8 us -> 35.5 us  [exchanged(): return lax.all_to_all(value, axes, 0, 0, tiled=True)]
    unnamed x9, waiting for transfers between devices: 25.7 us -> 15.3 us
    all_gather x1, waiting for transfers between devices: 0.02 us -> 10.1 us  [local(): up_w = lax.all_gather(as_rows(up_cols), FEED_COPIES, axis=0, tiled=True)]
    pallas_call x3 -> x2, Pallas kernels: 29.7 us -> 20.8 us  [weight_grads(): pl.pallas_call(functools.partial(weight_kernel, parts, outs), grid=(rows...]
  transfers between devices with their start and end apart: 48 -> 48, of which waited for: 29 -> 27; matrix products, arithmetic and copies ran while one was open for 15% -> 12% of each run, Pallas kernels for 14% -> 16%
where the time goes in v3:
time: 698 us; the launch traced here: 688 us
  waiting for transfers between devices  332 us (48%)
  Pallas kernels  152 us (22%)
  starting transfers between devices  81 us (12%)
  local copies, waits for them, and re-layouts  47 us (7%)
  other arithmetic  41.2 us (6%)
  matrix products  19.5 us (3%)
  between operations  15.7 us (2%)
    ppermute x32, waiting for transfers between devices, turned(): return lax.ppermute(value, ordered if len(names) > 1 else axes, pairs)  251 us
    all_to_all x8, waiting for transfers between devices, exchanged(): return lax.all_to_all(value, axes, 0, 0, tiled=True)  54.8 us
    ppermute x32, starting transfers between devices, turned(): return lax.ppermute(value, ordered if len(names) > 1 else axes, pairs)  45 us
    all_to_all x8, starting transfers between devices, exchanged(): return lax.all_to_all(value, axes, 0, 0, tiled=True)  35.5 us
    pallas_call x2, Pallas kernels, both_cores(): pl.pallas_call(functools.partial(both_kernel, len(mine), wide), grid_spec...  26.5 us
    pallas_call x2, Pallas kernels, feed(): pl.pallas_call(feed_kernel, grid_spec=pltpu.PrefetchScalarGridSpec(num_sc...  23.8 us
    pallas_call x2, Pallas kernels, weight_grads(): pl.pallas_call(functools.partial(weight_kernel, parts, outs), grid=(rows...  20.8 us
    unnamed x9, waiting for transfers between devices  15.3 us
  transfers between devices with their start and end apart: 48, of which 27 were waited for; matrix products, arithmetic and copies ran while one was open for 12% of the time, Pallas kernels for 16%

profile of v3, /device:TPU:0, one launch (start us, length us, event | category | flops | bytes accessed | tf_op | source)
XLA Modules:
  0.0 688.5 jit_solution(6837809698831339497)
XLA Ops:
  11.3 7.3 %all-to-all-start = ((f32[32,1,448]{2,1,0:T(1,128)}), f32[32,1,448]{2,1,0:T(1,128)S(1)}, u32[]{:S(2)}, u32[]{:S(2)}) async-start(f32[32,1,448]{2,1,0:T(1,128)} %broadcast_in_dim.18), calls=%async_computation | async-start | bytes 131072 | tf_op jit(solution)/shard_map/all_to_all | solution.py:55
  27.8 3.7 collective-permute-start
  32.6 3.7 all-to-all-start.1
  39.7 14.9 %collective-permute-done.1 = bf16[64,2048]{1,0:T(8,128)(2,1)} collective-permute-done((bf16[64,2048]{1,0:T(8,128)(2,1)}, bf16[64,2048]{1,0:T(8,128)(2,1)}, u32[]{:S(2)}, u32[]{:S(2)}) %collective-permute-start.1) | collective-permute-done | bytes 262176 | tf_op jit(solution)/shard_map/ppermute | solution.py:43
  54.6 4.0 all-to-all-start.2
  63.4 18.1 %collective-permute-done.3 = bf16[128,2048]{1,0:T(8,128)(2,1)S(1)} collective-permute-done((bf16[128,2048]{1,0:T(8,128)(2,1)S(1)}, bf16[128,2048]{1,0:T(8,128)(2,1)S(1)}, u32[]{:S(2)}, u32[]{:S(2)}) %collective-permute-start.3) | collective-permute-done | bytes 524320 | tf_op jit(solution)/shard_map/ppermute | solution.py:43
  95.6 19.3 %collective-permute-done.4 = bf16[128,2048]{1,0:T(8,128)(2,1)} collective-permute-done((bf16[128,2048]{1,0:T(8,128)(2,1)S(1)}, bf16[128,2048]{1,0:T(8,128)(2,1)}, u32[]{:S(2)}, u32[]{:S(2)}) %collective-permute-start.4) | collective-permute-done | bytes 524320 | tf_op jit(solution)/shard_map/ppermute | solution.py:43
  117.6 3.7 collective-permute-start.7
  121.2 9.0 %collective-permute-done.5 = bf16[128,2048]{1,0:T(8,128)(2,1)} collective-permute-done((bf16[128,2048]{1,0:T(8,128)(2,1)S(1)}, bf16[128,2048]{1,0:T(8,128)(2,1)}, u32[]{:S(2)}, u32[]{:S(2)}) %collective-permute-start.5) | collective-permute-done | bytes 524320 | tf_op jit(solution)/shard_map/ppermute | solution.py:43
  136.3 4.0 collective-permute-start.8
  143.6 13.0 %collective-permute-done.8 = bf16[512,768]{1,0:T(8,128)(2,1)S(1)} collective-permute-done((bf16[512,768]{1,0:T(8,128)(2,1)S(1)}, bf16[512,768]{1,0:T(8,128)(2,1)S(1)}, u32[]{:S(2)}, u32[]{:S(2)}) %collective-permute-start.8) | collective-permute-done | bytes 786464 | tf_op jit(solution)/shard_map/ppermute | solution.py:43
  156.6 4.7 collective-permute-start.9
  164.2 5.5 shard_map.297
  169.8 6.9 %collective-permute-done.9 = bf16[512,768]{1,0:T(8,128)(2,1)} collective-permute-done((bf16[512,768]{1,0:T(8,128)(2,1)S(1)}, bf16[512,768]{1,0:T(8,128)(2,1)}, u32[]{:S(2)}, u32[]{:S(2)}) %collective-permute-start.9) | collective-permute-done | bytes 786464 | tf_op jit(solution)/shard_map/ppermute | solution.py:43
  177.9 6.3 fusion
  188.7 4.1 collective-permute-done.10
  196.2 10.1 %all-gather.10.cloned.1.call-done.u_ref.refs_5_ = bf16[2048,1024]{1,0:T(8,128)(2,1)} async-done(((bf16[512,1024]{1,0:T(8,128)(2,1)}), bf16[2048,1024]{1,0:T(8,128)(2,1)}) %all-gather.10.cloned.1.call-update) | async-done | bytes 4194320 | tf_op jit(solution)/shard_map/all_gather | solution.py:633
  211.5 10.4 %collective-permute-done.13 = bf16[128,2048]{1,0:T(8,128)(2,1)S(1)} collective-permute-done((bf16[128,2048]{1,0:T(8,128)(2,1)S(1)}, bf16[128,2048]{1,0:T(8,128)(2,1)S(1)}, u32[]{:S(2)}, u32[]{:S(2)}) %collective-permute-start.13) | collective-permute-done | bytes 524320 | tf_op jit(solution)/shard_map/ppermute | solution.py:43
  221.9 11.9 %collective-permute-done.12 = bf16[128,2048]{1,0:T(8,128)(2,1)S(1)} collective-permute-done((bf16[128,2048]{1,0:T(8,128)(2,1)S(1)}, bf16[128,2048]{1,0:T(8,128)(2,1)S(1)}, u32[]{:S(2)}, u32[]{:S(2)}) %collective-permute-start.12) | collective-permute-done | bytes 524320 | tf_op jit(solution)/shard_map/ppermute | solution.py:43
  239.8 23.4 %collective-permute-done.14.refs_1_ = bf16[128,2048]{1,0:T(8,128)(2,1)S(1)} collective-permute-done((bf16[128,2048]{1,0:T(8,128)(2,1)S(1)}, bf16[128,2048]{1,0:T(8,128)(2,1)S(1)}, u32[]{:S(2)}, u32[]{:S(2)}) %collective-permute-start.14) | collective-permute-done | bytes 524320 | tf_op jit(solution)/shard_map/ppermute | solution.py:43
  263.2 35.1 %collective-permute-done.15.refs_2_ = bf16[128,2048]{1,0:T(8,128)(2,1)S(1)} collective-permute-done((bf16[128,2048]{1,0:T(8,128)(2,1)S(1)}, bf16[128,2048]{1,0:T(8,128)(2,1)S(1)}, u32[]{:S(2)}, u32[]{:S(2)}) %collective-permute-start.15) | collective-permute-done | bytes 524320 | tf_op jit(solution)/shard_map/ppermute | solution.py:43
  302.2 11.9 %shard_map.299 = (bf16[512,1024]{1,0:T(8,128)(2,1)}, bf16[512,1024]{1,0:T(8,128)(2,1)}, bf16[512,1024]{1,0:T(8,128)(2,1)}) custom-call(s32[1]{0:T(128)} %bitcast.2.c_ref, bf16[512,2048]{1,0:T(8,128)(2,1)} %bitcast.187, bf16[4,2,128,2048]{3,2,1,0:T(8,128)(2,1)} %bitcast.180, bf16[2048,1024]{1,0:T(8,128)(2,1)} %all-gather.8.cloned.1.call-done.g_ref.refs_4_, ...), custom_call_target="tpu_custom_call" | custom-call | flops 1024 | bytes 1024 | tf_op jit(solution)/shard_map/pallas_call | solution.py:178
  315.4 11.9 %shard_map.300 = (bf16[512,1024]{1,0:T(8,128)(2,1)}, bf16[512,1024]{1,0:T(8,128)(2,1)}, bf16[512,1024]{1,0:T(8,128)(2,1)}) custom-call(s32[1]{0:T(128)S(6)} %sub.9.c_ref, bf16[512,2048]{1,0:T(8,128)(2,1)} %copy-done.13, bf16[4,2,128,2048]{3,2,1,0:T(8,128)(2,1)} %bitcast.181, bf16[2048,1024]{1,0:T(8,128)(2,1)} %all-gather.8.cloned.1.call-done.g_ref.refs_4_, ...), custom_call_target="tpu_custom_call" | custom-call | flops 1024 | bytes 1024 | tf_op jit(solution)/shard_map/pallas_call | solution.py:178
  327.4 15.6 %shard_map.301 = bf16[4,2,128,2048]{3,2,1,0:T(8,128)(2,1)} custom-call(s32[1]{0:T(128)} %bitcast.2.c_ref, bf16[512,1024]{1,0:T(8,128)(2,1)} %get-tuple-element.128.refs_0_.refs_2_, bf16[512,1024]{1,0:T(8,128)(2,1)} %get-tuple-element.129.refs_1_.refs_3_, bf16[512,1024]{1,0:T(8,128)(2,1)} %get-tuple-element.130.refs_2_.refs_4_, ...), custom_call_target="tpu_custom_call" | custom-call | flops 1024 | bytes 1024 | tf_op jit(solution)/shard_map/pallas_call | solution.py:286
  343.2 13.5 %shard_map.302 = bf16[2048,2048]{1,0:T(8,128)(2,1)} custom-call(bf16[512,2048]{1,0:T(8,128)(2,1)} %bitcast.188, bf16[512,2048]{1,0:T(8,128)(2,1)} %copy-done.13, bf16[512,1024]{1,0:T(8,128)(2,1)} %get-tuple-element.128.refs_0_.refs_2_, bf16[512,1024]{1,0:T(8,128)(2,1)} %get-tuple-element.129.refs_1_.refs_3_, ...), custom_call_target="tpu_custom_call" | custom-call | flops 1024 | bytes 1024 | tf_op jit(solution)/shard_map/pallas_call | solution.py:322
  356.7 8.7 %shard_map.303 = bf16[1024,2048]{1,0:T(8,128)(2,1)} custom-call(s32[1]{0:T(128)} %bitcast.2.c_ref, bf16[512,1024]{1,0:T(8,128)(2,1)} %get-tuple-element.135.mine_ref.refs_0_, bf16[512,1024]{1,0:T(8,128)(2,1)} %get-tuple-element.136.other_ref.refs_1_, bf16[4,2,128,2048]{3,2,1,0:T(8,128)(2,1)} %bitcast.182, bf16[4,2,128,2048]{3,2,1,0:T(8,128)(2,1)} %bitcast.183), custom_call_target="tpu_custom_call" | custom-call | flops 1024 | bytes 1024 | tf_op jit(solution)/shard_map/pallas_call | solution.py:213
  365.4 10.9 %shard_map.304 = bf16[4,2,128,2048]{3,2,1,0:T(8,128)(2,1)} custom-call(s32[1]{0:T(128)} %bitcast.2.c_ref, bf16[512,1024]{1,0:T(8,128)(2,1)} %get-tuple-element.135.mine_ref.refs_0_, bf16[512,1024]{1,0:T(8,128)(2,1)} %get-tuple-element.136.other_ref.refs_1_, bf16[1024,2048]{1,0:T(8,128)(2,1)} %all-gather.6.cloned.1.call-done.d_ref.refs_2_), custom_call_target="tpu_custom_call" | custom-call | flops 1024 | bytes 1024 | tf_op jit(solution)/shard_map/pallas_call | solution.py:286
  376.3 15.2 %reduce-scatter.13.cloned.1.call-done = bf16[128,2048]{1,0:T(8,128)(2,1)} async-done(((bf16[1024,2048]{1,0:T(8,128)(2,1)}), bf16[128,2048]{1,0:T(8,128)(2,1)}) %reduce-scatter.13.cloned.1.call-update) | async-done | bytes 524304
  400.2 11.4 %collective-permute-done.20 = bf16[128,2048]{1,0:T(8,128)(2,1)S(1)} collective-permute-done((bf16[128,2048]{1,0:T(8,128)(2,1)S(1)}, bf16[128,2048]{1,0:T(8,128)(2,1)S(1)}, u32[]{:S(2)}, u32[]{:S(2)}) %collective-permute-start.20) | collective-permute-done | bytes 524320 | tf_op jit(solution)/shard_map/ppermute | solution.py:43
  412.2 7.3 %collective-permute-done.18 = bf16[128,2048]{1,0:T(8,128)(2,1)S(1)} collective-permute-done((bf16[128,2048]{1,0:T(8,128)(2,1)S(1)}, bf16[128,2048]{1,0:T(8,128)(2,1)S(1)}, u32[]{:S(2)}, u32[]{:S(2)}) %collective-permute-start.18) | collective-permute-done | bytes 524320 | tf_op jit(solution)/shard_map/ppermute | solution.py:43
  419.8 4.2 collective-permute-done.21
  432.6 7.3 %shard_map.305 = bf16[2048,768]{1,0:T(8,128)(2,1)} custom-call(bf16[1024,2048]{1,0:T(8,128)(2,1)} %bitcast.191, bf16[1024,768]{1,0:T(8,128)(2,1)} %pad_maximum_fusion.1.refs_1_), custom_call_target="tpu_custom_call" | custom-call | flops 1024 | bytes 1024 | tf_op jit(solution)/shard_map/pallas_call | solution.py:322
  447.6 5.5 shard_map.306
  457.8 5.7 shard_map.307
  463.6 5.5 fusion.35
  470.1 11.6 %collective-permute-done.23 = bf16[64,2048]{1,0:T(8,128)(2,1)S(1)} collective-permute-done((bf16[64,2048]{1,0:T(8,128)(2,1)S(1)}, bf16[64,2048]{1,0:T(8,128)(2,1)S(1)}, u32[]{:S(2)}, u32[]{:S(2)}) %collective-permute-start.23) | collective-permute-done | bytes 262176 | tf_op jit(solution)/shard_map/ppermute | solution.py:43
  484.6 20.9 %collective-permute-done.25 = bf16[512,768]{1,0:T(8,128)(2,1)S(1)} collective-permute-done((bf16[512,768]{1,0:T(8,128)(2,1)S(1)}, bf16[512,768]{1,0:T(8,128)(2,1)S(1)}, u32[]{:S(2)}, u32[]{:S(2)}) %collective-permute-start.25) | collective-permute-done | bytes 786464 | tf_op jit(solution)/shard_map/ppermute | solution.py:43
  505.8 5.3 collective-permute-done.27
  511.3 20.9 %collective-permute-done.28 = bf16[64,2048]{1,0:T(8,128)(2,1)S(1)} collective-permute-done((bf16[64,2048]{1,0:T(8,128)(2,1)S(1)}, bf16[64,2048]{1,0:T(8,128)(2,1)S(1)}, u32[]{:S(2)}, u32[]{:S(2)}) %collective-permute-start.28) | collective-permute-done | bytes 262176 | tf_op jit(solution)/shard_map/ppermute | solution.py:43
  544.3 42.0 %all-to-all-done.4 = bf16[8,64,2048]{2,1,0:T(8,128)(2,1)S(1)} async-done(((bf16[8,64,2048]{2,1,0:T(8,128)(2,1)}), bf16[8,64,2048]{2,1,0:T(8,128)(2,1)S(1)}, u32[]{:S(2)}, u32[]{:S(2)}) %all-to-all-start.4) | async-done | bytes 2097184 | tf_op jit(solution)/shard_map/all_to_all | solution.py:55
  586.3 4.2 all-to-all-start.5
  600.2 7.5 %shard_map.309 = (f32[64,24576]{1,0:T(8,128)}, f32[64,24576]{1,0:T(8,128)}, f32[64,24576]{1,0:T(8,128)}, f32[64,24576]{1,0:T(8,128)}, f32[1,2,8,128]{3,2,1,0:T(8,128)}) custom-call(f32[64,24576]{1,0:T(8,128)} %w_ref.17, f32[64,24576]{1,0:T(8,128)} %m_ref.8, ...), custom_call_target="tpu_custom_call", output_to_operand_aliasing={{0}: (4, {}), {1}: (5, {}), {2}: (6, {}), {3}: (7, {})} | custom-call | flops 1024 | bytes 1024 | tf_op jit(solution)/shard_map/pallas_call | solution.py:423
  607.7 7.5 %shard_map.310 = (f32[64,24576]{1,0:T(8,128)}, f32[64,24576]{1,0:T(8,128)}, f32[64,24576]{1,0:T(8,128)}, f32[64,24576]{1,0:T(8,128)}, f32[1,2,8,128]{3,2,1,0:T(8,128)}) custom-call(f32[64,24576]{1,0:T(8,128)} %w_ref.17, f32[64,24576]{1,0:T(8,128)} %m_ref.8, ...), custom_call_target="tpu_custom_call", output_to_operand_aliasing={{0}: (4, {}), {1}: (5, {}), {2}: (6, {}), {3}: (7, {})} | custom-call | flops 1024 | bytes 1024 | tf_op jit(solution)/shard_map/pallas_call | solution.py:423
  615.3 7.6 %shard_map.312 = (f32[256,2048]{1,0:T(8,128)}, f32[256,2048]{1,0:T(8,128)}, f32[256,2048]{1,0:T(8,128)}, f32[256,2048]{1,0:T(8,128)}, f32[1,2,8,128]{3,2,1,0:T(8,128)}) custom-call(f32[256,2048]{1,0:T(8,128)} %w_ref.16, f32[256,2048]{1,0:T(8,128)} %m_ref.9, f32[256,2048]{1,0:T(8,128)} %v_ref.9, bf16[256,2048]{1,0:T(8,128)(2,1)} %reduce-scatter.11.cloned.1.call-done.g_ref), custom_call_target="tpu_custom_call" | custom-call | flops 1024 | bytes 1024 | tf_op jit(solution)/shard_map/pallas_call | solution.py:465
  633.8 6.9 %shard_map.311 = (f32[64,24576]{1,0:T(8,128)}, f32[64,24576]{1,0:T(8,128)}, f32[64,24576]{1,0:T(8,128)}, f32[64,24576]{1,0:T(8,128)}, f32[1,2,8,128]{3,2,1,0:T(8,128)}) custom-call(f32[64,24576]{1,0:T(8,128)} %w_ref.17, f32[64,24576]{1,0:T(8,128)} %m_ref.8, ...), custom_call_target="tpu_custom_call", output_to_operand_aliasing={{0}: (4, {}), {1}: (5, {}), {2}: (6, {}), {3}: (7, {})} | custom-call | flops 1024 | bytes 1024 | tf_op jit(solution)/shard_map/pallas_call | solution.py:492
  647.0 5.8 all-to-all-start.7
  654.3 9.2 %all-to-all-done.7 = f32[32,8,2,128]{3,1,2,0:T(8,128)S(1)} async-done(((f32[32,8,2,128]{3,1,2,0:T(8,128)}), f32[32,8,2,128]{3,1,2,0:T(8,128)S(1)}, u32[]{:S(2)}, u32[]{:S(2)}) %all-to-all-start.7) | async-done | bytes 262176 | tf_op jit(solution)/shard_map/all_to_all | solution.py:55
  665.6 12.2 %shard_map.313 = f32[64,24576]{1,0:T(8,128)} custom-call(f32[4]{0:T(128)} %slice_bitcast_fusion.3.ratio_ref, f32[64,24576]{1,0:T(8,128)} %w_ref.17, f32[64,24576]{1,0:T(8,128)} %get-tuple-element.191.dir_ref), custom_call_target="tpu_custom_call" | custom-call | flops 1024 | bytes 1024 | tf_op jit(solution)/shard_map/pallas_call | solution.py:515
  (319 shorter events, 157.2 us)
Async XLA Ops:
  7.2 77.9 %all-gather.6.cloned.1.call-start = ((), (), s32[]{:S(2)}) async-start(), calls=%async_computation.12 | async-start | bytes 5242880 | tf_op jit(solution)/shard_map/all_gather | solution.py:619
  11.3 16.5 %all-to-all-start = ((f32[32,1,448]{2,1,0:T(1,128)}), f32[32,1,448]{2,1,0:T(1,128)S(1)}, u32[]{:S(2)}, u32[]{:S(2)}) async-start(f32[32,1,448]{2,1,0:T(1,128)} %broadcast_in_dim.18), calls=%async_computation | async-start | bytes 131072 | tf_op jit(solution)/shard_map/all_to_all | solution.py:55
  27.8 11.8 %collective-permute-start = (bf16[64,2048]{1,0:T(8,128)(2,1)}, bf16[64,2048]{1,0:T(8,128)(2,1)}, u32[]{:S(2)}, u32[]{:S(2)}) collective-permute-start(bf16[64,2048]{1,0:T(8,128)(2,1)} %slice.283), channel_id=1, source_target_pairs={{0,6},{2,0},{4,2},{6,4},{1,7},{3,1},{5,3},{7,5},{8,14},{10,8},{12,... | collective-permute-start | bytes 786440 | tf_op jit(solution)/shard_map/ppermute | solution.py:43
  31.5 23.1 %collective-permute-start.1 = (bf16[64,2048]{1,0:T(8,128)(2,1)}, bf16[64,2048]{1,0:T(8,128)(2,1)}, u32[]{:S(2)}, u32[]{:S(2)}) collective-permute-start(bf16[64,2048]{1,0:T(8,128)(2,1)} %slice.283), channel_id=1, source_target_pairs={{0,4},{2,6},{4,0},{6,2},{1,5},{3,7},{5,1},{7,3},{8,12},{10,14},{12... | collective-permute-start | bytes 786440 | tf_op jit(solution)/shard_map/ppermute | solution.py:43
  31.5 23.1 %collective-permute-start.2 = (bf16[64,2048]{1,0:T(8,128)(2,1)}, bf16[64,2048]{1,0:T(8,128)(2,1)}, u32[]{:S(2)}, u32[]{:S(2)}) collective-permute-start(bf16[64,2048]{1,0:T(8,128)(2,1)} %slice.283), channel_id=1, source_target_pairs={{0,2},{2,4},{4,6},{6,0},{1,3},{3,5},{5,7},{7,1},{8,10},{10,12},{12... | collective-permute-start | bytes 786440 | tf_op jit(solution)/shard_map/ppermute | solution.py:43
  32.6 22.0 %all-to-all-start.1 = ((bf16[8,3,64,256]{3,2,1,0:T(8,128)(2,1)}), bf16[8,3,64,256]{3,2,1,0:T(8,128)(2,1)S(1)}, u32[]{:S(2)}, u32[]{:S(2)}) async-start(bf16[8,3,64,256]{3,2,1,0:T(8,128)(2,1)} %shard_map.294), calls=%async_computation.1 | async-start | bytes 1572864 | tf_op jit(solution)/shard_map/all_to_all | solution.py:55
  54.6 30.6 %all-to-all-start.2 = ((bf16[8,64,1024]{2,1,0:T(8,128)(2,1)}), bf16[8,64,1024]{2,1,0:T(8,128)(2,1)S(1)}, u32[]{:S(2)}, u32[]{:S(2)}) async-start(bf16[8,64,1024]{2,1,0:T(8,128)(2,1)} %shard_map.295), calls=%async_computation.2 | async-start | bytes 2097152 | tf_op jit(solution)/shard_map/all_to_all | solution.py:55
  58.6 118.2 %all-gather.8.cloned.1.call-start = ((), (), s32[]{:S(2)}) async-start(), calls=%async_computation.13 | async-start | bytes 5242880 | tf_op jit(solution)/shard_map/all_gather | solution.py:631
  58.6 23.0 %collective-permute-start.3 = (bf16[128,2048]{1,0:T(8,128)(2,1)S(1)}, bf16[128,2048]{1,0:T(8,128)(2,1)S(1)}, u32[]{:S(2)}, u32[]{:S(2)}) collective-permute-start(bf16[128,2048]{1,0:T(8,128)(2,1)S(1)} %reshape.344), channel_id=1, source_target_pairs={{0,17},{16,0},{1,16},{17,1},{2,19},{18,2},{3,18},{19,3},{4,21},{20... | collective-permute-start | bytes 1572872 | tf_op jit(solution)/shard_map/ppermute | solution.py:43
  86.2 30.5 %all-to-all-start.3 = ((bf16[8,64,1024]{2,1,0:T(8,128)(2,1)}), bf16[8,64,1024]{2,1,0:T(8,128)(2,1)S(1)}, u32[]{:S(2)}, u32[]{:S(2)}) async-start(bf16[8,64,1024]{2,1,0:T(8,128)(2,1)} %shard_map.296), calls=%async_computation.3 | async-start | bytes 2097152 | tf_op jit(solution)/shard_map/all_to_all | solution.py:55
  89.7 116.6 %all-gather.10.cloned.1.call-start = ((), (), s32[]{:S(2)}) async-start(), calls=%async_computation.14 | async-start | bytes 5242880 | tf_op jit(solution)/shard_map/all_gather | solution.py:633
  90.7 24.1 %collective-permute-start.4 = (bf16[128,2048]{1,0:T(8,128)(2,1)S(1)}, bf16[128,2048]{1,0:T(8,128)(2,1)}, u32[]{:S(2)}, u32[]{:S(2)}) collective-permute-start(bf16[128,2048]{1,0:T(8,128)(2,1)S(1)} %reshape.344), channel_id=1, source_target_pairs={{0,1},{16,17},{1,0},{17,16},{2,3},{18,19},{3,2},{19,18},{4,5},{20,... | collective-permute-start | bytes 1572872 | tf_op jit(solution)/shard_map/ppermute | solution.py:43
  92.4 37.9 %collective-permute-start.5 = (bf16[128,2048]{1,0:T(8,128)(2,1)S(1)}, bf16[128,2048]{1,0:T(8,128)(2,1)}, u32[]{:S(2)}, u32[]{:S(2)}) collective-permute-start(bf16[128,2048]{1,0:T(8,128)(2,1)S(1)} %reshape.344), channel_id=1, source_target_pairs={{0,16},{16,1},{1,17},{17,0},{2,18},{18,3},{3,19},{19,2},{4,20},{20... | collective-permute-start | bytes 1572872 | tf_op jit(solution)/shard_map/ppermute | solution.py:43
  117.6 18.7 %collective-permute-start.7 = (bf16[512,768]{1,0:T(8,128)(2,1)S(1)}, bf16[512,768]{1,0:T(8,128)(2,1)S(1)}, u32[]{:S(2)}, u32[]{:S(2)}) collective-permute-start(bf16[512,768]{1,0:T(8,128)(2,1)S(1)} %bitcast.211), channel_id=1, source_target_pairs={{0,6},{2,0},{4,2},{6,4},{1,7},{3,1},{5,3},{7,5},{8,14},{10,8},{12,... | collective-permute-start | bytes 2359304 | tf_op jit(solution)/shard_map/ppermute | solution.py:43
  132.2 32.1 %collective-permute-start.6 = (bf16[512,2048]{1,0:T(8,128)(2,1)}, bf16[512,2048]{1,0:T(8,128)(2,1)}, u32[]{:S(2)}, u32[]{:S(2)}) collective-permute-start(bf16[512,2048]{1,0:T(8,128)(2,1)} %constant_dynamic-update-slice_fusion.mine_ref), channel_id=1, source_target_pairs={{0,8},{8,0},{1,9},{9,1},{2,10},{10,2},{3,11},{11,3},{4,12},{12,4},... | collective-permute-start | bytes 6291464 | tf_op jit(solution)/shard_map/ppermute | solution.py:43
  135.2 167.0 %all-gather.12.cloned.1.call-start = ((), (), s32[]{:S(2)}) async-start(), calls=%async_computation.18 | async-start | bytes 4718592 | tf_op jit(solution)/shard_map/all_gather | solution.py:666
  136.3 20.3 %collective-permute-start.8 = (bf16[512,768]{1,0:T(8,128)(2,1)S(1)}, bf16[512,768]{1,0:T(8,128)(2,1)S(1)}, u32[]{:S(2)}, u32[]{:S(2)}) collective-permute-start(bf16[512,768]{1,0:T(8,128)(2,1)S(1)} %collective-permute-done.7), channel_id=1, source_target_pairs={{0,6},{2,0},{4,2},{6,4},{1,7},{3,1},{5,3},{7,5},{8,14},{10,8},{12,... | collective-permute-start | bytes 2359304 | tf_op jit(solution)/shard_map/ppermute | solution.py:43
  156.6 20.2 %collective-permute-start.9 = (bf16[512,768]{1,0:T(8,128)(2,1)S(1)}, bf16[512,768]{1,0:T(8,128)(2,1)}, u32[]{:S(2)}, u32[]{:S(2)}) collective-permute-start(bf16[512,768]{1,0:T(8,128)(2,1)S(1)} %collective-permute-done.8), channel_id=1, source_target_pairs={{0,6},{2,0},{4,2},{6,4},{1,7},{3,1},{5,3},{7,5},{8,14},{10,8},{12,... | collective-permute-start | bytes 2359304 | tf_op jit(solution)/shard_map/ppermute | solution.py:43
  188.7 4.2 collective-permute-start.10
  206.4 185.1 %reduce-scatter.13.cloned.1.call-start = ((), (), s32[]{:S(2)}) async-start(), calls=%async_computation.19 | async-start | bytes 4718592
  208.0 14.0 %collective-permute-start.13 = (bf16[128,2048]{1,0:T(8,128)(2,1)S(1)}, bf16[128,2048]{1,0:T(8,128)(2,1)S(1)}, u32[]{:S(2)}, u32[]{:S(2)}) collective-permute-start(bf16[128,2048]{1,0:T(8,128)(2,1)S(1)} %get-tuple-element.236), channel_id=1, source_target_pairs={{0,17},{16,0},{1,16},{17,1},{2,19},{18,2},{3,18},{19,3},{4,21},{20... | collective-permute-start | bytes 1572872 | tf_op jit(solution)/shard_map/ppermute | solution.py:43
  209.5 24.4 %collective-permute-start.12 = (bf16[128,2048]{1,0:T(8,128)(2,1)S(1)}, bf16[128,2048]{1,0:T(8,128)(2,1)S(1)}, u32[]{:S(2)}, u32[]{:S(2)}) collective-permute-start(bf16[128,2048]{1,0:T(8,128)(2,1)S(1)} %get-tuple-element.237), channel_id=1, source_target_pairs={{0,1},{16,17},{1,0},{17,16},{2,3},{18,19},{3,2},{19,18},{4,5},{20,... | collective-permute-start | bytes 1572872 | tf_op jit(solution)/shard_map/ppermute | solution.py:43
  210.9 23.2 %collective-permute-start.11 = (bf16[128,2048]{1,0:T(8,128)(2,1)S(1)}, bf16[128,2048]{1,0:T(8,128)(2,1)S(1)}, u32[]{:S(2)}, u32[]{:S(2)}) collective-permute-start(bf16[128,2048]{1,0:T(8,128)(2,1)S(1)} %get-tuple-element.235), channel_id=1, source_target_pairs={{0,16},{16,1},{1,17},{17,0},{2,18},{18,3},{3,19},{19,2},{4,20},{20... | collective-permute-start | bytes 1572872 | tf_op jit(solution)/shard_map/ppermute | solution.py:43
  235.3 27.9 %collective-permute-start.14 = (bf16[128,2048]{1,0:T(8,128)(2,1)S(1)}, bf16[128,2048]{1,0:T(8,128)(2,1)S(1)}, u32[]{:S(2)}, u32[]{:S(2)}) collective-permute-start(bf16[128,2048]{1,0:T(8,128)(2,1)S(1)} %copy.173.refs_0_), channel_id=1, source_target_pairs={{0,6},{2,0},{4,2},{6,4},{1,7},{3,1},{5,3},{7,5},{8,14},{10,8},{12,... | collective-permute-start | bytes 1572872 | tf_op jit(solution)/shard_map/ppermute | solution.py:43
  238.7 59.5 %collective-permute-start.15 = (bf16[128,2048]{1,0:T(8,128)(2,1)S(1)}, bf16[128,2048]{1,0:T(8,128)(2,1)S(1)}, u32[]{:S(2)}, u32[]{:S(2)}) collective-permute-start(bf16[128,2048]{1,0:T(8,128)(2,1)S(1)} %copy.173.refs_0_), channel_id=1, source_target_pairs={{0,4},{2,6},{4,0},{6,2},{1,5},{3,7},{5,1},{7,3},{8,12},{10,14},{12... | collective-permute-start | bytes 1572872 | tf_op jit(solution)/shard_map/ppermute | solution.py:43
  238.7 59.5 %collective-permute-start.16 = (bf16[128,2048]{1,0:T(8,128)(2,1)S(1)}, bf16[128,2048]{1,0:T(8,128)(2,1)S(1)}, u32[]{:S(2)}, u32[]{:S(2)}) collective-permute-start(bf16[128,2048]{1,0:T(8,128)(2,1)S(1)} %copy.173.refs_0_), channel_id=1, source_target_pairs={{0,2},{2,4},{4,6},{6,0},{1,3},{3,5},{5,7},{7,1},{8,10},{10,12},{12... | collective-permute-start | bytes 1572872 | tf_op jit(solution)/shard_map/ppermute | solution.py:43
  302.2 11.9 %collective-permute-start.17 = (bf16[512,2048]{1,0:T(8,128)(2,1)}, bf16[512,2048]{1,0:T(8,128)(2,1)S(1)}, u32[]{:S(2)}, u32[]{:S(2)}) collective-permute-start(bf16[512,2048]{1,0:T(8,128)(2,1)} %bitcast.186), channel_id=1, source_target_pairs={{0,8},{8,0},{1,9},{9,1},{2,10},{10,2},{3,11},{11,3},{4,12},{12,4},... | collective-permute-start | bytes 6291464 | tf_op jit(solution)/shard_map/ppermute | solution.py:43
  343.0 102.7 %reduce-scatter.7.cloned.1.call-start = ((), (), s32[]{:S(2)}) async-start(), calls=%async_computation.15 | async-start | bytes 4718592 | tf_op jit(solution)/shard_map/reduce_scatter | solution.py:678
  392.9 140.9 %reduce-scatter.9.cloned.1.call-start = ((), (), s32[]{:S(2)}) async-start(), calls=%async_computation.16 | async-start | bytes 10485760 | tf_op jit(solution)/shard_map/reduce_scatter | solution.py:678
  395.8 15.8 %collective-permute-start.20 = (bf16[128,2048]{1,0:T(8,128)(2,1)S(1)}, bf16[128,2048]{1,0:T(8,128)(2,1)S(1)}, u32[]{:S(2)}, u32[]{:S(2)}) collective-permute-start(bf16[128,2048]{1,0:T(8,128)(2,1)S(1)} %get-tuple-element.222), channel_id=1, source_target_pairs={{0,16},{16,1},{1,17},{17,0},{2,18},{18,3},{3,19},{19,2},{4,20},{20... | collective-permute-start | bytes 1572872 | tf_op jit(solution)/shard_map/ppermute | solution.py:43
  397.3 14.9 %collective-permute-start.19 = (bf16[128,2048]{1,0:T(8,128)(2,1)S(1)}, bf16[128,2048]{1,0:T(8,128)(2,1)S(1)}, u32[]{:S(2)}, u32[]{:S(2)}) collective-permute-start(bf16[128,2048]{1,0:T(8,128)(2,1)S(1)} %get-tuple-element.222), channel_id=1, source_target_pairs={{0,1},{16,17},{1,0},{17,16},{2,3},{18,19},{3,2},{19,18},{4,5},{20,... | collective-permute-start | bytes 1572872 | tf_op jit(solution)/shard_map/ppermute | solution.py:43
  398.8 20.7 %collective-permute-start.18 = (bf16[128,2048]{1,0:T(8,128)(2,1)S(1)}, bf16[128,2048]{1,0:T(8,128)(2,1)S(1)}, u32[]{:S(2)}, u32[]{:S(2)}) collective-permute-start(bf16[128,2048]{1,0:T(8,128)(2,1)S(1)} %get-tuple-element.222), channel_id=1, source_target_pairs={{0,17},{16,0},{1,16},{17,1},{2,19},{18,2},{3,18},{19,3},{4,21},{20... | collective-permute-start | bytes 1572872 | tf_op jit(solution)/shard_map/ppermute | solution.py:43
  419.6 4.4 collective-permute-start.21
  424.0 191.3 %reduce-scatter.11.cloned.1.call-start = ((), (), s32[]{:S(2)}) async-start(), calls=%async_computation.17 | async-start | bytes 5242880 | tf_op jit(solution)/shard_map/reduce_scatter | solution.py:678
  453.1 10.4 %collective-permute-start.24 = (bf16[512,2048]{1,0:T(8,128)(2,1)}, bf16[512,2048]{1,0:T(8,128)(2,1)}, u32[]{:S(2)}, u32[]{:S(2)}) collective-permute-start(bf16[512,2048]{1,0:T(8,128)(2,1)} %shard_map.306), channel_id=1, source_target_pairs={{0,8},{8,0},{1,9},{9,1},{2,10},{10,2},{3,11},{11,3},{4,12},{12,4},... | collective-permute-start | bytes 6291464 | tf_op jit(solution)/shard_map/ppermute | solution.py:43
  454.5 27.3 %collective-permute-start.22 = (bf16[512,768]{1,0:T(8,128)(2,1)S(1)}, bf16[512,768]{1,0:T(8,128)(2,1)}, u32[]{:S(2)}, u32[]{:S(2)}) collective-permute-start(bf16[512,768]{1,0:T(8,128)(2,1)S(1)} %slice_bitcast_fusion), channel_id=1, source_target_pairs={{0,2},{2,4},{4,6},{6,0},{1,3},{3,5},{5,7},{7,1},{8,10},{10,12},{12... | collective-permute-start | bytes 2359304 | tf_op jit(solution)/shard_map/ppermute | solution.py:43
  455.9 25.9 %collective-permute-start.23 = (bf16[64,2048]{1,0:T(8,128)(2,1)S(1)}, bf16[64,2048]{1,0:T(8,128)(2,1)S(1)}, u32[]{:S(2)}, u32[]{:S(2)}) collective-permute-start(bf16[64,2048]{1,0:T(8,128)(2,1)S(1)} %slice_bitcast_fusion.1), channel_id=1, source_target_pairs={{0,2},{2,4},{4,6},{6,0},{1,3},{3,5},{5,7},{7,1},{8,10},{10,12},{12... | collective-permute-start | bytes 786440 | tf_op jit(solution)/shard_map/ppermute | solution.py:43
  483.2 22.3 %collective-permute-start.25 = (bf16[512,768]{1,0:T(8,128)(2,1)S(1)}, bf16[512,768]{1,0:T(8,128)(2,1)S(1)}, u32[]{:S(2)}, u32[]{:S(2)}) collective-permute-start(bf16[512,768]{1,0:T(8,128)(2,1)S(1)} %fusion.6), channel_id=1, source_target_pairs={{0,2},{2,4},{4,6},{6,0},{1,3},{3,5},{5,7},{7,1},{8,10},{10,12},{12... | collective-permute-start | bytes 2359304 | tf_op jit(solution)/shard_map/ppermute | solution.py:43
  483.3 27.8 %collective-permute-start.27 = (bf16[64,2048]{1,0:T(8,128)(2,1)S(1)}, bf16[64,2048]{1,0:T(8,128)(2,1)S(1)}, u32[]{:S(2)}, u32[]{:S(2)}) collective-permute-start(bf16[64,2048]{1,0:T(8,128)(2,1)S(1)} %fusion.26), channel_id=1, source_target_pairs={{0,2},{2,4},{4,6},{6,0},{1,3},{3,5},{5,7},{7,1},{8,10},{10,12},{12... | collective-permute-start | bytes 786440 | tf_op jit(solution)/shard_map/ppermute | solution.py:43
  505.7 26.4 %collective-permute-start.26 = (bf16[512,768]{1,0:T(8,128)(2,1)S(1)}, bf16[512,768]{1,0:T(8,128)(2,1)S(1)}, u32[]{:S(2)}, u32[]{:S(2)}) collective-permute-start(bf16[512,768]{1,0:T(8,128)(2,1)S(1)} %fusion.5), channel_id=1, source_target_pairs={{0,2},{2,4},{4,6},{6,0},{1,3},{3,5},{5,7},{7,1},{8,10},{10,12},{12... | collective-permute-start | bytes 2359304 | tf_op jit(solution)/shard_map/ppermute | solution.py:43
  511.2 20.9 %collective-permute-start.28 = (bf16[64,2048]{1,0:T(8,128)(2,1)S(1)}, bf16[64,2048]{1,0:T(8,128)(2,1)S(1)}, u32[]{:S(2)}, u32[]{:S(2)}) collective-permute-start(bf16[64,2048]{1,0:T(8,128)(2,1)S(1)} %fusion.25), channel_id=1, source_target_pairs={{0,2},{2,4},{4,6},{6,0},{1,3},{3,5},{5,7},{7,1},{8,10},{10,12},{12... | collective-permute-start | bytes 786440 | tf_op jit(solution)/shard_map/ppermute | solution.py:43
  533.8 52.6 %all-to-all-start.4 = ((bf16[8,64,2048]{2,1,0:T(8,128)(2,1)}), bf16[8,64,2048]{2,1,0:T(8,128)(2,1)S(1)}, u32[]{:S(2)}, u32[]{:S(2)}) async-start(bf16[8,64,2048]{2,1,0:T(8,128)(2,1)} %bitcast.220), calls=%async_computation.6 | async-start | bytes 4194304 | tf_op jit(solution)/shard_map/all_to_all | solution.py:55
  586.3 38.4 %all-to-all-start.5 = ((bf16[8,3,64,256]{3,2,1,0:T(8,128)(2,1)}), bf16[8,3,64,256]{3,2,1,0:T(8,128)(2,1)}, u32[]{:S(2)}, u32[]{:S(2)}) async-start(bf16[8,3,64,256]{3,2,1,0:T(8,128)(2,1)} %bitcast.210), calls=%async_computation.7 | async-start | bytes 1572864 | tf_op jit(solution)/shard_map/all_to_all | solution.py:55
  593.2 29.7 %collective-permute-start.29 = (bf16[128,2048]{1,0:T(8,128)(2,1)}, bf16[128,2048]{1,0:T(8,128)(2,1)S(1)}, u32[]{:S(2)}, u32[]{:S(2)}) collective-permute-start(bf16[128,2048]{1,0:T(8,128)(2,1)} %get-tuple-element.234), channel_id=1, source_target_pairs={{0,16},{16,1},{1,17},{17,0},{2,18},{18,3},{3,19},{19,2},{4,20},{20... | collective-permute-start | bytes 1572872 | tf_op jit(solution)/shard_map/ppermute | solution.py:43
  595.1 27.8 %collective-permute-start.30 = (bf16[128,2048]{1,0:T(8,128)(2,1)}, bf16[128,2048]{1,0:T(8,128)(2,1)S(1)}, u32[]{:S(2)}, u32[]{:S(2)}) collective-permute-start(bf16[128,2048]{1,0:T(8,128)(2,1)} %get-tuple-element.233), channel_id=1, source_target_pairs={{0,1},{16,17},{1,0},{17,16},{2,3},{18,19},{3,2},{19,18},{4,5},{20,... | collective-permute-start | bytes 1572872 | tf_op jit(solution)/shard_map/ppermute | solution.py:43
  596.5 28.2 %collective-permute-start.31 = (bf16[128,2048]{1,0:T(8,128)(2,1)}, bf16[128,2048]{1,0:T(8,128)(2,1)}, u32[]{:S(2)}, u32[]{:S(2)}) collective-permute-start(bf16[128,2048]{1,0:T(8,128)(2,1)} %get-tuple-element.232), channel_id=1, source_target_pairs={{0,17},{16,0},{1,16},{17,1},{2,19},{18,2},{3,18},{19,3},{4,21},{20... | collective-permute-start | bytes 1572872 | tf_op jit(solution)/shard_map/ppermute | solution.py:43
  630.3 11.2 %all-to-all-start.6 = ((f32[32,1,320]{2,1,0:T(1,128)}), f32[32,1,320]{2,1,0:T(1,128)S(1)}, u32[]{:S(2)}, u32[]{:S(2)}) async-start(f32[32,1,320]{2,1,0:T(1,128)} %reshape.401), calls=%async_computation.9 | async-start | bytes 98304 | tf_op jit(solution)/shard_map/all_to_all | solution.py:55
  647.0 16.5 %all-to-all-start.7 = ((f32[32,8,2,128]{3,1,2,0:T(8,128)}), f32[32,8,2,128]{3,1,2,0:T(8,128)S(1)}, u32[]{:S(2)}, u32[]{:S(2)}) async-start(f32[32,8,2,128]{3,1,2,0:T(8,128)} %broadcast_in_dim.49), calls=%async_computation.10 | async-start | bytes 524288 | tf_op jit(solution)/shard_map/all_to_all | solution.py:55
  (48 other events, 489.9 us)
Sparse Core Ops, SparseCore 0:
  10.5 68.6 all-gather.5
  86.3 64.6 all-gather.7
  153.4 52.8 all-gather.9
  207.8 54.1 all-gather.11
  343.1 48.2 reduce-scatter.12
  394.2 48.1 reduce-scatter.6
  445.4 84.5 reduce-scatter.8
  533.3 52.6 reduce-scatter.10

commit v4 on v3

--- a/solution.py
+++ b/solution.py
@@ -409,25 +409,25 @@
 
 def adam_gate_kernel(w_ref, m_ref, v_ref, got_ref, *refs):
     grad = jnp.concatenate([got_ref[h, 0] for h in range(got_ref.shape[0])], 1).astype(WIDE)
-    adam_step(pl.program_id(0) == 0, grad, w_ref, m_ref, v_ref, *refs[-5:])
-
-
-def adam_gate(sizes, w, m, v, got, kind, done=()):
+    adam_step(pl.program_id(1) == 0, grad, w_ref, m_ref, v_ref, *refs[-5:])
+
+
+def adam_gate(sizes, w, m, v, got, done=()):
     ny, nc, nh, _ = sizes
     rows = w.shape[0]
     part = got.shape[2] // (2 * ny)
     width = nh * part
-    first = 4 * D + kind * FF
-    column = pl.BlockSpec((rows, width), lambda b: (0, first // width + b))
+    blocks = ny * nc
+    column = pl.BlockSpec((rows, width), lambda k, b: (0, 4 * D // width + k * blocks + b))
     like = jax.ShapeDtypeStruct(w.shape, WIDE)
     return pl.pallas_call(
         adam_gate_kernel,
-        grid=(ny * nc,),
+        grid=(2, blocks),
         in_specs=[column] * 3
-        + [pl.BlockSpec((nh, 1, rows, part), lambda b: (0, b % nc, 0, kind * ny + b // nc))]
+        + [pl.BlockSpec((nh, 1, rows, part), lambda k, b: (0, b % nc, 0, k * ny + b // nc))]
         + [pl.BlockSpec(memory_space=pl.ANY) for _ in done],
-        out_specs=[column] * 4 + [pl.BlockSpec((1, 2, 8, 128), lambda b: (0, 0, 0, 0))],
-        out_shape=[like] * 4 + [jax.ShapeDtypeStruct((1, 2, 8, 128), WIDE)],
+        out_specs=[column] * 4 + [pl.BlockSpec((1, 2, 8, 128), lambda k, b: (k, 0, 0, 0))],
+        out_shape=[like] * 4 + [jax.ShapeDtypeStruct((2, 2, 8, 128), WIDE)],
         input_output_aliases={4 + k: k for k in range(len(done))},
         compiler_params=pltpu.CompilerParams(vmem_limit_bytes=ROOM),
         cost_estimate=SHORT,
@@ -503,19 +503,25 @@
     )(w, m, v, got, *done)
 
 
-def step_kernel(ratio_ref, w_ref, dir_ref, out_ref):
-    block = pl.program_id(0)
-    piece = jnp.where(block < 3, 0, jnp.where(block < 4, 1, jnp.where(block < 4 + FF // D, 2, 3)))
-    out_ref[...] = w_ref[...] + dir_ref[...] * ratio_ref[piece]
+def step_kernel(count, ratio_ref, w_ref, dir_ref, out_ref):
+    for k in range(count):
+        block = pl.program_id(0) * count + k
+        piece = jnp.where(block < 3, 0, jnp.where(block < 4, 1, jnp.where(block < 4 + FF // D, 2, 3)))
+        at = slice(k * D, (k + 1) * D)
+        out_ref[:, at] = w_ref[:, at] + dir_ref[:, at] * ratio_ref[piece]
 
 
 def stepped(ratio, w, direction):
     rows, cols = w.shape
-    column = pl.BlockSpec((rows, D), lambda b, r: (0, b))
-    return pl.pallas_call(
-        step_kernel,
+    count = 3
+    column = pl.BlockSpec((rows, count * D), lambda b, r: (0, b))
+    return pl.pallas_call(
+        functools.partial(step_kernel, count),
         grid_spec=pltpu.PrefetchScalarGridSpec(
-            num_scalar_prefetch=1, grid=(cols // D,), in_specs=[column] * 2, out_specs=column
+            num_scalar_prefetch=1,
+            grid=(cols // (count * D),),
+            in_specs=[column] * 2,
+            out_specs=column,
         ),
         out_shape=jax.ShapeDtypeStruct(w.shape, WIDE),
         compiler_params=pltpu.CompilerParams(vmem_limit_bytes=ROOM),
@@ -736,7 +742,7 @@
     got_feed = exchanged(got_feed.reshape(nh * nc, rows, -1), FEED)
     *done, sums_o = adam_columns(w_in, m_in, v_in, grad_o, 3 * D, 1)
     got_feed, part_p, sums_o = tied(got_feed, part_p, sums_o)
-    got_p, *sent = tied(exchanged(part_p, CONV), *sent)
+    got_p = exchanged(part_p, CONV)
     d_h_one = total(both, sent)
     d_values, d_gain_one = norm_backward(values, scale_one, gain_one, from_conv_order(d_h_one))
     input_grad = (d_values + d_middle).reshape(inputs.shape)
@@ -747,11 +753,12 @@
     )
     gain_terms = jnp.stack([d_gain_one, d_gain_two], 1).reshape(sizes + (rows, 2))
     terms = jnp.concatenate([tap_terms, gain_terms], -1).reshape(-1, rows, TAPS + 2)
+    terms, got_feed = tied(terms, got_feed)
+    *done, sums_wide = adam_gate(sizes, w_in, m_in, v_in, got_feed, done)
+    got_p, terms, sums_wide = tied(got_p, terms, sums_wide)
     terms = exchanged(terms, AXES)
-    *done, sums_gate = adam_gate(sizes, w_in, m_in, v_in, got_feed, 0, done)
-    *done, sums_up = adam_gate(sizes, w_in, m_in, v_in, got_feed, 1, done)
     *done, sums_p = adam_first(sizes, w_in, m_in, v_in, got_p, done)
-    grad_down, sums_up = tied(grad_down, sums_up)
+    grad_down, sums_wide = tied(grad_down, sums_wide)
     grad_down, new_m_down, new_v_down, dir_down, sums_down = adam_down(w_down, m_down, v_down, grad_down)
     grad_in, new_m_in, new_v_in, dir_in = done
     block_out = (middle + out_sum.astype(WIDE)).astype(LOW).reshape(inputs.shape)
@@ -760,22 +767,19 @@
     new_m_taps, new_v_taps, dir_taps = adam_direction(conv_taps, grad_taps, m_taps, v_taps)
     new_m_gains, new_v_gains, dir_gains = adam_direction(norm_gains, grad_gains, m_gains, v_gains)
 
-    def lanes(a):
-        return jnp.pad(jnp.sum(a * a, axis=0), (0, 128 - a.shape[1]))
-
     def small(taps_like, gains_like):
-        return jnp.stack(
-            [lanes(taps_like), lanes(gains_like[:, :1]), lanes(gains_like[:, 1:])], 0
+        return jnp.concatenate(
+            [jnp.sum(taps_like * taps_like)[None], jnp.sum(gains_like * gains_like, axis=0)]
         )
 
     sums = jnp.concatenate(
         [
-            jnp.sum(jnp.concatenate([sums_p, sums_o, sums_gate, sums_up, sums_down], 0), axis=2),
+            jnp.sum(jnp.concatenate([sums_p, sums_o, sums_wide, sums_down], 0), axis=(2, 3)),
             jnp.stack([small(conv_taps, norm_gains), small(dir_taps, dir_gains)], 1),
         ],
         0,
     )
-    lamb_norms = jnp.sqrt(jnp.sum(spread_to(sums, AXES), axis=(0, 3)).T)
+    lamb_norms = jnp.sqrt(jnp.sum(spread_to(sums, AXES), axis=0).T)
     ratio = -RATE * lamb_norms[0] / (lamb_norms[1] + 1e-06)
     new_w_in = stepped(ratio[:4], w_in, dir_in)
     new_w_down = w_down + dir_down * ratio[4]

time: 698 us -> 683 us (0.979)
  waiting for transfers between devices: 332 us -> 305 us
  starting transfers between devices: 81 us -> 96.7 us
    ppermute x32, waiting for transfers between devices: 251 us -> 231 us  [turned(): return lax.ppermute(value, ordered if len(names) > 1 else axes, pairs)]
    reduce_scatter x3, starting transfers between devices: 0.3 us -> 12 us  [summed(): return lax.psum_scatter(part, axes, scatter_dimension=0, tiled=True)]
    pallas_call x3 -> x2, Pallas kernels: 27.3 us -> 23.1 us  [the longest x1 14.6 us: adam_gate(): pl.pallas_call(adam_gate_kernel, grid=(2, blocks), in_specs=[column] * 3...]
  transfers between devices with their start and end apart: 48 -> 48, of which waited for: 27 -> 27; matrix products, arithmetic and copies ran while one was open for 12% -> 13% of each run, Pallas kernels for 16% -> 17%
where the time goes in v4:
time: 683 us; the launch traced here: 674 us
  waiting for transfers between devices  305 us (45%)
  Pallas kernels  149 us (22%)
  starting transfers between devices  96.7 us (14%)
  local copies, waits for them, and re-layouts  45.7 us (7%)
  other arithmetic  43.5 us (6%)
  matrix products  19.5 us (3%)
  between operations  15.6 us (2%)
    ppermute x32, waiting for transfers between devices, turned(): return lax.ppermute(value, ordered if len(names) > 1 else axes, pairs)  231 us
    ppermute x32, starting transfers between devices, turned(): return lax.ppermute(value, ordered if len(names) > 1 else axes, pairs)  48.1 us
    all_to_all x8, waiting for transfers between devices, exchanged(): return lax.all_to_all(value, axes, 0, 0, tiled=True)  48.1 us
    all_to_all x8, starting transfers between devices, exchanged(): return lax.all_to_all(value, axes, 0, 0, tiled=True)  36.4 us
    pallas_call x2, Pallas kernels, both_cores(): pl.pallas_call(functools.partial(both_kernel, len(mine), wide), grid_spec...  26.5 us
    pallas_call x2, Pallas kernels, feed(): pl.pallas_call(feed_kernel, grid_spec=pltpu.PrefetchScalarGridSpec(num_sc...  24 us
    pallas_call x2, Pallas kernels, weight_grads(): pl.pallas_call(functools.partial(weight_kernel, parts, outs), grid=(rows...  20.8 us
    unnamed x9, waiting for transfers between devices  15.1 us
  transfers between devices with their start and end apart: 48, of which 27 were waited for; matrix products, arithmetic and copies ran while one was open for 13% of the time, Pallas kernels for 17%

profile of v4, /device:TPU:0, one launch (start us, length us, event | category | flops | bytes accessed | tf_op | source)
XLA Modules:
  0.0 674.5 jit_solution(15048399251079302213)
XLA Ops:
  11.3 7.3 %all-to-all-start = ((f32[32,1,448]{2,1,0:T(1,128)}), f32[32,1,448]{2,1,0:T(1,128)S(1)}, u32[]{:S(2)}, u32[]{:S(2)}) async-start(f32[32,1,448]{2,1,0:T(1,128)} %broadcast_in_dim.22), calls=%async_computation | async-start | bytes 131072 | tf_op jit(solution)/shard_map/all_to_all | solution.py:55
  33.1 3.7 all-to-all-start.1
  40.2 9.3 %collective-permute-done.1 = bf16[64,2048]{1,0:T(8,128)(2,1)} collective-permute-done((bf16[64,2048]{1,0:T(8,128)(2,1)}, bf16[64,2048]{1,0:T(8,128)(2,1)}, u32[]{:S(2)}, u32[]{:S(2)}) %collective-permute-start.1) | collective-permute-done | bytes 262176 | tf_op jit(solution)/shard_map/ppermute | solution.py:43
  49.5 4.1 all-to-all-done.1
  53.6 4.4 all-to-all-start.2
  62.8 19.4 %collective-permute-done.3 = bf16[128,2048]{1,0:T(8,128)(2,1)S(1)} collective-permute-done((bf16[128,2048]{1,0:T(8,128)(2,1)S(1)}, bf16[128,2048]{1,0:T(8,128)(2,1)S(1)}, u32[]{:S(2)}, u32[]{:S(2)}) %collective-permute-start.3) | collective-permute-done | bytes 524320 | tf_op jit(solution)/shard_map/ppermute | solution.py:43
  94.9 19.3 %collective-permute-done.4 = bf16[128,2048]{1,0:T(8,128)(2,1)} collective-permute-done((bf16[128,2048]{1,0:T(8,128)(2,1)S(1)}, bf16[128,2048]{1,0:T(8,128)(2,1)}, u32[]{:S(2)}, u32[]{:S(2)}) %collective-permute-start.4) | collective-permute-done | bytes 524320 | tf_op jit(solution)/shard_map/ppermute | solution.py:43
  116.9 3.7 collective-permute-start.7
  120.7 8.9 %collective-permute-done.5 = bf16[128,2048]{1,0:T(8,128)(2,1)} collective-permute-done((bf16[128,2048]{1,0:T(8,128)(2,1)S(1)}, bf16[128,2048]{1,0:T(8,128)(2,1)}, u32[]{:S(2)}, u32[]{:S(2)}) %collective-permute-start.5) | collective-permute-done | bytes 524320 | tf_op jit(solution)/shard_map/ppermute | solution.py:43
  135.6 4.0 collective-permute-start.8
  143.0 12.9 %collective-permute-done.8 = bf16[512,768]{1,0:T(8,128)(2,1)S(1)} collective-permute-done((bf16[512,768]{1,0:T(8,128)(2,1)S(1)}, bf16[512,768]{1,0:T(8,128)(2,1)S(1)}, u32[]{:S(2)}, u32[]{:S(2)}) %collective-permute-start.8) | collective-permute-done | bytes 786464 | tf_op jit(solution)/shard_map/ppermute | solution.py:43
  155.9 4.6 collective-permute-start.9
  163.4 5.5 shard_map.297
  169.1 6.8 %collective-permute-done.9 = bf16[512,768]{1,0:T(8,128)(2,1)} collective-permute-done((bf16[512,768]{1,0:T(8,128)(2,1)S(1)}, bf16[512,768]{1,0:T(8,128)(2,1)}, u32[]{:S(2)}, u32[]{:S(2)}) %collective-permute-start.9) | collective-permute-done | bytes 786464 | tf_op jit(solution)/shard_map/ppermute | solution.py:43
  177.0 6.3 fusion
  187.9 4.1 collective-permute-done.10
  195.4 10.3 %all-gather.10.cloned.1.call-done.u_ref.refs_5_ = bf16[2048,1024]{1,0:T(8,128)(2,1)} async-done(((bf16[512,1024]{1,0:T(8,128)(2,1)}), bf16[2048,1024]{1,0:T(8,128)(2,1)}) %all-gather.10.cloned.1.call-update) | async-done | bytes 4194320 | tf_op jit(solution)/shard_map/all_gather | solution.py:639
  211.7 19.5 %collective-permute-done.11 = bf16[128,2048]{1,0:T(8,128)(2,1)S(1)} collective-permute-done((bf16[128,2048]{1,0:T(8,128)(2,1)S(1)}, bf16[128,2048]{1,0:T(8,128)(2,1)S(1)}, u32[]{:S(2)}, u32[]{:S(2)}) %collective-permute-start.11) | collective-permute-done | bytes 524320 | tf_op jit(solution)/shard_map/ppermute | solution.py:43
  241.0 22.5 %collective-permute-done.16.refs_3_ = bf16[128,2048]{1,0:T(8,128)(2,1)S(1)} collective-permute-done((bf16[128,2048]{1,0:T(8,128)(2,1)S(1)}, bf16[128,2048]{1,0:T(8,128)(2,1)S(1)}, u32[]{:S(2)}, u32[]{:S(2)}) %collective-permute-start.16) | collective-permute-done | bytes 524320 | tf_op jit(solution)/shard_map/ppermute | solution.py:43
  263.5 23.0 %collective-permute-done.15.refs_2_ = bf16[128,2048]{1,0:T(8,128)(2,1)S(1)} collective-permute-done((bf16[128,2048]{1,0:T(8,128)(2,1)S(1)}, bf16[128,2048]{1,0:T(8,128)(2,1)S(1)}, u32[]{:S(2)}, u32[]{:S(2)}) %collective-permute-start.15) | collective-permute-done | bytes 524320 | tf_op jit(solution)/shard_map/ppermute | solution.py:43
  290.4 11.9 %shard_map.299 = (bf16[512,1024]{1,0:T(8,128)(2,1)}, bf16[512,1024]{1,0:T(8,128)(2,1)}, bf16[512,1024]{1,0:T(8,128)(2,1)}) custom-call(s32[1]{0:T(128)} %bitcast.2.c_ref, bf16[512,2048]{1,0:T(8,128)(2,1)} %bitcast.175, bf16[4,2,128,2048]{3,2,1,0:T(8,128)(2,1)} %bitcast.170, bf16[2048,1024]{1,0:T(8,128)(2,1)} %all-gather.8.cloned.1.call-done.g_ref.refs_4_, ...), custom_call_target="tpu_custom_call" | custom-call | flops 1024 | bytes 1024 | tf_op jit(solution)/shard_map/pallas_call | solution.py:178
  303.7 12.0 %shard_map.300 = (bf16[512,1024]{1,0:T(8,128)(2,1)}, bf16[512,1024]{1,0:T(8,128)(2,1)}, bf16[512,1024]{1,0:T(8,128)(2,1)}) custom-call(s32[1]{0:T(128)S(6)} %sub.9.c_ref, bf16[512,2048]{1,0:T(8,128)(2,1)} %copy-done.13, bf16[4,2,128,2048]{3,2,1,0:T(8,128)(2,1)} %bitcast.171, bf16[2048,1024]{1,0:T(8,128)(2,1)} %all-gather.8.cloned.1.call-done.g_ref.refs_4_, ...), custom_call_target="tpu_custom_call" | custom-call | flops 1024 | bytes 1024 | tf_op jit(solution)/shard_map/pallas_call | solution.py:178
  315.7 15.6 %shard_map.301 = bf16[4,2,128,2048]{3,2,1,0:T(8,128)(2,1)} custom-call(s32[1]{0:T(128)} %bitcast.2.c_ref, bf16[512,1024]{1,0:T(8,128)(2,1)} %get-tuple-element.124.refs_0_.refs_2_, bf16[512,1024]{1,0:T(8,128)(2,1)} %get-tuple-element.125.refs_1_.refs_3_, bf16[512,1024]{1,0:T(8,128)(2,1)} %get-tuple-element.126.refs_2_.refs_4_, ...), custom_call_target="tpu_custom_call" | custom-call | flops 1024 | bytes 1024 | tf_op jit(solution)/shard_map/pallas_call | solution.py:286
  331.3 12.0 %reduce-scatter.7.cloned.1.call-start = ((), (), s32[]{:S(2)}) async-start(), calls=%async_computation.15 | async-start | bytes 4718592 | tf_op jit(solution)/shard_map/reduce_scatter | solution.py:684
  343.3 13.5 %shard_map.302 = bf16[2048,2048]{1,0:T(8,128)(2,1)} custom-call(bf16[512,2048]{1,0:T(8,128)(2,1)} %bitcast.176, bf16[512,2048]{1,0:T(8,128)(2,1)} %copy-done.13, bf16[512,1024]{1,0:T(8,128)(2,1)} %get-tuple-element.124.refs_0_.refs_2_, bf16[512,1024]{1,0:T(8,128)(2,1)} %get-tuple-element.125.refs_1_.refs_3_, ...), custom_call_target="tpu_custom_call" | custom-call | flops 1024 | bytes 1024 | tf_op jit(solution)/shard_map/pallas_call | solution.py:322
  356.8 10.9 %shard_map.304 = bf16[4,2,128,2048]{3,2,1,0:T(8,128)(2,1)} custom-call(s32[1]{0:T(128)} %bitcast.2.c_ref, bf16[512,1024]{1,0:T(8,128)(2,1)} %get-tuple-element.131.mine_ref.refs_0_, bf16[512,1024]{1,0:T(8,128)(2,1)} %get-tuple-element.132.other_ref.refs_1_, bf16[1024,2048]{1,0:T(8,128)(2,1)} %all-gather.6.cloned.1.call-done.d_ref.refs_2_), custom_call_target="tpu_custom_call" | custom-call | flops 1024 | bytes 1024 | tf_op jit(solution)/shard_map/pallas_call | solution.py:286
  367.7 8.8 %shard_map.303 = bf16[1024,2048]{1,0:T(8,128)(2,1)} custom-call(s32[1]{0:T(128)} %bitcast.2.c_ref, bf16[512,1024]{1,0:T(8,128)(2,1)} %get-tuple-element.131.mine_ref.refs_0_, bf16[512,1024]{1,0:T(8,128)(2,1)} %get-tuple-element.132.other_ref.refs_1_, bf16[4,2,128,2048]{3,2,1,0:T(8,128)(2,1)} %bitcast.172, bf16[4,2,128,2048]{3,2,1,0:T(8,128)(2,1)} %bitcast.173), custom_call_target="tpu_custom_call" | custom-call | flops 1024 | bytes 1024 | tf_op jit(solution)/shard_map/pallas_call | solution.py:213
  376.5 15.0 %reduce-scatter.13.cloned.1.call-done = bf16[128,2048]{1,0:T(8,128)(2,1)} async-done(((bf16[1024,2048]{1,0:T(8,128)(2,1)}), bf16[128,2048]{1,0:T(8,128)(2,1)}) %reduce-scatter.13.cloned.1.call-update) | async-done | bytes 524304
  400.2 11.4 %collective-permute-done.20 = bf16[128,2048]{1,0:T(8,128)(2,1)S(1)} collective-permute-done((bf16[128,2048]{1,0:T(8,128)(2,1)S(1)}, bf16[128,2048]{1,0:T(8,128)(2,1)S(1)}, u32[]{:S(2)}, u32[]{:S(2)}) %collective-permute-start.20) | collective-permute-done | bytes 524320 | tf_op jit(solution)/shard_map/ppermute | solution.py:43
  412.1 7.3 %collective-permute-done.18 = bf16[128,2048]{1,0:T(8,128)(2,1)S(1)} collective-permute-done((bf16[128,2048]{1,0:T(8,128)(2,1)S(1)}, bf16[128,2048]{1,0:T(8,128)(2,1)S(1)}, u32[]{:S(2)}, u32[]{:S(2)}) %collective-permute-start.18) | collective-permute-done | bytes 524320 | tf_op jit(solution)/shard_map/ppermute | solution.py:43
  419.8 4.2 collective-permute-done.21
  432.6 7.3 %shard_map.305 = bf16[2048,768]{1,0:T(8,128)(2,1)} custom-call(bf16[1024,2048]{1,0:T(8,128)(2,1)} %bitcast.179, bf16[1024,768]{1,0:T(8,128)(2,1)} %pad_maximum_fusion.1.refs_1_), custom_call_target="tpu_custom_call" | custom-call | flops 1024 | bytes 1024 | tf_op jit(solution)/shard_map/pallas_call | solution.py:322
  447.6 5.5 shard_map.306
  458.1 5.7 shard_map.307
  463.9 5.5 fusion.35
  470.4 11.3 %collective-permute-done.23 = bf16[64,2048]{1,0:T(8,128)(2,1)S(1)} collective-permute-done((bf16[64,2048]{1,0:T(8,128)(2,1)S(1)}, bf16[64,2048]{1,0:T(8,128)(2,1)S(1)}, u32[]{:S(2)}, u32[]{:S(2)}) %collective-permute-start.23) | collective-permute-done | bytes 262176 | tf_op jit(solution)/shard_map/ppermute | solution.py:43
  484.9 20.6 %collective-permute-done.28 = bf16[512,768]{1,0:T(8,128)(2,1)S(1)} collective-permute-done((bf16[512,768]{1,0:T(8,128)(2,1)S(1)}, bf16[512,768]{1,0:T(8,128)(2,1)S(1)}, u32[]{:S(2)}, u32[]{:S(2)}) %collective-permute-start.28) | collective-permute-done | bytes 786464 | tf_op jit(solution)/shard_map/ppermute | solution.py:43
  505.8 5.3 collective-permute-done.30
  511.2 20.9 %collective-permute-done.31 = bf16[64,2048]{1,0:T(8,128)(2,1)S(1)} collective-permute-done((bf16[64,2048]{1,0:T(8,128)(2,1)S(1)}, bf16[64,2048]{1,0:T(8,128)(2,1)S(1)}, u32[]{:S(2)}, u32[]{:S(2)}) %collective-permute-start.31) | collective-permute-done | bytes 262176 | tf_op jit(solution)/shard_map/ppermute | solution.py:43
  550.5 35.9 %all-to-all-done.4 = bf16[8,64,2048]{2,1,0:T(8,128)(2,1)S(1)} async-done(((bf16[8,64,2048]{2,1,0:T(8,128)(2,1)}), bf16[8,64,2048]{2,1,0:T(8,128)(2,1)S(1)}, u32[]{:S(2)}, u32[]{:S(2)}) %all-to-all-start.4) | async-done | bytes 2097184 | tf_op jit(solution)/shard_map/all_to_all | solution.py:55
  586.3 4.4 all-to-all-start.5
  599.6 14.6 %shard_map.309 = (f32[64,24576]{1,0:T(8,128)}, f32[64,24576]{1,0:T(8,128)}, f32[64,24576]{1,0:T(8,128)}, f32[64,24576]{1,0:T(8,128)}, f32[2,2,8,128]{3,2,1,0:T(8,128)}) custom-call(f32[64,24576]{1,0:T(8,128)} %w_ref.15, f32[64,24576]{1,0:T(8,128)} %m_ref.6, ...), custom_call_target="tpu_custom_call", output_to_operand_aliasing={{0}: (4, {}), {1}: (5, {}), {2}: (6, {}), {3}: (7, {})} | custom-call | flops 1024 | bytes 1024 | tf_op jit(solution)/shard_map/pallas_call | solution.py:423
  615.0 3.6 all-to-all-start.6
  619.4 7.5 %shard_map.311 = (f32[256,2048]{1,0:T(8,128)}, f32[256,2048]{1,0:T(8,128)}, f32[256,2048]{1,0:T(8,128)}, f32[256,2048]{1,0:T(8,128)}, f32[1,2,8,128]{3,2,1,0:T(8,128)}) custom-call(f32[256,2048]{1,0:T(8,128)} %w_ref.14, f32[256,2048]{1,0:T(8,128)} %m_ref.7, f32[256,2048]{1,0:T(8,128)} %v_ref.7, bf16[256,2048]{1,0:T(8,128)(2,1)} %reduce-scatter.11.cloned.1.call-done.g_ref), custom_call_target="tpu_custom_call" | custom-call | flops 1024 | bytes 1024 | tf_op jit(solution)/shard_map/pallas_call | solution.py:465
  627.0 6.9 %shard_map.310 = (f32[64,24576]{1,0:T(8,128)}, f32[64,24576]{1,0:T(8,128)}, f32[64,24576]{1,0:T(8,128)}, f32[64,24576]{1,0:T(8,128)}, f32[1,2,8,128]{3,2,1,0:T(8,128)}) custom-call(f32[64,24576]{1,0:T(8,128)} %w_ref.15, f32[64,24576]{1,0:T(8,128)} %m_ref.6, ...), custom_call_target="tpu_custom_call", output_to_operand_aliasing={{0}: (4, {}), {1}: (5, {}), {2}: (6, {}), {3}: (7, {})} | custom-call | flops 1024 | bytes 1024 | tf_op jit(solution)/shard_map/pallas_call | solution.py:492
  640.2 5.8 all-to-all-start.7
  647.5 5.7 all-to-all-done.7
  655.2 8.5 %shard_map.312 = f32[64,24576]{1,0:T(8,128)} custom-call(f32[4]{0:T(128)} %slice_bitcast_fusion.3.ratio_ref, f32[64,24576]{1,0:T(8,128)} %w_ref.15, f32[64,24576]{1,0:T(8,128)} %get-tuple-element.183.dir_ref), custom_call_target="tpu_custom_call" | custom-call | flops 1024 | bytes 1024 | tf_op jit(solution)/shard_map/pallas_call | solution.py:518
  (295 shorter events, 161.5 us)
Async XLA Ops:
  7.2 77.3 %all-gather.6.cloned.1.call-start = ((), (), s32[]{:S(2)}) async-start(), calls=%async_computation.12 | async-start | bytes 5242880 | tf_op jit(solution)/shard_map/all_gather | solution.py:625
  11.3 16.1 %all-to-all-start = ((f32[32,1,448]{2,1,0:T(1,128)}), f32[32,1,448]{2,1,0:T(1,128)S(1)}, u32[]{:S(2)}, u32[]{:S(2)}) async-start(f32[32,1,448]{2,1,0:T(1,128)} %broadcast_in_dim.22), calls=%async_computation | async-start | bytes 131072 | tf_op jit(solution)/shard_map/all_to_all | solution.py:55
  27.4 12.8 %collective-permute-start.2 = (bf16[64,2048]{1,0:T(8,128)(2,1)}, bf16[64,2048]{1,0:T(8,128)(2,1)}, u32[]{:S(2)}, u32[]{:S(2)}) collective-permute-start(bf16[64,2048]{1,0:T(8,128)(2,1)} %slice.263), channel_id=1, source_target_pairs={{0,2},{2,4},{4,6},{6,0},{1,3},{3,5},{5,7},{7,1},{8,10},{10,12},{12... | collective-permute-start | bytes 786440 | tf_op jit(solution)/shard_map/ppermute | solution.py:43
  29.3 20.2 %collective-permute-start.1 = (bf16[64,2048]{1,0:T(8,128)(2,1)}, bf16[64,2048]{1,0:T(8,128)(2,1)}, u32[]{:S(2)}, u32[]{:S(2)}) collective-permute-start(bf16[64,2048]{1,0:T(8,128)(2,1)} %slice.263), channel_id=1, source_target_pairs={{0,4},{2,6},{4,0},{6,2},{1,5},{3,7},{5,1},{7,3},{8,12},{10,14},{12... | collective-permute-start | bytes 786440 | tf_op jit(solution)/shard_map/ppermute | solution.py:43
  31.7 17.8 %collective-permute-start = (bf16[64,2048]{1,0:T(8,128)(2,1)}, bf16[64,2048]{1,0:T(8,128)(2,1)}, u32[]{:S(2)}, u32[]{:S(2)}) collective-permute-start(bf16[64,2048]{1,0:T(8,128)(2,1)} %slice.263), channel_id=1, source_target_pairs={{0,6},{2,0},{4,2},{6,4},{1,7},{3,1},{5,3},{7,5},{8,14},{10,8},{12,... | collective-permute-start | bytes 786440 | tf_op jit(solution)/shard_map/ppermute | solution.py:43
  33.1 20.4 %all-to-all-start.1 = ((bf16[8,3,64,256]{3,2,1,0:T(8,128)(2,1)}), bf16[8,3,64,256]{3,2,1,0:T(8,128)(2,1)S(1)}, u32[]{:S(2)}, u32[]{:S(2)}) async-start(bf16[8,3,64,256]{3,2,1,0:T(8,128)(2,1)} %shard_map.294), calls=%async_computation.1 | async-start | bytes 1572864 | tf_op jit(solution)/shard_map/all_to_all | solution.py:55
  53.6 31.0 %all-to-all-start.2 = ((bf16[8,64,1024]{2,1,0:T(8,128)(2,1)}), bf16[8,64,1024]{2,1,0:T(8,128)(2,1)S(1)}, u32[]{:S(2)}, u32[]{:S(2)}) async-start(bf16[8,64,1024]{2,1,0:T(8,128)(2,1)} %shard_map.295), calls=%async_computation.2 | async-start | bytes 2097152 | tf_op jit(solution)/shard_map/all_to_all | solution.py:55
  57.9 117.9 %all-gather.8.cloned.1.call-start = ((), (), s32[]{:S(2)}) async-start(), calls=%async_computation.13 | async-start | bytes 5242880 | tf_op jit(solution)/shard_map/all_gather | solution.py:637
  58.0 24.2 %collective-permute-start.3 = (bf16[128,2048]{1,0:T(8,128)(2,1)S(1)}, bf16[128,2048]{1,0:T(8,128)(2,1)S(1)}, u32[]{:S(2)}, u32[]{:S(2)}) collective-permute-start(bf16[128,2048]{1,0:T(8,128)(2,1)S(1)} %reshape.339), channel_id=1, source_target_pairs={{0,17},{16,0},{1,16},{17,1},{2,19},{18,2},{3,18},{19,3},{4,21},{20... | collective-permute-start | bytes 1572872 | tf_op jit(solution)/shard_map/ppermute | solution.py:43
  85.5 30.6 %all-to-all-start.3 = ((bf16[8,64,1024]{2,1,0:T(8,128)(2,1)}), bf16[8,64,1024]{2,1,0:T(8,128)(2,1)S(1)}, u32[]{:S(2)}, u32[]{:S(2)}) async-start(bf16[8,64,1024]{2,1,0:T(8,128)(2,1)} %shard_map.296), calls=%async_computation.3 | async-start | bytes 2097152 | tf_op jit(solution)/shard_map/all_to_all | solution.py:55
  89.1 116.6 %all-gather.10.cloned.1.call-start = ((), (), s32[]{:S(2)}) async-start(), calls=%async_computation.14 | async-start | bytes 5242880 | tf_op jit(solution)/shard_map/all_gather | solution.py:639
  90.1 24.1 %collective-permute-start.4 = (bf16[128,2048]{1,0:T(8,128)(2,1)S(1)}, bf16[128,2048]{1,0:T(8,128)(2,1)}, u32[]{:S(2)}, u32[]{:S(2)}) collective-permute-start(bf16[128,2048]{1,0:T(8,128)(2,1)S(1)} %reshape.339), channel_id=1, source_target_pairs={{0,1},{16,17},{1,0},{17,16},{2,3},{18,19},{3,2},{19,18},{4,5},{20,... | collective-permute-start | bytes 1572872 | tf_op jit(solution)/shard_map/ppermute | solution.py:43
  91.7 37.9 %collective-permute-start.5 = (bf16[128,2048]{1,0:T(8,128)(2,1)S(1)}, bf16[128,2048]{1,0:T(8,128)(2,1)}, u32[]{:S(2)}, u32[]{:S(2)}) collective-permute-start(bf16[128,2048]{1,0:T(8,128)(2,1)S(1)} %reshape.339), channel_id=1, source_target_pairs={{0,16},{16,1},{1,17},{17,0},{2,18},{18,3},{3,19},{19,2},{4,20},{20... | collective-permute-start | bytes 1572872 | tf_op jit(solution)/shard_map/ppermute | solution.py:43
  116.9 18.7 %collective-permute-start.7 = (bf16[512,768]{1,0:T(8,128)(2,1)S(1)}, bf16[512,768]{1,0:T(8,128)(2,1)S(1)}, u32[]{:S(2)}, u32[]{:S(2)}) collective-permute-start(bf16[512,768]{1,0:T(8,128)(2,1)S(1)} %bitcast.199), channel_id=1, source_target_pairs={{0,6},{2,0},{4,2},{6,4},{1,7},{3,1},{5,3},{7,5},{8,14},{10,8},{12,... | collective-permute-start | bytes 2359304 | tf_op jit(solution)/shard_map/ppermute | solution.py:43
  131.5 32.0 %collective-permute-start.6 = (bf16[512,2048]{1,0:T(8,128)(2,1)}, bf16[512,2048]{1,0:T(8,128)(2,1)}, u32[]{:S(2)}, u32[]{:S(2)}) collective-permute-start(bf16[512,2048]{1,0:T(8,128)(2,1)} %constant_dynamic-update-slice_fusion.mine_ref), channel_id=1, source_target_pairs={{0,8},{8,0},{1,9},{9,1},{2,10},{10,2},{3,11},{11,3},{4,12},{12,4},... | collective-permute-start | bytes 6291464 | tf_op jit(solution)/shard_map/ppermute | solution.py:43
  134.5 155.9 %all-gather.12.cloned.1.call-start = ((), (), s32[]{:S(2)}) async-start(), calls=%async_computation.18 | async-start | bytes 4718592 | tf_op jit(solution)/shard_map/all_gather | solution.py:672
  135.6 20.3 %collective-permute-start.8 = (bf16[512,768]{1,0:T(8,128)(2,1)S(1)}, bf16[512,768]{1,0:T(8,128)(2,1)S(1)}, u32[]{:S(2)}, u32[]{:S(2)}) collective-permute-start(bf16[512,768]{1,0:T(8,128)(2,1)S(1)} %collective-permute-done.7), channel_id=1, source_target_pairs={{0,6},{2,0},{4,2},{6,4},{1,7},{3,1},{5,3},{7,5},{8,14},{10,8},{12,... | collective-permute-start | bytes 2359304 | tf_op jit(solution)/shard_map/ppermute | solution.py:43
  155.9 20.0 %collective-permute-start.9 = (bf16[512,768]{1,0:T(8,128)(2,1)S(1)}, bf16[512,768]{1,0:T(8,128)(2,1)}, u32[]{:S(2)}, u32[]{:S(2)}) collective-permute-start(bf16[512,768]{1,0:T(8,128)(2,1)S(1)} %collective-permute-done.8), channel_id=1, source_target_pairs={{0,6},{2,0},{4,2},{6,4},{1,7},{3,1},{5,3},{7,5},{8,14},{10,8},{12,... | collective-permute-start | bytes 2359304 | tf_op jit(solution)/shard_map/ppermute | solution.py:43
  187.8 4.2 collective-permute-start.10
  205.7 185.8 %reduce-scatter.13.cloned.1.call-start = ((), (), s32[]{:S(2)}) async-start(), calls=%async_computation.19 | async-start | bytes 4718592
  207.3 23.9 %collective-permute-start.11 = (bf16[128,2048]{1,0:T(8,128)(2,1)S(1)}, bf16[128,2048]{1,0:T(8,128)(2,1)S(1)}, u32[]{:S(2)}, u32[]{:S(2)}) collective-permute-start(bf16[128,2048]{1,0:T(8,128)(2,1)S(1)} %get-tuple-element.224), channel_id=1, source_target_pairs={{0,16},{16,1},{1,17},{17,0},{2,18},{18,3},{3,19},{19,2},{4,20},{20... | collective-permute-start | bytes 1572872 | tf_op jit(solution)/shard_map/ppermute | solution.py:43
  208.8 24.3 %collective-permute-start.13 = (bf16[128,2048]{1,0:T(8,128)(2,1)S(1)}, bf16[128,2048]{1,0:T(8,128)(2,1)S(1)}, u32[]{:S(2)}, u32[]{:S(2)}) collective-permute-start(bf16[128,2048]{1,0:T(8,128)(2,1)S(1)} %get-tuple-element.225), channel_id=1, source_target_pairs={{0,17},{16,0},{1,16},{17,1},{2,19},{18,2},{3,18},{19,3},{4,21},{20... | collective-permute-start | bytes 1572872 | tf_op jit(solution)/shard_map/ppermute | solution.py:43
  210.3 24.1 %collective-permute-start.12 = (bf16[128,2048]{1,0:T(8,128)(2,1)S(1)}, bf16[128,2048]{1,0:T(8,128)(2,1)S(1)}, u32[]{:S(2)}, u32[]{:S(2)}) collective-permute-start(bf16[128,2048]{1,0:T(8,128)(2,1)S(1)} %get-tuple-element.226), channel_id=1, source_target_pairs={{0,1},{16,17},{1,0},{17,16},{2,3},{18,19},{3,2},{19,18},{4,5},{20,... | collective-permute-start | bytes 1572872 | tf_op jit(solution)/shard_map/ppermute | solution.py:43
  235.6 27.8 %collective-permute-start.16 = (bf16[128,2048]{1,0:T(8,128)(2,1)S(1)}, bf16[128,2048]{1,0:T(8,128)(2,1)S(1)}, u32[]{:S(2)}, u32[]{:S(2)}) collective-permute-start(bf16[128,2048]{1,0:T(8,128)(2,1)S(1)} %copy.142.refs_0_), channel_id=1, source_target_pairs={{0,2},{2,4},{4,6},{6,0},{1,3},{3,5},{5,7},{7,1},{8,10},{10,12},{12... | collective-permute-start | bytes 1572872 | tf_op jit(solution)/shard_map/ppermute | solution.py:43
  237.2 49.3 %collective-permute-start.15 = (bf16[128,2048]{1,0:T(8,128)(2,1)S(1)}, bf16[128,2048]{1,0:T(8,128)(2,1)S(1)}, u32[]{:S(2)}, u32[]{:S(2)}) collective-permute-start(bf16[128,2048]{1,0:T(8,128)(2,1)S(1)} %copy.142.refs_0_), channel_id=1, source_target_pairs={{0,4},{2,6},{4,0},{6,2},{1,5},{3,7},{5,1},{7,3},{8,12},{10,14},{12... | collective-permute-start | bytes 1572872 | tf_op jit(solution)/shard_map/ppermute | solution.py:43
  239.6 46.9 %collective-permute-start.14 = (bf16[128,2048]{1,0:T(8,128)(2,1)S(1)}, bf16[128,2048]{1,0:T(8,128)(2,1)S(1)}, u32[]{:S(2)}, u32[]{:S(2)}) collective-permute-start(bf16[128,2048]{1,0:T(8,128)(2,1)S(1)} %copy.142.refs_0_), channel_id=1, source_target_pairs={{0,6},{2,0},{4,2},{6,4},{1,7},{3,1},{5,3},{7,5},{8,14},{10,8},{12,... | collective-permute-start | bytes 1572872 | tf_op jit(solution)/shard_map/ppermute | solution.py:43
  290.4 12.0 %collective-permute-start.17 = (bf16[512,2048]{1,0:T(8,128)(2,1)}, bf16[512,2048]{1,0:T(8,128)(2,1)S(1)}, u32[]{:S(2)}, u32[]{:S(2)}) collective-permute-start(bf16[512,2048]{1,0:T(8,128)(2,1)} %bitcast.174), channel_id=1, source_target_pairs={{0,8},{8,0},{1,9},{9,1},{2,10},{10,2},{3,11},{11,3},{4,12},{12,4},... | collective-permute-start | bytes 6291464 | tf_op jit(solution)/shard_map/ppermute | solution.py:43
  331.3 114.4 %reduce-scatter.7.cloned.1.call-start = ((), (), s32[]{:S(2)}) async-start(), calls=%async_computation.15 | async-start | bytes 4718592 | tf_op jit(solution)/shard_map/reduce_scatter | solution.py:684
  392.9 140.8 %reduce-scatter.9.cloned.1.call-start = ((), (), s32[]{:S(2)}) async-start(), calls=%async_computation.16 | async-start | bytes 10485760 | tf_op jit(solution)/shard_map/reduce_scatter | solution.py:684
  395.8 15.8 %collective-permute-start.20 = (bf16[128,2048]{1,0:T(8,128)(2,1)S(1)}, bf16[128,2048]{1,0:T(8,128)(2,1)S(1)}, u32[]{:S(2)}, u32[]{:S(2)}) collective-permute-start(bf16[128,2048]{1,0:T(8,128)(2,1)S(1)} %get-tuple-element.211), channel_id=1, source_target_pairs={{0,16},{16,1},{1,17},{17,0},{2,18},{18,3},{3,19},{19,2},{4,20},{20... | collective-permute-start | bytes 1572872 | tf_op jit(solution)/shard_map/ppermute | solution.py:43
  397.3 14.9 %collective-permute-start.19 = (bf16[128,2048]{1,0:T(8,128)(2,1)S(1)}, bf16[128,2048]{1,0:T(8,128)(2,1)S(1)}, u32[]{:S(2)}, u32[]{:S(2)}) collective-permute-start(bf16[128,2048]{1,0:T(8,128)(2,1)S(1)} %get-tuple-element.211), channel_id=1, source_target_pairs={{0,1},{16,17},{1,0},{17,16},{2,3},{18,19},{3,2},{19,18},{4,5},{20,... | collective-permute-start | bytes 1572872 | tf_op jit(solution)/shard_map/ppermute | solution.py:43
  398.7 20.7 %collective-permute-start.18 = (bf16[128,2048]{1,0:T(8,128)(2,1)S(1)}, bf16[128,2048]{1,0:T(8,128)(2,1)S(1)}, u32[]{:S(2)}, u32[]{:S(2)}) collective-permute-start(bf16[128,2048]{1,0:T(8,128)(2,1)S(1)} %get-tuple-element.211), channel_id=1, source_target_pairs={{0,17},{16,0},{1,16},{17,1},{2,19},{18,2},{3,18},{19,3},{4,21},{20... | collective-permute-start | bytes 1572872 | tf_op jit(solution)/shard_map/ppermute | solution.py:43
  419.6 4.4 collective-permute-start.21
  424.0 195.4 %reduce-scatter.11.cloned.1.call-start = ((), (), s32[]{:S(2)}) async-start(), calls=%async_computation.17 | async-start | bytes 5242880 | tf_op jit(solution)/shard_map/reduce_scatter | solution.py:684
  453.1 10.8 %collective-permute-start.24 = (bf16[512,2048]{1,0:T(8,128)(2,1)}, bf16[512,2048]{1,0:T(8,128)(2,1)}, u32[]{:S(2)}, u32[]{:S(2)}) collective-permute-start(bf16[512,2048]{1,0:T(8,128)(2,1)} %shard_map.306), channel_id=1, source_target_pairs={{0,8},{8,0},{1,9},{9,1},{2,10},{10,2},{3,11},{11,3},{4,12},{12,4},... | collective-permute-start | bytes 6291464 | tf_op jit(solution)/shard_map/ppermute | solution.py:43
  454.5 27.3 %collective-permute-start.22 = (bf16[512,768]{1,0:T(8,128)(2,1)S(1)}, bf16[512,768]{1,0:T(8,128)(2,1)}, u32[]{:S(2)}, u32[]{:S(2)}) collective-permute-start(bf16[512,768]{1,0:T(8,128)(2,1)S(1)} %slice_bitcast_fusion), channel_id=1, source_target_pairs={{0,2},{2,4},{4,6},{6,0},{1,3},{3,5},{5,7},{7,1},{8,10},{10,12},{12... | collective-permute-start | bytes 2359304 | tf_op jit(solution)/shard_map/ppermute | solution.py:43
  455.8 25.9 %collective-permute-start.23 = (bf16[64,2048]{1,0:T(8,128)(2,1)S(1)}, bf16[64,2048]{1,0:T(8,128)(2,1)S(1)}, u32[]{:S(2)}, u32[]{:S(2)}) collective-permute-start(bf16[64,2048]{1,0:T(8,128)(2,1)S(1)} %slice_bitcast_fusion.1), channel_id=1, source_target_pairs={{0,2},{2,4},{4,6},{6,0},{1,3},{3,5},{5,7},{7,1},{8,10},{10,12},{12... | collective-permute-start | bytes 786440 | tf_op jit(solution)/shard_map/ppermute | solution.py:43
  483.1 22.3 %collective-permute-start.28 = (bf16[512,768]{1,0:T(8,128)(2,1)S(1)}, bf16[512,768]{1,0:T(8,128)(2,1)S(1)}, u32[]{:S(2)}, u32[]{:S(2)}) collective-permute-start(bf16[512,768]{1,0:T(8,128)(2,1)S(1)} %fusion.6), channel_id=1, source_target_pairs={{0,2},{2,4},{4,6},{6,0},{1,3},{3,5},{5,7},{7,1},{8,10},{10,12},{12... | collective-permute-start | bytes 2359304 | tf_op jit(solution)/shard_map/ppermute | solution.py:43
  483.3 27.8 %collective-permute-start.30 = (bf16[64,2048]{1,0:T(8,128)(2,1)S(1)}, bf16[64,2048]{1,0:T(8,128)(2,1)S(1)}, u32[]{:S(2)}, u32[]{:S(2)}) collective-permute-start(bf16[64,2048]{1,0:T(8,128)(2,1)S(1)} %fusion.26), channel_id=1, source_target_pairs={{0,2},{2,4},{4,6},{6,0},{1,3},{3,5},{5,7},{7,1},{8,10},{10,12},{12... | collective-permute-start | bytes 786440 | tf_op jit(solution)/shard_map/ppermute | solution.py:43
  505.7 26.4 %collective-permute-start.29 = (bf16[512,768]{1,0:T(8,128)(2,1)S(1)}, bf16[512,768]{1,0:T(8,128)(2,1)S(1)}, u32[]{:S(2)}, u32[]{:S(2)}) collective-permute-start(bf16[512,768]{1,0:T(8,128)(2,1)S(1)} %fusion.5), channel_id=1, source_target_pairs={{0,2},{2,4},{4,6},{6,0},{1,3},{3,5},{5,7},{7,1},{8,10},{10,12},{12... | collective-permute-start | bytes 2359304 | tf_op jit(solution)/shard_map/ppermute | solution.py:43
  511.2 20.9 %collective-permute-start.31 = (bf16[64,2048]{1,0:T(8,128)(2,1)S(1)}, bf16[64,2048]{1,0:T(8,128)(2,1)S(1)}, u32[]{:S(2)}, u32[]{:S(2)}) collective-permute-start(bf16[64,2048]{1,0:T(8,128)(2,1)S(1)} %fusion.25), channel_id=1, source_target_pairs={{0,2},{2,4},{4,6},{6,0},{1,3},{3,5},{5,7},{7,1},{8,10},{10,12},{12... | collective-permute-start | bytes 786440 | tf_op jit(solution)/shard_map/ppermute | solution.py:43
  533.7 52.6 %all-to-all-start.4 = ((bf16[8,64,2048]{2,1,0:T(8,128)(2,1)}), bf16[8,64,2048]{2,1,0:T(8,128)(2,1)S(1)}, u32[]{:S(2)}, u32[]{:S(2)}) async-start(bf16[8,64,2048]{2,1,0:T(8,128)(2,1)} %bitcast.208), calls=%async_computation.6 | async-start | bytes 4194304 | tf_op jit(solution)/shard_map/all_to_all | solution.py:55
  540.4 50.4 %collective-permute-start.25 = (bf16[128,2048]{1,0:T(8,128)(2,1)}, bf16[128,2048]{1,0:T(8,128)(2,1)}, u32[]{:S(2)}, u32[]{:S(2)}) collective-permute-start(bf16[128,2048]{1,0:T(8,128)(2,1)} %get-tuple-element.221), channel_id=1, source_target_pairs={{0,16},{16,1},{1,17},{17,0},{2,18},{18,3},{3,19},{19,2},{4,20},{20... | collective-permute-start | bytes 1572872 | tf_op jit(solution)/shard_map/ppermute | solution.py:43
  542.1 48.7 %collective-permute-start.27 = (bf16[128,2048]{1,0:T(8,128)(2,1)}, bf16[128,2048]{1,0:T(8,128)(2,1)}, u32[]{:S(2)}, u32[]{:S(2)}) collective-permute-start(bf16[128,2048]{1,0:T(8,128)(2,1)} %get-tuple-element.222), channel_id=1, source_target_pairs={{0,17},{16,0},{1,16},{17,1},{2,19},{18,2},{3,18},{19,3},{4,21},{20... | collective-permute-start | bytes 1572872 | tf_op jit(solution)/shard_map/ppermute | solution.py:43
  543.3 47.5 %collective-permute-start.26 = (bf16[128,2048]{1,0:T(8,128)(2,1)}, bf16[128,2048]{1,0:T(8,128)(2,1)}, u32[]{:S(2)}, u32[]{:S(2)}) collective-permute-start(bf16[128,2048]{1,0:T(8,128)(2,1)} %get-tuple-element.223), channel_id=1, source_target_pairs={{0,1},{16,17},{1,0},{17,16},{2,3},{18,19},{3,2},{19,18},{4,5},{20,... | collective-permute-start | bytes 1572872 | tf_op jit(solution)/shard_map/ppermute | solution.py:43
  586.3 27.9 %all-to-all-start.5 = ((bf16[8,3,64,256]{3,2,1,0:T(8,128)(2,1)}), bf16[8,3,64,256]{3,2,1,0:T(8,128)(2,1)}, u32[]{:S(2)}, u32[]{:S(2)}) async-start(bf16[8,3,64,256]{3,2,1,0:T(8,128)(2,1)} %bitcast.166), calls=%async_computation.7 | async-start | bytes 1572864 | tf_op jit(solution)/shard_map/all_to_all | solution.py:55
  615.0 19.9 %all-to-all-start.6 = ((f32[32,1,320]{2,1,0:T(1,128)}), f32[32,1,320]{2,1,0:T(1,128)S(1)}, u32[]{:S(2)}, u32[]{:S(2)}) async-start(f32[32,1,320]{2,1,0:T(1,128)} %reshape.396), calls=%async_computation.9 | async-start | bytes 98304 | tf_op jit(solution)/shard_map/all_to_all | solution.py:55
  640.2 13.0 %all-to-all-start.7 = ((f32[32,8,2]{1,2,0:T(2,128)}), f32[32,8,2]{1,2,0:T(2,128)S(1)}, u32[]{:S(2)}, u32[]{:S(2)}) async-start(f32[32,8,2]{1,2,0:T(2,128)} %broadcast_in_dim.57), calls=%async_computation.10 | async-start | bytes 65536 | tf_op jit(solution)/shard_map/all_to_all | solution.py:55
  (43 other events, 422.0 us)
Sparse Core Ops, SparseCore 0:
  10.5 70.4 all-gather.5
  85.6 64.6 all-gather.7
  152.8 52.8 all-gather.9
  207.1 76.2 all-gather.11
  331.5 59.9 reduce-scatter.12
  394.2 48.1 reduce-scatter.6
  445.4 84.5 reduce-scatter.8
  533.2 81.6 reduce-scatter.10

commit v5 on v4

--- a/solution.py
+++ b/solution.py
@@ -626,9 +626,9 @@
     values = inputs.reshape(own, D).astype(WIDE)
     norm_one, scale_one = norm_forward(values, gain_one)
     low_one = conv_order(norm_one.astype(LOW))
-    cols_p, gate_cols, low_one, *o_pieces = tied(
-        exchanged(p_cols, CONV), prep_feed(sizes, w_in, 4 * D), low_one, *o_pieces
-    )
+    cols_p, low_one, *o_pieces = tied(exchanged(p_cols, CONV), low_one, *o_pieces)
+    later, cols_p = tied(w_in, cols_p)
+    gate_cols = prep_feed(sizes, later, 4 * D)
     h_pieces = [low_one] + near(low_one, LINES)
     gate_cols, up_cols, cols_p, down, h_pieces[1] = tied(
         exchanged(gate_cols, FEED), prep_feed(sizes, w_in, 4 * D + FF), cols_p, down, h_pieces[1]
@@ -636,13 +636,13 @@
     mine, other = with_core(h_pieces)
     gate_w = lax.all_gather(as_rows(gate_cols), FEED_COPIES, axis=0, tiled=True)
     up_cols, cols_p = tied(exchanged(up_cols, FEED), cols_p)
-    up_w = lax.all_gather(as_rows(up_cols), FEED_COPIES, axis=0, tiled=True)
     o_w = placed(o_pieces, "h").reshape(channels, D)
     pieces = [cols_p.swapaxes(1, 2).reshape(-1, 3 * channels)]
     for k in range(1, nh):
         piece = turned(pieces[-1], "h", -1)
         pieces.append(piece)
-    pieces[-1], gate_w = tied(pieces[-1], gate_w)
+    pieces[-1], gate_w, grad_low = tied(pieces[-1], gate_w, grad_low)
+    e_all = lax.all_gather(grad_low, FEED, axis=0)
     p_w = jnp.concatenate(pieces, 0)
 
     line = li * ny + yi
@@ -668,8 +668,8 @@
 
     y_mine, y_other = by_core(y_mix)
     both, sent = scatter(times(y_other, o_w).astype(LOW), lambda: times(y_mine, o_w), LINES)
-    both, up_w, grad_low = tied(both, up_w, grad_low)
-    e_all = lax.all_gather(grad_low, FEED, axis=0)
+    up_cols, e_all, *sent = tied(up_cols, e_all, *sent)
+    up_w = lax.all_gather(as_rows(up_cols), FEED_COPIES, axis=0, tiled=True)
     middle = values + total(both, sent)
 
     norm_two, scale_two = norm_forward(middle, gain_two)

time: 683 us -> 670 us (0.981)
  blocking collectives: 0 us -> 30.8 us
  waiting for transfers between devices: 305 us -> 283 us
  starting transfers between devices: 96.7 us -> 79.5 us
    all_to_all x0 -> x1, blocking collectives: none -> 30.8 us  [exchanged(): return lax.all_to_all(value, axes, 0, 0, tiled=True)]
    ppermute x32, waiting for transfers between devices: 231 us -> 208 us  [turned(): return lax.ppermute(value, ordered if len(names) > 1 else axes, pairs)]
    reduce_scatter x3, starting transfers between devices: 12 us -> 0.3 us  [summed(): return lax.psum_scatter(part, axes, scatter_dimension=0, tiled=True)]
    all_to_all x8 -> x7, waiting for transfers between devices: 48.1 us -> 47.6 us  [exchanged(): return lax.all_to_all(value, axes, 0, 0, tiled=True)]
    all_to_all x8 -> x7, starting transfers between devices: 36.4 us -> 36.5 us  [exchanged(): return lax.all_to_all(value, axes, 0, 0, tiled=True)]
  transfers between devices with their start and end apart: 48 -> 47, of which waited for: 27 -> 26; matrix products, arithmetic and copies ran while one was open for 13% -> 13% of each run, Pallas kernels for 17% -> 17%
where the time goes in v5:
time: 670 us; the launch traced here: 661 us
  waiting for transfers between devices  283 us (42%)
  Pallas kernels  148 us (22%)
  starting transfers between devices  79.5 us (12%)
  other arithmetic  46.2 us (7%)
  local copies, waits for them, and re-layouts  41.6 us (6%)
  blocking collectives  30.8 us (5%)
  matrix products  16.5 us (2%)
  between operations  15.4 us (2%)
    ppermute x32, waiting for transfers between devices, turned(): return lax.ppermute(value, ordered if len(names) > 1 else axes, pairs)  208 us
    all_to_all x7, waiting for transfers between devices, exchanged(): return lax.all_to_all(value, axes, 0, 0, tiled=True)  47.6 us
    ppermute x32, starting transfers between devices, turned(): return lax.ppermute(value, ordered if len(names) > 1 else axes, pairs)  42.3 us
    all_to_all x7, starting transfers between devices, exchanged(): return lax.all_to_all(value, axes, 0, 0, tiled=True)  36.5 us
    all_to_all x1, blocking collectives, exchanged(): return lax.all_to_all(value, axes, 0, 0, tiled=True)  30.8 us
    pallas_call x2, Pallas kernels, both_cores(): pl.pallas_call(functools.partial(both_kernel, len(mine), wide), grid_spec...  26.5 us
    pallas_call x2, Pallas kernels, feed(): pl.pallas_call(feed_kernel, grid_spec=pltpu.PrefetchScalarGridSpec(num_sc...  23.8 us
    pallas_call x2, Pallas kernels, weight_grads(): pl.pallas_call(functools.partial(weight_kernel, parts, outs), grid=(rows...  20.8 us
  transfers between devices with their start and end apart: 47, of which 26 were waited for; matrix products, arithmetic and copies ran while one was open for 13% of the time, Pallas kernels for 17%

profile of v5, /device:TPU:0, one launch (start us, length us, event | category | flops | bytes accessed | tf_op | source)
XLA Modules:
  0.0 661.2 jit_solution(17618744924044750407)
XLA Ops:
  11.3 7.3 %all-to-all-start = ((f32[32,1,448]{2,1,0:T(1,128)}), f32[32,1,448]{2,1,0:T(1,128)S(1)}, u32[]{:S(2)}, u32[]{:S(2)}) async-start(f32[32,1,448]{2,1,0:T(1,128)} %broadcast_in_dim.22), calls=%async_computation | async-start | bytes 131072 | tf_op jit(solution)/shard_map/all_to_all | solution.py:55
  30.7 3.7 all-to-all-start.1
  37.8 9.9 %collective-permute-done.1 = bf16[64,2048]{1,0:T(8,128)(2,1)} collective-permute-done((bf16[64,2048]{1,0:T(8,128)(2,1)}, bf16[64,2048]{1,0:T(8,128)(2,1)}, u32[]{:S(2)}, u32[]{:S(2)}) %collective-permute-start.1) | collective-permute-done | bytes 262176 | tf_op jit(solution)/shard_map/ppermute | solution.py:43
  50.1 7.7 %all-to-all-start.2 = ((bf16[8,64,1024]{2,1,0:T(8,128)(2,1)}), bf16[8,64,1024]{2,1,0:T(8,128)(2,1)S(1)}, u32[]{:S(2)}, u32[]{:S(2)}) async-start(bf16[8,64,1024]{2,1,0:T(8,128)(2,1)} %shard_map.295), calls=%async_computation.2 | async-start | bytes 2097152 | tf_op jit(solution)/shard_map/all_to_all | solution.py:55
  62.8 17.0 %collective-permute-done.3 = bf16[128,2048]{1,0:T(8,128)(2,1)S(1)} collective-permute-done((bf16[128,2048]{1,0:T(8,128)(2,1)S(1)}, bf16[128,2048]{1,0:T(8,128)(2,1)S(1)}, u32[]{:S(2)}, u32[]{:S(2)}) %collective-permute-start.3) | collective-permute-done | bytes 524320 | tf_op jit(solution)/shard_map/ppermute | solution.py:43
  79.7 4.7 all-to-all-done.2
  85.5 30.8 %all_to_all.44 = bf16[8,64,1024]{2,1,0:T(8,128)(2,1)} all-to-all(bf16[8,64,1024]{2,1,0:T(8,128)(2,1)} %shard_map.296), channel_id=1, replica_groups=mesh['y'=2,'c'=2,'h'=4,'l'=2] {'h','c'}, dimensions={0} | all-to-all | bytes 2097152 | tf_op jit(solution)/shard_map/all_to_all | solution.py:55
  120.8 15.4 %collective-permute-done.7 = bf16[512,768]{1,0:T(8,128)(2,1)S(1)} collective-permute-done((bf16[512,768]{1,0:T(8,128)(2,1)S(1)}, bf16[512,768]{1,0:T(8,128)(2,1)S(1)}, u32[]{:S(2)}, u32[]{:S(2)}) %collective-permute-start.7) | collective-permute-done | bytes 786464 | tf_op jit(solution)/shard_map/ppermute | solution.py:43
  136.2 3.6 collective-permute-start.8
  146.9 9.1 %collective-permute-done.8 = bf16[512,768]{1,0:T(8,128)(2,1)} collective-permute-done((bf16[512,768]{1,0:T(8,128)(2,1)S(1)}, bf16[512,768]{1,0:T(8,128)(2,1)}, u32[]{:S(2)}, u32[]{:S(2)}) %collective-permute-start.8) | collective-permute-done | bytes 786464 | tf_op jit(solution)/shard_map/ppermute | solution.py:43
  156.0 4.4 collective-permute-start.9
  162.6 13.4 %collective-permute-done.9 = bf16[512,768]{1,0:T(8,128)(2,1)} collective-permute-done((bf16[512,768]{1,0:T(8,128)(2,1)}, bf16[512,768]{1,0:T(8,128)(2,1)}, u32[]{:S(2)}, u32[]{:S(2)}) %collective-permute-start.9) | collective-permute-done | bytes 786464 | tf_op jit(solution)/shard_map/ppermute | solution.py:43
  179.3 5.4 shard_map.297
  194.3 4.1 collective-permute-done.10
  205.0 11.2 %collective-permute-done.13 = bf16[128,2048]{1,0:T(8,128)(2,1)S(1)} collective-permute-done((bf16[128,2048]{1,0:T(8,128)(2,1)S(1)}, bf16[128,2048]{1,0:T(8,128)(2,1)S(1)}, u32[]{:S(2)}, u32[]{:S(2)}) %collective-permute-start.13) | collective-permute-done | bytes 524320 | tf_op jit(solution)/shard_map/ppermute | solution.py:43
  216.3 11.5 %collective-permute-done.12 = bf16[128,2048]{1,0:T(8,128)(2,1)} collective-permute-done((bf16[128,2048]{1,0:T(8,128)(2,1)S(1)}, bf16[128,2048]{1,0:T(8,128)(2,1)}, u32[]{:S(2)}, u32[]{:S(2)}) %collective-permute-start.12) | collective-permute-done | bytes 524320 | tf_op jit(solution)/shard_map/ppermute | solution.py:43
  230.8 4.7 collective-permute-start.15
  235.9 12.0 %collective-permute-done.16.refs_3_ = bf16[128,2048]{1,0:T(8,128)(2,1)S(1)} collective-permute-done((bf16[128,2048]{1,0:T(8,128)(2,1)S(1)}, bf16[128,2048]{1,0:T(8,128)(2,1)S(1)}, u32[]{:S(2)}, u32[]{:S(2)}) %collective-permute-start.16) | collective-permute-done | bytes 524320 | tf_op jit(solution)/shard_map/ppermute | solution.py:43
  248.0 20.8 %collective-permute-done.15.refs_2_ = bf16[128,2048]{1,0:T(8,128)(2,1)S(1)} collective-permute-done((bf16[128,2048]{1,0:T(8,128)(2,1)S(1)}, bf16[128,2048]{1,0:T(8,128)(2,1)S(1)}, u32[]{:S(2)}, u32[]{:S(2)}) %collective-permute-start.15) | collective-permute-done | bytes 524320 | tf_op jit(solution)/shard_map/ppermute | solution.py:43
  272.7 9.6 %all-gather.10.cloned.1.call-done.u_ref.refs_5_ = bf16[2048,1024]{1,0:T(8,128)(2,1)} async-done(((bf16[512,1024]{1,0:T(8,128)(2,1)}), bf16[2048,1024]{1,0:T(8,128)(2,1)}) %all-gather.10.cloned.1.call-update) | async-done | bytes 4194320 | tf_op jit(solution)/shard_map/all_gather | solution.py:672
  282.3 11.9 %shard_map.299 = (bf16[512,1024]{1,0:T(8,128)(2,1)}, bf16[512,1024]{1,0:T(8,128)(2,1)}, bf16[512,1024]{1,0:T(8,128)(2,1)}) custom-call(s32[1]{0:T(128)} %bitcast.2.c_ref, bf16[512,2048]{1,0:T(8,128)(2,1)} %bitcast.176, bf16[4,2,128,2048]{3,2,1,0:T(8,128)(2,1)} %bitcast.171, bf16[2048,1024]{1,0:T(8,128)(2,1)} %all-gather.8.cloned.1.call-done.g_ref.refs_4_, ...), custom_call_target="tpu_custom_call" | custom-call | flops 1024 | bytes 1024 | tf_op jit(solution)/shard_map/pallas_call | solution.py:178
  294.2 12.0 %shard_map.300 = (bf16[512,1024]{1,0:T(8,128)(2,1)}, bf16[512,1024]{1,0:T(8,128)(2,1)}, bf16[512,1024]{1,0:T(8,128)(2,1)}) custom-call(s32[1]{0:T(128)S(6)} %sub.9.c_ref, bf16[512,2048]{1,0:T(8,128)(2,1)} %collective-permute-done.17.h_ref.refs_1_, bf16[4,2,128,2048]{3,2,1,0:T(8,128)(2,1)} %bitcast.172, ...), custom_call_target="tpu_custom_call" | custom-call | flops 1024 | bytes 1024 | tf_op jit(solution)/shard_map/pallas_call | solution.py:178
  306.2 15.6 %shard_map.301 = bf16[4,2,128,2048]{3,2,1,0:T(8,128)(2,1)} custom-call(s32[1]{0:T(128)} %bitcast.2.c_ref, bf16[512,1024]{1,0:T(8,128)(2,1)} %get-tuple-element.132.refs_0_.refs_2_, bf16[512,1024]{1,0:T(8,128)(2,1)} %get-tuple-element.133.refs_1_.refs_3_, bf16[512,1024]{1,0:T(8,128)(2,1)} %get-tuple-element.134.refs_2_.refs_4_, ...), custom_call_target="tpu_custom_call" | custom-call | flops 1024 | bytes 1024 | tf_op jit(solution)/shard_map/pallas_call | solution.py:286
  321.9 13.4 %shard_map.302 = bf16[2048,2048]{1,0:T(8,128)(2,1)} custom-call(bf16[512,2048]{1,0:T(8,128)(2,1)} %bitcast.177, bf16[512,2048]{1,0:T(8,128)(2,1)} %collective-permute-done.17.h_ref.refs_1_, bf16[512,1024]{1,0:T(8,128)(2,1)} %get-tuple-element.132.refs_0_.refs_2_, bf16[512,1024]{1,0:T(8,128)(2,1)} %get-tuple-element.133.refs_1_.refs_3_, ...), custom_call_target="tpu_custom_call" | custom-call | flops 1024 | bytes 1024 | tf_op jit(solution)/shard_map/pallas_call | solution.py:322
  335.3 10.9 %shard_map.304 = bf16[4,2,128,2048]{3,2,1,0:T(8,128)(2,1)} custom-call(s32[1]{0:T(128)} %bitcast.2.c_ref, bf16[512,1024]{1,0:T(8,128)(2,1)} %get-tuple-element.139.mine_ref.refs_0_, bf16[512,1024]{1,0:T(8,128)(2,1)} %get-tuple-element.140.other_ref.refs_1_, bf16[1024,2048]{1,0:T(8,128)(2,1)} %all-gather.6.cloned.1.call-done.d_ref.refs_2_), custom_call_target="tpu_custom_call" | custom-call | flops 1024 | bytes 1024 | tf_op jit(solution)/shard_map/pallas_call | solution.py:286
  346.2 8.8 %shard_map.303 = bf16[1024,2048]{1,0:T(8,128)(2,1)} custom-call(s32[1]{0:T(128)} %bitcast.2.c_ref, bf16[512,1024]{1,0:T(8,128)(2,1)} %get-tuple-element.139.mine_ref.refs_0_, bf16[512,1024]{1,0:T(8,128)(2,1)} %get-tuple-element.140.other_ref.refs_1_, bf16[4,2,128,2048]{3,2,1,0:T(8,128)(2,1)} %bitcast.173, bf16[4,2,128,2048]{3,2,1,0:T(8,128)(2,1)} %bitcast.174), custom_call_target="tpu_custom_call" | custom-call | flops 1024 | bytes 1024 | tf_op jit(solution)/shard_map/pallas_call | solution.py:213
  355.0 17.3 %reduce-scatter.13.cloned.1.call-done = bf16[128,2048]{1,0:T(8,128)(2,1)} async-done(((bf16[1024,2048]{1,0:T(8,128)(2,1)}), bf16[128,2048]{1,0:T(8,128)(2,1)}) %reduce-scatter.13.cloned.1.call-update) | async-done | bytes 524304
  384.9 11.4 %collective-permute-done.20 = bf16[128,2048]{1,0:T(8,128)(2,1)S(1)} collective-permute-done((bf16[128,2048]{1,0:T(8,128)(2,1)S(1)}, bf16[128,2048]{1,0:T(8,128)(2,1)S(1)}, u32[]{:S(2)}, u32[]{:S(2)}) %collective-permute-start.20) | collective-permute-done | bytes 524320 | tf_op jit(solution)/shard_map/ppermute | solution.py:43
  396.9 7.3 %collective-permute-done.18 = bf16[128,2048]{1,0:T(8,128)(2,1)S(1)} collective-permute-done((bf16[128,2048]{1,0:T(8,128)(2,1)S(1)}, bf16[128,2048]{1,0:T(8,128)(2,1)S(1)}, u32[]{:S(2)}, u32[]{:S(2)}) %collective-permute-start.18) | collective-permute-done | bytes 524320 | tf_op jit(solution)/shard_map/ppermute | solution.py:43
  405.8 4.4 collective-permute-done.21
  418.9 7.4 %shard_map.305 = bf16[2048,768]{1,0:T(8,128)(2,1)} custom-call(bf16[1024,2048]{1,0:T(8,128)(2,1)} %bitcast.179, bf16[1024,768]{1,0:T(8,128)(2,1)} %pad_maximum_fusion.1.refs_1_), custom_call_target="tpu_custom_call" | custom-call | flops 1024 | bytes 1024 | tf_op jit(solution)/shard_map/pallas_call | solution.py:322
  434.1 5.4 shard_map.306
  444.7 5.7 shard_map.307
  450.4 5.5 fusion.38
  456.9 11.3 %collective-permute-done.23 = bf16[64,2048]{1,0:T(8,128)(2,1)S(1)} collective-permute-done((bf16[64,2048]{1,0:T(8,128)(2,1)S(1)}, bf16[64,2048]{1,0:T(8,128)(2,1)S(1)}, u32[]{:S(2)}, u32[]{:S(2)}) %collective-permute-start.23) | collective-permute-done | bytes 262176 | tf_op jit(solution)/shard_map/ppermute | solution.py:43
  471.4 20.6 %collective-permute-done.28 = bf16[512,768]{1,0:T(8,128)(2,1)S(1)} collective-permute-done((bf16[512,768]{1,0:T(8,128)(2,1)S(1)}, bf16[512,768]{1,0:T(8,128)(2,1)S(1)}, u32[]{:S(2)}, u32[]{:S(2)}) %collective-permute-start.28) | collective-permute-done | bytes 786464 | tf_op jit(solution)/shard_map/ppermute | solution.py:43
  492.3 5.3 collective-permute-done.30
  497.8 20.8 %collective-permute-done.31 = bf16[64,2048]{1,0:T(8,128)(2,1)S(1)} collective-permute-done((bf16[64,2048]{1,0:T(8,128)(2,1)S(1)}, bf16[64,2048]{1,0:T(8,128)(2,1)S(1)}, u32[]{:S(2)}, u32[]{:S(2)}) %collective-permute-start.31) | collective-permute-done | bytes 262176 | tf_op jit(solution)/shard_map/ppermute | solution.py:43
  520.3 3.6 all-to-all-start.4
  536.8 36.0 %all-to-all-done.4 = bf16[8,64,2048]{2,1,0:T(8,128)(2,1)S(1)} async-done(((bf16[8,64,2048]{2,1,0:T(8,128)(2,1)}), bf16[8,64,2048]{2,1,0:T(8,128)(2,1)S(1)}, u32[]{:S(2)}, u32[]{:S(2)}) %all-to-all-start.4) | async-done | bytes 2097184 | tf_op jit(solution)/shard_map/all_to_all | solution.py:55
  572.9 4.5 all-to-all-start.5
  586.2 14.6 %shard_map.309 = (f32[64,24576]{1,0:T(8,128)}, f32[64,24576]{1,0:T(8,128)}, f32[64,24576]{1,0:T(8,128)}, f32[64,24576]{1,0:T(8,128)}, f32[2,2,8,128]{3,2,1,0:T(8,128)}) custom-call(f32[64,24576]{1,0:T(8,128)} %w_ref.14, f32[64,24576]{1,0:T(8,128)} %m_ref.6, ...), custom_call_target="tpu_custom_call", output_to_operand_aliasing={{0}: (4, {}), {1}: (5, {}), {2}: (6, {}), {3}: (7, {})} | custom-call | flops 1024 | bytes 1024 | tf_op jit(solution)/shard_map/pallas_call | solution.py:423
  601.6 3.8 all-to-all-start.6
  606.2 7.5 %shard_map.311 = (f32[256,2048]{1,0:T(8,128)}, f32[256,2048]{1,0:T(8,128)}, f32[256,2048]{1,0:T(8,128)}, f32[256,2048]{1,0:T(8,128)}, f32[1,2,8,128]{3,2,1,0:T(8,128)}) custom-call(f32[256,2048]{1,0:T(8,128)} %w_ref.13, f32[256,2048]{1,0:T(8,128)} %m_ref.7, f32[256,2048]{1,0:T(8,128)} %v_ref.7, bf16[256,2048]{1,0:T(8,128)(2,1)} %reduce-scatter.11.cloned.1.call-done.g_ref), custom_call_target="tpu_custom_call" | custom-call | flops 1024 | bytes 1024 | tf_op jit(solution)/shard_map/pallas_call | solution.py:465
  613.8 6.9 %shard_map.310 = (f32[64,24576]{1,0:T(8,128)}, f32[64,24576]{1,0:T(8,128)}, f32[64,24576]{1,0:T(8,128)}, f32[64,24576]{1,0:T(8,128)}, f32[1,2,8,128]{3,2,1,0:T(8,128)}) custom-call(f32[64,24576]{1,0:T(8,128)} %w_ref.14, f32[64,24576]{1,0:T(8,128)} %m_ref.6, ...), custom_call_target="tpu_custom_call", output_to_operand_aliasing={{0}: (4, {}), {1}: (5, {}), {2}: (6, {}), {3}: (7, {})} | custom-call | flops 1024 | bytes 1024 | tf_op jit(solution)/shard_map/pallas_call | solution.py:492
  627.1 5.8 all-to-all-start.7
  634.4 5.7 all-to-all-done.7
  642.1 8.5 %shard_map.312 = f32[64,24576]{1,0:T(8,128)} custom-call(f32[4]{0:T(128)} %slice_bitcast_fusion.3.ratio_ref, f32[64,24576]{1,0:T(8,128)} %w_ref.14, f32[64,24576]{1,0:T(8,128)} %get-tuple-element.191.dir_ref), custom_call_target="tpu_custom_call" | custom-call | flops 1024 | bytes 1024 | tf_op jit(solution)/shard_map/pallas_call | solution.py:518
  (281 shorter events, 147.1 us)
Async XLA Ops:
  7.2 77.2 %all-gather.6.cloned.1.call-start = ((), (), s32[]{:S(2)}) async-start(), calls=%async_computation.12 | async-start | bytes 5242880 | tf_op jit(solution)/shard_map/all_gather | solution.py:625
  11.3 14.7 %all-to-all-start = ((f32[32,1,448]{2,1,0:T(1,128)}), f32[32,1,448]{2,1,0:T(1,128)S(1)}, u32[]{:S(2)}, u32[]{:S(2)}) async-start(f32[32,1,448]{2,1,0:T(1,128)} %broadcast_in_dim.22), calls=%async_computation | async-start | bytes 131072 | tf_op jit(solution)/shard_map/all_to_all | solution.py:55
  26.0 11.8 %collective-permute-start.2 = (bf16[64,2048]{1,0:T(8,128)(2,1)}, bf16[64,2048]{1,0:T(8,128)(2,1)}, u32[]{:S(2)}, u32[]{:S(2)}) collective-permute-start(bf16[64,2048]{1,0:T(8,128)(2,1)} %slice.270), channel_id=1, source_target_pairs={{0,2},{2,4},{4,6},{6,0},{1,3},{3,5},{5,7},{7,1},{8,10},{10,12},{12... | collective-permute-start | bytes 786440 | tf_op jit(solution)/shard_map/ppermute | solution.py:43
  26.9 20.9 %collective-permute-start.1 = (bf16[64,2048]{1,0:T(8,128)(2,1)}, bf16[64,2048]{1,0:T(8,128)(2,1)}, u32[]{:S(2)}, u32[]{:S(2)}) collective-permute-start(bf16[64,2048]{1,0:T(8,128)(2,1)} %slice.270), channel_id=1, source_target_pairs={{0,4},{2,6},{4,0},{6,2},{1,5},{3,7},{5,1},{7,3},{8,12},{10,14},{12... | collective-permute-start | bytes 786440 | tf_op jit(solution)/shard_map/ppermute | solution.py:43
  29.3 18.5 %collective-permute-start = (bf16[64,2048]{1,0:T(8,128)(2,1)}, bf16[64,2048]{1,0:T(8,128)(2,1)}, u32[]{:S(2)}, u32[]{:S(2)}) collective-permute-start(bf16[64,2048]{1,0:T(8,128)(2,1)} %slice.270), channel_id=1, source_target_pairs={{0,6},{2,0},{4,2},{6,4},{1,7},{3,1},{5,3},{7,5},{8,14},{10,8},{12,... | collective-permute-start | bytes 786440 | tf_op jit(solution)/shard_map/ppermute | solution.py:43
  30.7 17.0 %all-to-all-start.1 = ((bf16[8,3,64,256]{3,2,1,0:T(8,128)(2,1)}), bf16[8,3,64,256]{3,2,1,0:T(8,128)(2,1)S(1)}, u32[]{:S(2)}, u32[]{:S(2)}) async-start(bf16[8,3,64,256]{3,2,1,0:T(8,128)(2,1)} %shard_map.294), calls=%async_computation.1 | async-start | bytes 1572864 | tf_op jit(solution)/shard_map/all_to_all | solution.py:55
  50.1 34.3 %all-to-all-start.2 = ((bf16[8,64,1024]{2,1,0:T(8,128)(2,1)}), bf16[8,64,1024]{2,1,0:T(8,128)(2,1)S(1)}, u32[]{:S(2)}, u32[]{:S(2)}) async-start(bf16[8,64,1024]{2,1,0:T(8,128)(2,1)} %shard_map.295), calls=%async_computation.2 | async-start | bytes 2097152 | tf_op jit(solution)/shard_map/all_to_all | solution.py:55
  57.9 118.1 %all-gather.8.cloned.1.call-start = ((), (), s32[]{:S(2)}) async-start(), calls=%async_computation.13 | async-start | bytes 5242880 | tf_op jit(solution)/shard_map/all_gather | solution.py:637
  57.9 21.8 %collective-permute-start.3 = (bf16[128,2048]{1,0:T(8,128)(2,1)S(1)}, bf16[128,2048]{1,0:T(8,128)(2,1)S(1)}, u32[]{:S(2)}, u32[]{:S(2)}) collective-permute-start(bf16[128,2048]{1,0:T(8,128)(2,1)S(1)} %reshape.339), channel_id=1, source_target_pairs={{0,17},{16,0},{1,16},{17,1},{2,19},{18,2},{3,18},{19,3},{4,21},{20... | collective-permute-start | bytes 1572872 | tf_op jit(solution)/shard_map/ppermute | solution.py:43
  85.5 142.5 %all-gather.12.cloned.1.call-start = ((), (), s32[]{:S(2)}) async-start(), calls=%async_computation.18 | async-start | bytes 4718592 | tf_op jit(solution)/shard_map/all_gather | solution.py:645
  117.2 19.0 %collective-permute-start.7 = (bf16[512,768]{1,0:T(8,128)(2,1)S(1)}, bf16[512,768]{1,0:T(8,128)(2,1)S(1)}, u32[]{:S(2)}, u32[]{:S(2)}) collective-permute-start(bf16[512,768]{1,0:T(8,128)(2,1)S(1)} %bitcast.202), channel_id=1, source_target_pairs={{0,6},{2,0},{4,2},{6,4},{1,7},{3,1},{5,3},{7,5},{8,14},{10,8},{12,... | collective-permute-start | bytes 2359304 | tf_op jit(solution)/shard_map/ppermute | solution.py:43
  119.3 25.7 %collective-permute-start.4 = (bf16[128,2048]{1,0:T(8,128)(2,1)S(1)}, bf16[128,2048]{1,0:T(8,128)(2,1)}, u32[]{:S(2)}, u32[]{:S(2)}) collective-permute-start(bf16[128,2048]{1,0:T(8,128)(2,1)S(1)} %reshape.339), channel_id=1, source_target_pairs={{0,1},{16,17},{1,0},{17,16},{2,3},{18,19},{3,2},{19,18},{4,5},{20,... | collective-permute-start | bytes 1572872 | tf_op jit(solution)/shard_map/ppermute | solution.py:43
  136.2 19.8 %collective-permute-start.8 = (bf16[512,768]{1,0:T(8,128)(2,1)S(1)}, bf16[512,768]{1,0:T(8,128)(2,1)}, u32[]{:S(2)}, u32[]{:S(2)}) collective-permute-start(bf16[512,768]{1,0:T(8,128)(2,1)S(1)} %collective-permute-done.7), channel_id=1, source_target_pairs={{0,6},{2,0},{4,2},{6,4},{1,7},{3,1},{5,3},{7,5},{8,14},{10,8},{12,... | collective-permute-start | bytes 2359304 | tf_op jit(solution)/shard_map/ppermute | solution.py:43
  140.0 20.4 %collective-permute-start.5 = (bf16[128,2048]{1,0:T(8,128)(2,1)S(1)}, bf16[128,2048]{1,0:T(8,128)(2,1)S(1)}, u32[]{:S(2)}, u32[]{:S(2)}) collective-permute-start(bf16[128,2048]{1,0:T(8,128)(2,1)S(1)} %reshape.339), channel_id=1, source_target_pairs={{0,16},{16,1},{1,17},{17,0},{2,18},{18,3},{3,19},{19,2},{4,20},{20... | collective-permute-start | bytes 1572872 | tf_op jit(solution)/shard_map/ppermute | solution.py:43
  156.0 20.0 %collective-permute-start.9 = (bf16[512,768]{1,0:T(8,128)(2,1)}, bf16[512,768]{1,0:T(8,128)(2,1)}, u32[]{:S(2)}, u32[]{:S(2)}) collective-permute-start(bf16[512,768]{1,0:T(8,128)(2,1)} %collective-permute-done.8), channel_id=1, source_target_pairs={{0,6},{2,0},{4,2},{6,4},{1,7},{3,1},{5,3},{7,5},{8,14},{10,8},{12,... | collective-permute-start | bytes 2359304 | tf_op jit(solution)/shard_map/ppermute | solution.py:43
  161.2 18.0 %collective-permute-start.6 = (bf16[512,2048]{1,0:T(8,128)(2,1)}, bf16[512,2048]{1,0:T(8,128)(2,1)}, u32[]{:S(2)}, u32[]{:S(2)}) collective-permute-start(bf16[512,2048]{1,0:T(8,128)(2,1)} %constant_dynamic-update-slice_fusion.mine_ref), channel_id=1, source_target_pairs={{0,8},{8,0},{1,9},{9,1},{2,10},{10,2},{3,11},{11,3},{4,12},{12,4},... | collective-permute-start | bytes 6291464 | tf_op jit(solution)/shard_map/ppermute | solution.py:43
  176.0 106.3 %all-gather.10.cloned.1.call-start = ((), (), s32[]{:S(2)}) async-start(), calls=%async_computation.14 | async-start | bytes 5242880 | tf_op jit(solution)/shard_map/all_gather | solution.py:672
  194.3 4.2 collective-permute-start.10
  201.4 14.8 %collective-permute-start.13 = (bf16[128,2048]{1,0:T(8,128)(2,1)S(1)}, bf16[128,2048]{1,0:T(8,128)(2,1)S(1)}, u32[]{:S(2)}, u32[]{:S(2)}) collective-permute-start(bf16[128,2048]{1,0:T(8,128)(2,1)S(1)} %get-tuple-element.232), channel_id=1, source_target_pairs={{0,17},{16,0},{1,16},{17,1},{2,19},{18,2},{3,18},{19,3},{4,21},{20... | collective-permute-start | bytes 1572872 | tf_op jit(solution)/shard_map/ppermute | solution.py:43
  203.9 23.9 %collective-permute-start.12 = (bf16[128,2048]{1,0:T(8,128)(2,1)S(1)}, bf16[128,2048]{1,0:T(8,128)(2,1)}, u32[]{:S(2)}, u32[]{:S(2)}) collective-permute-start(bf16[128,2048]{1,0:T(8,128)(2,1)S(1)} %get-tuple-element.233), channel_id=1, source_target_pairs={{0,1},{16,17},{1,0},{17,16},{2,3},{18,19},{3,2},{19,18},{4,5},{20,... | collective-permute-start | bytes 1572872 | tf_op jit(solution)/shard_map/ppermute | solution.py:43
  204.5 23.5 %collective-permute-start.11 = (bf16[128,2048]{1,0:T(8,128)(2,1)S(1)}, bf16[128,2048]{1,0:T(8,128)(2,1)}, u32[]{:S(2)}, u32[]{:S(2)}) collective-permute-start(bf16[128,2048]{1,0:T(8,128)(2,1)S(1)} %get-tuple-element.234), channel_id=1, source_target_pairs={{0,16},{16,1},{1,17},{17,0},{2,18},{18,3},{3,19},{19,2},{4,20},{20... | collective-permute-start | bytes 1572872 | tf_op jit(solution)/shard_map/ppermute | solution.py:43
  228.0 144.3 %reduce-scatter.13.cloned.1.call-start = ((), (), s32[]{:S(2)}) async-start(), calls=%async_computation.19 | async-start | bytes 4718592
  230.7 38.0 %copy-start.21 = (bf16[128,2048]{1,0:T(8,128)(2,1)}, bf16[128,2048]{1,0:T(8,128)(2,1)S(1)}, u32[]{:S(2)}) copy-start(bf16[128,2048]{1,0:T(8,128)(2,1)S(1)} %copy.142.refs_0_) | copy-start | bytes 1572868
  230.8 17.2 %collective-permute-start.16 = (bf16[128,2048]{1,0:T(8,128)(2,1)S(1)}, bf16[128,2048]{1,0:T(8,128)(2,1)S(1)}, u32[]{:S(2)}, u32[]{:S(2)}) collective-permute-start(bf16[128,2048]{1,0:T(8,128)(2,1)S(1)} %copy.142.refs_0_), channel_id=1, source_target_pairs={{0,2},{2,4},{4,6},{6,0},{1,3},{3,5},{5,7},{7,1},{8,10},{10,12},{12... | collective-permute-start | bytes 1572872 | tf_op jit(solution)/shard_map/ppermute | solution.py:43
  230.8 37.9 %collective-permute-start.15 = (bf16[128,2048]{1,0:T(8,128)(2,1)S(1)}, bf16[128,2048]{1,0:T(8,128)(2,1)S(1)}, u32[]{:S(2)}, u32[]{:S(2)}) collective-permute-start(bf16[128,2048]{1,0:T(8,128)(2,1)S(1)} %copy.142.refs_0_), channel_id=1, source_target_pairs={{0,4},{2,6},{4,0},{6,2},{1,5},{3,7},{5,1},{7,3},{8,12},{10,14},{12... | collective-permute-start | bytes 1572872 | tf_op jit(solution)/shard_map/ppermute | solution.py:43
  235.5 33.2 %collective-permute-start.14 = (bf16[128,2048]{1,0:T(8,128)(2,1)S(1)}, bf16[128,2048]{1,0:T(8,128)(2,1)S(1)}, u32[]{:S(2)}, u32[]{:S(2)}) collective-permute-start(bf16[128,2048]{1,0:T(8,128)(2,1)S(1)} %copy.142.refs_0_), channel_id=1, source_target_pairs={{0,6},{2,0},{4,2},{6,4},{1,7},{3,1},{5,3},{7,5},{8,14},{10,8},{12,... | collective-permute-start | bytes 1572872 | tf_op jit(solution)/shard_map/ppermute | solution.py:43
  272.7 21.5 %collective-permute-start.17 = (bf16[512,2048]{1,0:T(8,128)(2,1)}, bf16[512,2048]{1,0:T(8,128)(2,1)}, u32[]{:S(2)}, u32[]{:S(2)}) collective-permute-start(bf16[512,2048]{1,0:T(8,128)(2,1)} %bitcast.175), channel_id=1, source_target_pairs={{0,8},{8,0},{1,9},{9,1},{2,10},{10,2},{3,11},{11,3},{4,12},{12,4},... | collective-permute-start | bytes 6291464 | tf_op jit(solution)/shard_map/ppermute | solution.py:43
  321.8 110.6 %reduce-scatter.7.cloned.1.call-start = ((), (), s32[]{:S(2)}) async-start(), calls=%async_computation.15 | async-start | bytes 4718592 | tf_op jit(solution)/shard_map/reduce_scatter | solution.py:684
  375.5 144.8 %reduce-scatter.9.cloned.1.call-start = ((), (), s32[]{:S(2)}) async-start(), calls=%async_computation.16 | async-start | bytes 10485760 | tf_op jit(solution)/shard_map/reduce_scatter | solution.py:684
  380.5 15.8 %collective-permute-start.20 = (bf16[128,2048]{1,0:T(8,128)(2,1)S(1)}, bf16[128,2048]{1,0:T(8,128)(2,1)S(1)}, u32[]{:S(2)}, u32[]{:S(2)}) collective-permute-start(bf16[128,2048]{1,0:T(8,128)(2,1)S(1)} %get-tuple-element.219), channel_id=1, source_target_pairs={{0,16},{16,1},{1,17},{17,0},{2,18},{18,3},{3,19},{19,2},{4,20},{20... | collective-permute-start | bytes 1572872 | tf_op jit(solution)/shard_map/ppermute | solution.py:43
  382.0 14.9 %collective-permute-start.19 = (bf16[128,2048]{1,0:T(8,128)(2,1)S(1)}, bf16[128,2048]{1,0:T(8,128)(2,1)S(1)}, u32[]{:S(2)}, u32[]{:S(2)}) collective-permute-start(bf16[128,2048]{1,0:T(8,128)(2,1)S(1)} %get-tuple-element.219), channel_id=1, source_target_pairs={{0,1},{16,17},{1,0},{17,16},{2,3},{18,19},{3,2},{19,18},{4,5},{20,... | collective-permute-start | bytes 1572872 | tf_op jit(solution)/shard_map/ppermute | solution.py:43
  383.5 20.7 %collective-permute-start.18 = (bf16[128,2048]{1,0:T(8,128)(2,1)S(1)}, bf16[128,2048]{1,0:T(8,128)(2,1)S(1)}, u32[]{:S(2)}, u32[]{:S(2)}) collective-permute-start(bf16[128,2048]{1,0:T(8,128)(2,1)S(1)} %get-tuple-element.219), channel_id=1, source_target_pairs={{0,17},{16,0},{1,16},{17,1},{2,19},{18,2},{3,18},{19,3},{4,21},{20... | collective-permute-start | bytes 1572872 | tf_op jit(solution)/shard_map/ppermute | solution.py:43
  405.7 4.5 collective-permute-start.21
  410.2 196.0 %reduce-scatter.11.cloned.1.call-start = ((), (), s32[]{:S(2)}) async-start(), calls=%async_computation.17 | async-start | bytes 5242880 | tf_op jit(solution)/shard_map/reduce_scatter | solution.py:684
  439.5 10.9 %collective-permute-start.24 = (bf16[512,2048]{1,0:T(8,128)(2,1)}, bf16[512,2048]{1,0:T(8,128)(2,1)}, u32[]{:S(2)}, u32[]{:S(2)}) collective-permute-start(bf16[512,2048]{1,0:T(8,128)(2,1)} %shard_map.306), channel_id=1, source_target_pairs={{0,8},{8,0},{1,9},{9,1},{2,10},{10,2},{3,11},{11,3},{4,12},{12,4},... | collective-permute-start | bytes 6291464 | tf_op jit(solution)/shard_map/ppermute | solution.py:43
  441.0 27.3 %collective-permute-start.22 = (bf16[512,768]{1,0:T(8,128)(2,1)S(1)}, bf16[512,768]{1,0:T(8,128)(2,1)}, u32[]{:S(2)}, u32[]{:S(2)}) collective-permute-start(bf16[512,768]{1,0:T(8,128)(2,1)S(1)} %slice_bitcast_fusion), channel_id=1, source_target_pairs={{0,2},{2,4},{4,6},{6,0},{1,3},{3,5},{5,7},{7,1},{8,10},{10,12},{12... | collective-permute-start | bytes 2359304 | tf_op jit(solution)/shard_map/ppermute | solution.py:43
  442.2 26.0 %collective-permute-start.23 = (bf16[64,2048]{1,0:T(8,128)(2,1)S(1)}, bf16[64,2048]{1,0:T(8,128)(2,1)S(1)}, u32[]{:S(2)}, u32[]{:S(2)}) collective-permute-start(bf16[64,2048]{1,0:T(8,128)(2,1)S(1)} %slice_bitcast_fusion.1), channel_id=1, source_target_pairs={{0,2},{2,4},{4,6},{6,0},{1,3},{3,5},{5,7},{7,1},{8,10},{10,12},{12... | collective-permute-start | bytes 786440 | tf_op jit(solution)/shard_map/ppermute | solution.py:43
  469.7 22.3 %collective-permute-start.28 = (bf16[512,768]{1,0:T(8,128)(2,1)S(1)}, bf16[512,768]{1,0:T(8,128)(2,1)S(1)}, u32[]{:S(2)}, u32[]{:S(2)}) collective-permute-start(bf16[512,768]{1,0:T(8,128)(2,1)S(1)} %fusion.6), channel_id=1, source_target_pairs={{0,2},{2,4},{4,6},{6,0},{1,3},{3,5},{5,7},{7,1},{8,10},{10,12},{12... | collective-permute-start | bytes 2359304 | tf_op jit(solution)/shard_map/ppermute | solution.py:43
  469.9 27.8 %collective-permute-start.30 = (bf16[64,2048]{1,0:T(8,128)(2,1)S(1)}, bf16[64,2048]{1,0:T(8,128)(2,1)S(1)}, u32[]{:S(2)}, u32[]{:S(2)}) collective-permute-start(bf16[64,2048]{1,0:T(8,128)(2,1)S(1)} %fusion.29), channel_id=1, source_target_pairs={{0,2},{2,4},{4,6},{6,0},{1,3},{3,5},{5,7},{7,1},{8,10},{10,12},{12... | collective-permute-start | bytes 786440 | tf_op jit(solution)/shard_map/ppermute | solution.py:43
  492.3 26.4 %collective-permute-start.29 = (bf16[512,768]{1,0:T(8,128)(2,1)S(1)}, bf16[512,768]{1,0:T(8,128)(2,1)S(1)}, u32[]{:S(2)}, u32[]{:S(2)}) collective-permute-start(bf16[512,768]{1,0:T(8,128)(2,1)S(1)} %fusion.5), channel_id=1, source_target_pairs={{0,2},{2,4},{4,6},{6,0},{1,3},{3,5},{5,7},{7,1},{8,10},{10,12},{12... | collective-permute-start | bytes 2359304 | tf_op jit(solution)/shard_map/ppermute | solution.py:43
  497.7 20.9 %collective-permute-start.31 = (bf16[64,2048]{1,0:T(8,128)(2,1)S(1)}, bf16[64,2048]{1,0:T(8,128)(2,1)S(1)}, u32[]{:S(2)}, u32[]{:S(2)}) collective-permute-start(bf16[64,2048]{1,0:T(8,128)(2,1)S(1)} %fusion.28), channel_id=1, source_target_pairs={{0,2},{2,4},{4,6},{6,0},{1,3},{3,5},{5,7},{7,1},{8,10},{10,12},{12... | collective-permute-start | bytes 786440 | tf_op jit(solution)/shard_map/ppermute | solution.py:43
  520.3 52.6 %all-to-all-start.4 = ((bf16[8,64,2048]{2,1,0:T(8,128)(2,1)}), bf16[8,64,2048]{2,1,0:T(8,128)(2,1)S(1)}, u32[]{:S(2)}, u32[]{:S(2)}) async-start(bf16[8,64,2048]{2,1,0:T(8,128)(2,1)} %bitcast.212), calls=%async_computation.6 | async-start | bytes 4194304 | tf_op jit(solution)/shard_map/all_to_all | solution.py:55
  526.9 50.4 %collective-permute-start.25 = (bf16[128,2048]{1,0:T(8,128)(2,1)}, bf16[128,2048]{1,0:T(8,128)(2,1)}, u32[]{:S(2)}, u32[]{:S(2)}) collective-permute-start(bf16[128,2048]{1,0:T(8,128)(2,1)} %get-tuple-element.229), channel_id=1, source_target_pairs={{0,16},{16,1},{1,17},{17,0},{2,18},{18,3},{3,19},{19,2},{4,20},{20... | collective-permute-start | bytes 1572872 | tf_op jit(solution)/shard_map/ppermute | solution.py:43
  528.8 48.6 %collective-permute-start.27 = (bf16[128,2048]{1,0:T(8,128)(2,1)}, bf16[128,2048]{1,0:T(8,128)(2,1)}, u32[]{:S(2)}, u32[]{:S(2)}) collective-permute-start(bf16[128,2048]{1,0:T(8,128)(2,1)} %get-tuple-element.230), channel_id=1, source_target_pairs={{0,17},{16,0},{1,16},{17,1},{2,19},{18,2},{3,18},{19,3},{4,21},{20... | collective-permute-start | bytes 1572872 | tf_op jit(solution)/shard_map/ppermute | solution.py:43
  529.9 47.5 %collective-permute-start.26 = (bf16[128,2048]{1,0:T(8,128)(2,1)}, bf16[128,2048]{1,0:T(8,128)(2,1)}, u32[]{:S(2)}, u32[]{:S(2)}) collective-permute-start(bf16[128,2048]{1,0:T(8,128)(2,1)} %get-tuple-element.231), channel_id=1, source_target_pairs={{0,1},{16,17},{1,0},{17,16},{2,3},{18,19},{3,2},{19,18},{4,5},{20,... | collective-permute-start | bytes 1572872 | tf_op jit(solution)/shard_map/ppermute | solution.py:43
  572.9 28.0 %all-to-all-start.5 = ((bf16[8,3,64,256]{3,2,1,0:T(8,128)(2,1)}), bf16[8,3,64,256]{3,2,1,0:T(8,128)(2,1)}, u32[]{:S(2)}, u32[]{:S(2)}) async-start(bf16[8,3,64,256]{3,2,1,0:T(8,128)(2,1)} %bitcast.167), calls=%async_computation.7 | async-start | bytes 1572864 | tf_op jit(solution)/shard_map/all_to_all | solution.py:55
  601.6 20.0 %all-to-all-start.6 = ((f32[32,1,320]{2,1,0:T(1,128)}), f32[32,1,320]{2,1,0:T(1,128)S(1)}, u32[]{:S(2)}, u32[]{:S(2)}) async-start(f32[32,1,320]{2,1,0:T(1,128)} %reshape.395), calls=%async_computation.9 | async-start | bytes 98304 | tf_op jit(solution)/shard_map/all_to_all | solution.py:55
  627.1 13.0 %all-to-all-start.7 = ((f32[32,8,2]{1,2,0:T(2,128)}), f32[32,8,2]{1,2,0:T(2,128)S(1)}, u32[]{:S(2)}, u32[]{:S(2)}) async-start(f32[32,8,2]{1,2,0:T(2,128)} %broadcast_in_dim.57), calls=%async_computation.10 | async-start | bytes 65536 | tf_op jit(solution)/shard_map/all_to_all | solution.py:55
  (36 other events, 272.3 us)
Sparse Core Ops, SparseCore 0:
  10.5 65.6 all-gather.5
  85.6 62.7 all-gather.7
  176.1 49.0 all-gather.11
  228.1 54.1 all-gather.9
  321.9 50.3 reduce-scatter.12
  375.6 48.1 reduce-scatter.6
  426.8 84.5 reduce-scatter.8
  514.7 82.9 reduce-scatter.10
